TPU v7x, 256 devices: a whole 4x4x8 slice. The times are simulated.
256 devices in a mesh: island: 16 (over y, z_lo), fsdp: 16 (over x, z_hi, core).
Axes of the slice: x: 4, y: 4, z: 8 (z_hi: 2, z_lo: 4; z = z_hi * 4 + z_lo), core: 2. Of those that a mesh axis runs over, the one named last changes fastest.
Arguments:
- local_weights: bfloat16 [16, 8, 8192, 1024], P('island', None, 'fsdp'), may hold values from -6 to 6
- master: float32 [8, 8192, 1024], P(None, ('fsdp', 'island')), may hold values from -6 to 6
- momentum: float32 [8, 8192, 1024], P(None, ('fsdp', 'island')), may hold values from -4 to 4
Outputs:
- fresh_weights: bfloat16 [8, 8192, 1024], P(None, 'fsdp')
- new_master: float32 [8, 8192, 1024], P(None, ('fsdp', 'island'))
- new_momentum: float32 [8, 8192, 1024], P(None, ('fsdp', 'island'))
All inputs are finite; a program needn't handle non-finite values.
Results may differ from a plain program's by a relative error of at most 0.015.
Values may be sent and summed in bfloat16 or wider, within the bound.
No kernel may reach another device: no remote copies, remote signals or barrier semaphores. Data moves between devices by JAX's collectives and lax.ppermute only.
A program may use at most 128 MiB of HBM per device.

v0:
```python
import functools

import jax
import jax.numpy as jnp
from jax import lax
from jax.experimental import pallas as pl
from jax.experimental.pallas import tpu as pltpu
from jax.sharding import Mesh, PartitionSpec as P

RATE = 0.7
MU = 0.9
NY = 4
NZ = 4
CHUNKS = 4
F32 = jnp.float32
BF16 = jnp.bfloat16
ANY = pl.BlockSpec(memory_space=pl.ANY)
HBM = pl.BlockSpec(memory_space=pltpu.HBM)
ROWS = 32
VMEM = 16 << 20


def shift(a, s):
    return lax.ppermute(a, "y", [(i, (i + s) % NY) for i in range(NY)])


def swap(a, k):
    return lax.ppermute(a, "z", [(i, i ^ k) for i in range(NZ)])


def ds(block, n):
    return pl.ds(pl.multiple_of(block * n, n), n)


def move(*copies):
    started = [pltpu.make_async_copy(*c) for c in copies]
    for c in started:
        c.start()
    for c in started:
        c.wait()


class Steps:
    def __init__(self, x, master, momentum, where):
        self.x, self.master, self.momentum, self.where = x, master, momentum, where
        _, self.projs, rows, self.w = x.shape
        self.p = self.projs // CHUNKS
        self.h = self.p // 2
        self.n = rows // NY
        self.m = self.n // NZ
        self.last = None
        self.out, self.new_master, self.new_momentum = None, {}, {}

    def call(self, body, ins, outs, alias=(), scratch=()):
        arrays = [a for a, _ in ins]
        specs = [s for _, s in ins]
        n_in, n_out = len(arrays), len(outs)
        aliases = {}
        for array, k in alias:
            if array is not None:
                aliases[1 + len(arrays)] = k
                arrays.append(array)
                specs.append(outs[k][2])
        if self.last is not None:
            arrays.append(self.last)
            specs.append(ANY)
        total = len(arrays)

        def kernel(where, *refs):
            body(where, *refs[:n_in], *refs[total:])

        got = pl.pallas_call(
            kernel,
            out_shape=[jax.ShapeDtypeStruct(s, t) for s, t, _ in outs],
            grid_spec=pltpu.PrefetchScalarGridSpec(
                num_scalar_prefetch=1,
                grid=(1,),
                in_specs=specs,
                out_specs=[s for _, _, s in outs],
                scratch_shapes=scratch,
            ),
            input_output_aliases=aliases,
            compiler_params=pltpu.CompilerParams(vmem_limit_bytes=VMEM),
            cost_estimate=pl.CostEstimate(flops=1000, bytes_accessed=1000, transcendentals=0),
        )(self.where, *arrays)
        if len(got) > 1:
            self.last = got[-1]
        return got

    def full(self, shape):
        return pl.BlockSpec(shape, lambda i, w: (0,) * len(shape))

    def of_x(self, where, c, d, first, count):
        return (0, pl.ds(c * self.p + first, count), ds((where[0] + d) % NY, self.n))

    def of_out(self, where, c, d, first, count):
        return (pl.ds(c * self.p + first, count), ds((where[0] + d) % NY, self.n))

    def first(self, c):
        p, h, n, w = self.p, self.h, self.n, self.w

        def body(where, x, up, down, sems):
            move(
                (x.at[self.of_x(where, c, 2, h, h)], up, sems.at[0]),
                (x.at[self.of_x(where, c, 2, 0, h)], down, sems.at[1]),
            )

        up, down = self.call(body, [(self.x, HBM)], [((h, n, w), BF16, ANY)] * 2, scratch=[pltpu.SemaphoreType.DMA((2,))])
        return shift(up, 1), shift(down, -1)

    def second(self, c, got):
        p, h, n, w = self.p, self.h, self.n, self.w

        def body(where, x, below, above, up, down, sems):
            move(
                (x.at[self.of_x(where, c, 1, 0, p)], up, sems.at[0]),
                (x.at[self.of_x(where, c, 3, 0, p)], down, sems.at[1]),
            )

            @pl.loop(0, n // ROWS)
            def _(i):
                r = ds(i, ROWS)
                up[h:, r] = (up[h:, r].astype(F32) + below[:, r].astype(F32)).astype(BF16)
                down[:h, r] = (down[:h, r].astype(F32) + above[:, r].astype(F32)).astype(BF16)

        up, down = self.call(
            body,
            [(self.x, HBM), (got[0], self.full((h, n, w))), (got[1], self.full((h, n, w)))],
            [((p, n, w), BF16, self.full((p, n, w)))] * 2,
            scratch=[pltpu.SemaphoreType.DMA((2,))],
        )
        return shift(up, 1), shift(down, -1)

    def third(self, c, got):
        p, n, m, w = self.p, self.n, self.m, self.w

        def body(where, x, below, above, keep, send, own, sems):
            move((x.at[self.of_x(where, c, 0, 0, p)], own, sems.at[0]))
            z = where[1]
            for out, at, k in ((keep, 0, 0), (keep, m, 3), (send, 0, 1), (send, m, 2)):
                r = ds(z ^ k, m)
                t = own[:, r].astype(F32) + below[:, r].astype(F32) + above[:, r].astype(F32)
                out[:, at : at + m] = t.astype(out.dtype)

        keep, send = self.call(
            body,
            [(self.x, HBM), (got[0], self.full((p, n, w))), (got[1], self.full((p, n, w)))],
            [
                ((p, 2 * m, w), F32, self.full((p, 2 * m, w))),
                ((p, 2 * m, w), BF16, self.full((p, 2 * m, w))),
            ],
            scratch=[pltpu.VMEM((p, n, w), BF16), pltpu.SemaphoreType.DMA((1,))],
        )
        return keep, swap(send, 1)

    def fourth(self, c, got):
        p, m, w = self.p, self.m, self.w

        def body(where, kept, came, keep, send):
            keep[...] = kept[:, :m] + came[:, :m].astype(F32)
            send[...] = (kept[:, m:] + came[:, m:].astype(F32)).astype(BF16)

        keep, send = self.call(
            body,
            [(a, self.full((p, 2 * m, w))) for a in got],
            [((p, m, w), F32, self.full((p, m, w))), ((p, m, w), BF16, self.full((p, m, w)))],
        )
        return keep, swap(send, 3)

    def update(self, c, got):
        p, m, w = self.p, self.m, self.w
        mine = pl.BlockSpec((p, m, w), lambda i, w_: (c, 0, 0))

        def body(where, kept, came, master, momentum, new_master, new_momentum, fresh):
            pseudo = master[...] - (kept[...] + came[...].astype(F32)) / 16
            nv = MU * momentum[...] + pseudo
            nm = master[...] - RATE * (pseudo + MU * nv)
            new_master[...] = nm
            new_momentum[...] = nv
            fresh[...] = nm.astype(BF16)

        nm, nv, fresh = self.call(
            body,
            [(a, self.full((p, m, w))) for a in got] + [(self.master, mine), (self.momentum, mine)],
            [
                ((p, m, w), F32, self.full((p, m, w))),
                ((p, m, w), F32, self.full((p, m, w))),
                ((p, m, w), BF16, self.full((p, m, w))),
            ],
        )
        self.new_master[c], self.new_momentum[c] = nm, nv
        return fresh, swap(fresh, 3)

    def pair(self, c, got):
        p, m, w = self.p, self.m, self.w

        def body(where, mine, came, both, mark):
            both[:, :m] = mine[...]
            both[:, m:] = came[...]

        both, _ = self.call(
            body,
            [(a, self.full((p, m, w))) for a in got],
            [((p, 2 * m, w), BF16, self.full((p, 2 * m, w))), ((8, 128), F32, self.full((8, 128)))],
        )
        return both, swap(both, 1)

    def whole(self, c, got):
        p, n, m, w = self.p, self.n, self.m, self.w

        def body(where, mine, came, out, block, sems):
            z = where[1]
            for src, at, k in ((mine, 0, 0), (mine, m, 3), (came, 0, 1), (came, m, 2)):
                block[:, ds(z ^ k, m)] = src[:, at : at + m]
            move((block, out.at[self.of_out(where, c, 0, 0, p)], sems.at[0]))

        self.out, block = self.call(
            body,
            [(a, self.full((p, 2 * m, w))) for a in got],
            [((self.projs, NY * n, w), BF16, HBM), ((p, n, w), BF16, self.full((p, n, w)))],
            alias=[(self.out, 0)],
            scratch=[pltpu.SemaphoreType.DMA((1,))],
        )
        return shift(block, 1), shift(block, -1)

    def pass_on(self, c, got):
        p, h, n, w = self.p, self.h, self.n, self.w

        def body(where, below, above, out, up, down, sems):
            move(
                (below.at[pl.ds(0, h)], up, sems.at[0]),
                (above.at[pl.ds(h, h)], down, sems.at[1]),
                (below, out.at[self.of_out(where, c, 3, 0, p)], sems.at[2]),
                (above, out.at[self.of_out(where, c, 1, 0, p)], sems.at[3]),
            )

        self.out, up, down = self.call(
            body,
            [(a, ANY) for a in got],
            [(self.out.shape, BF16, HBM), ((h, n, w), BF16, ANY), ((h, n, w), BF16, ANY)],
            alias=[(self.out, 0)],
            scratch=[pltpu.SemaphoreType.DMA((4,))],
        )
        return shift(up, 1), shift(down, -1)

    def finish(self, c, got):
        p, h, n, w = self.p, self.h, self.n, self.w

        def body(where, low, high, out, sems):
            move(
                (low, out.at[self.of_out(where, c, 2, 0, h)], sems.at[0]),
                (high, out.at[self.of_out(where, c, 2, h, h)], sems.at[1]),
            )

        (self.out,) = self.call(
            body,
            [(a, ANY) for a in got],
            [(self.out.shape, BF16, HBM)],
            alias=[(self.out, 0)],
            scratch=[pltpu.SemaphoreType.DMA((2,))],
        )


PLAN = "a0 a1 m0 a2 m1 s0 a3 h0 m2 s1 u0 h1 p0 m3 s2 u1 g0 h2 p1 s3 u2 h3 g1 p2 u3 o0 g2 p3 o1 f0 g3 o2 f1 o3 f2 f3"


def on_device(x, master, momentum):
    where = jnp.stack([lax.axis_index("y"), lax.axis_index("z")]).astype(jnp.int32)
    s = Steps(x, master, momentum, where)
    held = [None] * CHUNKS
    kinds = dict(a=None, m=s.second, s=s.third, h=s.fourth, u=s.update, p=s.pair, g=s.whole, o=s.pass_on, f=s.finish)
    for step in PLAN.split():
        c = int(step[1:])
        held[c] = s.first(c) if step[0] == "a" else kinds[step[0]](c, held[c])
    join = lambda d: jnp.concatenate([d[c] for c in range(CHUNKS)])
    return s.out, join(s.new_master), join(s.new_momentum)


def solution(mesh):
    fine = Mesh(mesh.devices.reshape(NY, NZ, -1), ("y", "z", "fsdp"))
    owned = P(None, ("fsdp", "y", "z"), None)
    return jax.shard_map(
        on_device,
        mesh=fine,
        in_specs=(P(("y", "z"), None, "fsdp", None), owned, owned),
        out_specs=(P(None, "fsdp", None), owned, owned),
        check_vma=False,
    )
```

profile of v0, /device:TPU:56, one launch (start us, length us, event | category | flops | bytes accessed | tf_op | source)
XLA Modules:
  0.0 188.1 jit_solution(16937224374893281281)
XLA Ops:
  0.7 3.4 %copy-done = bf16[1,8,512,1024]{3,2,1,0:T(8,128)(2,1)S(1)} copy-done((bf16[1,8,512,1024]{3,2,1,0:T(8,128)(2,1)S(1)}, bf16[1,8,512,1024]{3,2,1,0:T(8,128)(2,1)}, u32[]{:S(2)}) %copy-start) | copy-done | bytes 8388632
  4.7 0.8 collective-permute-start.1
  5.5 2.5 %collective-permute-start = (bf16[1,128,1024]{2,1,0:T(8,128)(2,1)S(1)}, bf16[1,128,1024]{2,1,0:T(8,128)(2,1)S(1)}, u32[]{:S(2)}, u32[]{:S(2)}) collective-permute-start(bf16[1,128,1024]{2,1,0:T(8,128)(2,1)S(1)} %get-tuple-element.75), channel_id=1, source_target_pairs={{0,64},{64,128},{128,192},{192,0},{1,65},{65,129},{129,193},{193,1... | collective-permute-start | bytes 786440 | tf_op jit(solution)/shard_map/ppermute | solution.py:24
  8.6 5.4 %collective-permute-done.1.refs_2_ = bf16[1,128,1024]{2,1,0:T(8,128)(2,1)S(1)} collective-permute-done((bf16[1,128,1024]{2,1,0:T(8,128)(2,1)S(1)}, bf16[1,128,1024]{2,1,0:T(8,128)(2,1)S(1)}, u32[]{:S(2)}, u32[]{:S(2)}) %collective-permute-start.1) | collective-permute-done | bytes 262176 | tf_op jit(solution)/shard_map/ppermute | solution.py:24
  14.9 3.2 %collective-permute-start.2 = (bf16[2,128,1024]{2,1,0:T(8,128)(2,1)S(1)}, bf16[2,128,1024]{2,1,0:T(8,128)(2,1)S(1)}, u32[]{:S(2)}, u32[]{:S(2)}) collective-permute-start(bf16[2,128,1024]{2,1,0:T(8,128)(2,1)S(1)} %get-tuple-element.78), channel_id=1, source_target_pairs={{0,64},{64,128},{128,192},{192,0},{1,65},{65,129},{129,193},{193,1... | collective-permute-start | bytes 1572872 | tf_op jit(solution)/shard_map/ppermute | solution.py:24
  18.2 3.2 %collective-permute-start.4 = (bf16[1,128,1024]{2,1,0:T(8,128)(2,1)S(1)}, bf16[1,128,1024]{2,1,0:T(8,128)(2,1)S(1)}, u32[]{:S(2)}, u32[]{:S(2)}) collective-permute-start(bf16[1,128,1024]{2,1,0:T(8,128)(2,1)S(1)} %get-tuple-element.80), channel_id=1, source_target_pairs={{0,64},{64,128},{128,192},{192,0},{1,65},{65,129},{129,193},{193,1... | collective-permute-start | bytes 786440 | tf_op jit(solution)/shard_map/ppermute | solution.py:24
  22.0 12.5 %collective-permute-done.5.refs_2_ = bf16[1,128,1024]{2,1,0:T(8,128)(2,1)S(1)} collective-permute-done((bf16[1,128,1024]{2,1,0:T(8,128)(2,1)S(1)}, bf16[1,128,1024]{2,1,0:T(8,128)(2,1)S(1)}, u32[]{:S(2)}, u32[]{:S(2)}) %collective-permute-start.5) | collective-permute-done | bytes 262176 | tf_op jit(solution)/shard_map/ppermute | solution.py:24
  35.3 3.0 %collective-permute-start.10 = (bf16[2,128,1024]{2,1,0:T(8,128)(2,1)S(1)}, bf16[2,128,1024]{2,1,0:T(8,128)(2,1)S(1)}, u32[]{:S(2)}, u32[]{:S(2)}) collective-permute-start(bf16[2,128,1024]{2,1,0:T(8,128)(2,1)S(1)} %get-tuple-element.89), channel_id=1, source_target_pairs={{0,64},{64,128},{128,192},{192,0},{1,65},{65,129},{129,193},{193,1... | collective-permute-start | bytes 1572872 | tf_op jit(solution)/shard_map/ppermute | solution.py:24
  39.4 3.2 %collective-permute-start.12 = (bf16[1,128,1024]{2,1,0:T(8,128)(2,1)S(1)}, bf16[1,128,1024]{2,1,0:T(8,128)(2,1)S(1)}, u32[]{:S(2)}, u32[]{:S(2)}) collective-permute-start(bf16[1,128,1024]{2,1,0:T(8,128)(2,1)S(1)} %get-tuple-element.90), channel_id=1, source_target_pairs={{0,64},{64,128},{128,192},{192,0},{1,65},{65,129},{129,193},{193,1... | collective-permute-start | bytes 786440 | tf_op jit(solution)/shard_map/ppermute | solution.py:24
  43.2 2.4 %collective-permute-done.8.refs_1_ = bf16[2,64,1024]{2,1,0:T(8,128)(2,1)S(1)} collective-permute-done((bf16[2,64,1024]{2,1,0:T(8,128)(2,1)S(1)}, bf16[2,64,1024]{2,1,0:T(8,128)(2,1)S(1)}, u32[]{:S(2)}, u32[]{:S(2)}) %collective-permute-start.8) | collective-permute-done | bytes 262176 | tf_op jit(solution)/shard_map/ppermute | solution.py:28
  46.2 6.9 %collective-permute-done.12.refs_1_ = bf16[1,128,1024]{2,1,0:T(8,128)(2,1)S(1)} collective-permute-done((bf16[1,128,1024]{2,1,0:T(8,128)(2,1)S(1)}, bf16[1,128,1024]{2,1,0:T(8,128)(2,1)S(1)}, u32[]{:S(2)}, u32[]{:S(2)}) %collective-permute-start.12) | collective-permute-done | bytes 262176 | tf_op jit(solution)/shard_map/ppermute | solution.py:24
  53.1 3.4 %collective-permute-done.13.refs_2_ = bf16[1,128,1024]{2,1,0:T(8,128)(2,1)S(1)} collective-permute-done((bf16[1,128,1024]{2,1,0:T(8,128)(2,1)S(1)}, bf16[1,128,1024]{2,1,0:T(8,128)(2,1)S(1)}, u32[]{:S(2)}, u32[]{:S(2)}) %collective-permute-start.13) | collective-permute-done | bytes 262176 | tf_op jit(solution)/shard_map/ppermute | solution.py:24
  56.5 0.8 shard_map.66
  58.3 3.7 %collective-permute-start.9 = (bf16[2,32,1024]{2,1,0:T(8,128)(2,1)S(1)}, bf16[2,32,1024]{2,1,0:T(8,128)(2,1)S(1)}, u32[]{:S(2)}, u32[]{:S(2)}) collective-permute-start(bf16[2,32,1024]{2,1,0:T(8,128)(2,1)S(1)} %get-tuple-element.88.refs_3_), channel_id=1, source_target_pairs={{0,48},{16,32},{32,16},{48,0},{1,49},{17,33},{33,17},{49,1},{2,50}... | collective-permute-start | bytes 393224 | tf_op jit(solution)/shard_map/ppermute | solution.py:28
  62.3 1.7 collective-permute-start.20
  64.1 1.5 collective-permute-start.6
  65.6 2.6 %collective-permute-done.9.refs_1_ = bf16[2,32,1024]{2,1,0:T(8,128)(2,1)S(1)} collective-permute-done((bf16[2,32,1024]{2,1,0:T(8,128)(2,1)S(1)}, bf16[2,32,1024]{2,1,0:T(8,128)(2,1)S(1)}, u32[]{:S(2)}, u32[]{:S(2)}) %collective-permute-start.9) | collective-permute-done | bytes 131104 | tf_op jit(solution)/shard_map/ppermute | solution.py:28
  68.8 2.6 %collective-permute-start.14 = (bf16[2,32,1024]{2,1,0:T(8,128)(2,1)S(1)}, bf16[2,32,1024]{2,1,0:T(8,128)(2,1)S(1)}, u32[]{:S(2)}, u32[]{:S(2)}) collective-permute-start(bf16[2,32,1024]{2,1,0:T(8,128)(2,1)S(1)} %get-tuple-element.93.refs_2_.refs_0_), channel_id=1, source_target_pairs={{0,48},{16,32},{32,16},{48,0},{1,49},{17,33},{33,17},{49,1},{2,50}... | collective-permute-start | bytes 393224 | tf_op jit(solution)/shard_map/ppermute | solution.py:28
  72.0 3.7 %collective-permute-done.14.refs_1_ = bf16[2,32,1024]{2,1,0:T(8,128)(2,1)S(1)} collective-permute-done((bf16[2,32,1024]{2,1,0:T(8,128)(2,1)S(1)}, bf16[2,32,1024]{2,1,0:T(8,128)(2,1)S(1)}, u32[]{:S(2)}, u32[]{:S(2)}) %collective-permute-start.14) | collective-permute-done | bytes 131104 | tf_op jit(solution)/shard_map/ppermute | solution.py:28
  76.3 1.2 collective-permute-done.6.refs_1_
  77.5 1.5 collective-permute-done.7.refs_2_
  80.4 1.5 collective-permute-start.17
  82.2 1.7 collective-permute-start.23
  83.9 0.8 shard_map.72
  85.1 3.6 %collective-permute-done.18.refs_1_ = bf16[2,32,1024]{2,1,0:T(8,128)(2,1)S(1)} collective-permute-done((bf16[2,32,1024]{2,1,0:T(8,128)(2,1)S(1)}, bf16[2,32,1024]{2,1,0:T(8,128)(2,1)S(1)}, u32[]{:S(2)}, u32[]{:S(2)}) %collective-permute-start.18) | collective-permute-done | bytes 131104 | tf_op jit(solution)/shard_map/ppermute | solution.py:28
  89.3 2.5 %collective-permute-start.21 = (bf16[2,32,1024]{2,1,0:T(8,128)(2,1)S(1)}, bf16[2,32,1024]{2,1,0:T(8,128)(2,1)S(1)}, u32[]{:S(2)}, u32[]{:S(2)}) collective-permute-start(bf16[2,32,1024]{2,1,0:T(8,128)(2,1)S(1)} %get-tuple-element.102.refs_2_.refs_0_), channel_id=1, source_target_pairs={{0,48},{16,32},{32,16},{48,0},{1,49},{17,33},{33,17},{49,1},{2,50}... | collective-permute-start | bytes 393224 | tf_op jit(solution)/shard_map/ppermute | solution.py:28
  91.9 1.4 shard_map.74
  93.3 1.3 collective-permute-done.22.refs_1_
  95.1 1.0 collective-permute-done.21.refs_1_
  96.7 0.8 shard_map.77
  97.5 6.3 %collective-permute-start.24 = (bf16[2,64,1024]{2,1,0:T(8,128)(2,1)S(1)}, bf16[2,64,1024]{2,1,0:T(8,128)(2,1)S(1)}, u32[]{:S(2)}, u32[]{:S(2)}) collective-permute-start(bf16[2,64,1024]{2,1,0:T(8,128)(2,1)S(1)} %get-tuple-element.109.refs_4_), channel_id=1, source_target_pairs={{0,16},{16,0},{32,48},{48,32},{1,17},{17,1},{33,49},{49,33},{2,18}... | collective-permute-start | bytes 786440 | tf_op jit(solution)/shard_map/ppermute | solution.py:28
  103.9 2.1 %collective-permute-start.31 = (bf16[2,128,1024]{2,1,0:T(8,128)(2,1)S(1)}, bf16[2,128,1024]{2,1,0:T(8,128)(2,1)S(1)}, u32[]{:S(2)}, u32[]{:S(2)}) collective-permute-start(bf16[2,128,1024]{2,1,0:T(8,128)(2,1)S(1)} %get-tuple-element.105.refs_2_), channel_id=1, source_target_pairs={{0,64},{64,128},{128,192},{192,0},{1,65},{65,129},{129,193},{193,1... | collective-permute-start | bytes 1572872 | tf_op jit(solution)/shard_map/ppermute | solution.py:24
  106.0 4.2 %collective-permute-done.25.refs_1_ = bf16[2,32,1024]{2,1,0:T(8,128)(2,1)S(1)} collective-permute-done((bf16[2,32,1024]{2,1,0:T(8,128)(2,1)S(1)}, bf16[2,32,1024]{2,1,0:T(8,128)(2,1)S(1)}, u32[]{:S(2)}, u32[]{:S(2)}) %collective-permute-start.25) | collective-permute-done | bytes 131104 | tf_op jit(solution)/shard_map/ppermute | solution.py:28
  111.9 1.4 shard_map.80
  113.3 5.0 %collective-permute-start.36 = (bf16[2,128,1024]{2,1,0:T(8,128)(2,1)S(1)}, bf16[2,128,1024]{2,1,0:T(8,128)(2,1)S(1)}, u32[]{:S(2)}, u32[]{:S(2)}) collective-permute-start(bf16[2,128,1024]{2,1,0:T(8,128)(2,1)S(1)} %get-tuple-element.116.refs_2_), channel_id=1, source_target_pairs={{0,64},{64,128},{128,192},{192,0},{1,65},{65,129},{129,193},{193,1... | collective-permute-start | bytes 1572872 | tf_op jit(solution)/shard_map/ppermute | solution.py:24
  118.3 2.0 %collective-permute-start.26 = (bf16[2,32,1024]{2,1,0:T(8,128)(2,1)S(1)}, bf16[2,32,1024]{2,1,0:T(8,128)(2,1)S(1)}, u32[]{:S(2)}, u32[]{:S(2)}) collective-permute-start(bf16[2,32,1024]{2,1,0:T(8,128)(2,1)S(1)} %get-tuple-element.113.refs_3_), channel_id=1, source_target_pairs={{0,48},{16,32},{32,16},{48,0},{1,49},{17,33},{33,17},{49,1},{2,50}... | collective-permute-start | bytes 393224 | tf_op jit(solution)/shard_map/ppermute | solution.py:28
  120.3 4.5 %collective-permute-done.27.refs_1_ = bf16[2,32,1024]{2,1,0:T(8,128)(2,1)S(1)} collective-permute-done((bf16[2,32,1024]{2,1,0:T(8,128)(2,1)S(1)}, bf16[2,32,1024]{2,1,0:T(8,128)(2,1)S(1)}, u32[]{:S(2)}, u32[]{:S(2)}) %collective-permute-start.27) | collective-permute-done | bytes 131104 | tf_op jit(solution)/shard_map/ppermute | solution.py:28
  125.3 3.0 %collective-permute-start.30 = (bf16[2,64,1024]{2,1,0:T(8,128)(2,1)S(1)}, bf16[2,64,1024]{2,1,0:T(8,128)(2,1)S(1)}, u32[]{:S(2)}, u32[]{:S(2)}) collective-permute-start(bf16[2,64,1024]{2,1,0:T(8,128)(2,1)S(1)} %get-tuple-element.119.refs_0_), channel_id=1, source_target_pairs={{0,16},{16,0},{32,48},{48,32},{1,17},{17,1},{33,49},{49,33},{2,18}... | collective-permute-start | bytes 786440 | tf_op jit(solution)/shard_map/ppermute | solution.py:28
  130.2 1.6 shard_map.83
  131.8 3.3 %collective-permute-start.34 = (bf16[1,128,1024]{2,1,0:T(8,128)(2,1)S(1)}, bf16[1,128,1024]{2,1,0:T(8,128)(2,1)S(1)}, u32[]{:S(2)}, u32[]{:S(2)}) collective-permute-start(bf16[1,128,1024]{2,1,0:T(8,128)(2,1)S(1)} %get-tuple-element.125), channel_id=1, source_target_pairs={{0,64},{64,128},{128,192},{192,0},{1,65},{65,129},{129,193},{193,1... | collective-permute-start | bytes 786440 | tf_op jit(solution)/shard_map/ppermute | solution.py:24
  135.1 1.4 shard_map.84
  136.5 3.3 %collective-permute-start.42 = (bf16[2,128,1024]{2,1,0:T(8,128)(2,1)S(1)}, bf16[2,128,1024]{2,1,0:T(8,128)(2,1)S(1)}, u32[]{:S(2)}, u32[]{:S(2)}) collective-permute-start(bf16[2,128,1024]{2,1,0:T(8,128)(2,1)S(1)} %get-tuple-element.123.refs_2_), channel_id=1, source_target_pairs={{0,64},{64,128},{128,192},{192,0},{1,65},{65,129},{129,193},{193,1... | collective-permute-start | bytes 1572872 | tf_op jit(solution)/shard_map/ppermute | solution.py:24
  140.4 2.1 %collective-permute-start.33 = (bf16[2,64,1024]{2,1,0:T(8,128)(2,1)S(1)}, bf16[2,64,1024]{2,1,0:T(8,128)(2,1)S(1)}, u32[]{:S(2)}, u32[]{:S(2)}) collective-permute-start(bf16[2,64,1024]{2,1,0:T(8,128)(2,1)S(1)} %get-tuple-element.124.refs_0_), channel_id=1, source_target_pairs={{0,16},{16,0},{32,48},{48,32},{1,17},{17,1},{33,49},{49,33},{2,18}... | collective-permute-start | bytes 786440 | tf_op jit(solution)/shard_map/ppermute | solution.py:28
  142.4 1.6 collective-permute-done.37.refs_1_
  144.0 1.6 shard_map.86
  145.6 4.0 %collective-permute-done.35.refs_1_ = bf16[1,128,1024]{2,1,0:T(8,128)(2,1)S(1)} collective-permute-done((bf16[1,128,1024]{2,1,0:T(8,128)(2,1)S(1)}, bf16[1,128,1024]{2,1,0:T(8,128)(2,1)S(1)}, u32[]{:S(2)}, u32[]{:S(2)}) %collective-permute-start.35) | collective-permute-done | bytes 262176 | tf_op jit(solution)/shard_map/ppermute | solution.py:24
  149.7 1.4 shard_map.87.refs_2_
  151.0 1.4 shard_map.88
  152.4 1.2 collective-permute-start.38
  153.6 0.9 collective-permute-start.39
  154.5 2.3 %collective-permute-start.40 = (bf16[1,128,1024]{2,1,0:T(8,128)(2,1)S(1)}, bf16[1,128,1024]{2,1,0:T(8,128)(2,1)S(1)}, u32[]{:S(2)}, u32[]{:S(2)}) collective-permute-start(bf16[1,128,1024]{2,1,0:T(8,128)(2,1)S(1)} %get-tuple-element.131), channel_id=1, source_target_pairs={{0,64},{64,128},{128,192},{192,0},{1,65},{65,129},{129,193},{193,1... | collective-permute-start | bytes 786440 | tf_op jit(solution)/shard_map/ppermute | solution.py:24
  156.9 4.0 %collective-permute-done.43.refs_1_ = bf16[2,128,1024]{2,1,0:T(8,128)(2,1)S(1)} collective-permute-done((bf16[2,128,1024]{2,1,0:T(8,128)(2,1)S(1)}, bf16[2,128,1024]{2,1,0:T(8,128)(2,1)S(1)}, u32[]{:S(2)}, u32[]{:S(2)}) %collective-permute-start.43) | collective-permute-done | bytes 524320 | tf_op jit(solution)/shard_map/ppermute | solution.py:24
  160.9 1.6 shard_map.89
  162.5 1.2 collective-permute-start.46
  163.7 1.7 collective-permute-done.40.refs_0_
  165.4 10.5 %collective-permute-done.41.refs_1_ = bf16[1,128,1024]{2,1,0:T(8,128)(2,1)S(1)} collective-permute-done((bf16[1,128,1024]{2,1,0:T(8,128)(2,1)S(1)}, bf16[1,128,1024]{2,1,0:T(8,128)(2,1)S(1)}, u32[]{:S(2)}, u32[]{:S(2)}) %collective-permute-start.41) | collective-permute-done | bytes 262176 | tf_op jit(solution)/shard_map/ppermute | solution.py:24
  175.9 1.4 shard_map.90.refs_2_
  177.3 1.6 shard_map.91
  179.0 2.0 %collective-permute-start.45 = (bf16[1,128,1024]{2,1,0:T(8,128)(2,1)S(1)}, bf16[1,128,1024]{2,1,0:T(8,128)(2,1)S(1)}, u32[]{:S(2)}, u32[]{:S(2)}) collective-permute-start(bf16[1,128,1024]{2,1,0:T(8,128)(2,1)S(1)} %get-tuple-element.136.refs_3_), channel_id=1, source_target_pairs={{0,192},{64,0},{128,64},{192,128},{1,193},{65,1},{129,65},{193,129... | collective-permute-start | bytes 786440 | tf_op jit(solution)/shard_map/ppermute | solution.py:24
  181.0 1.5 pad_maximum_fusion
  182.4 1.4 shard_map.92.refs_2_
  183.8 1.5 collective-permute-done.44.refs_0_
  185.3 1.3 collective-permute-done.45.refs_1_
  186.6 1.4 shard_map.93
  (81 shorter events, 17.6 us)
Async XLA Ops:
  0.7 3.4 %copy-start = (bf16[1,8,512,1024]{3,2,1,0:T(8,128)(2,1)S(1)}, bf16[1,8,512,1024]{3,2,1,0:T(8,128)(2,1)}, u32[]{:S(2)}) copy-start(bf16[1,8,512,1024]{3,2,1,0:T(8,128)(2,1)} %refs_0_.23) | copy-start | bytes 25165828
  4.7 9.3 %collective-permute-start.1 = (bf16[1,128,1024]{2,1,0:T(8,128)(2,1)S(1)}, bf16[1,128,1024]{2,1,0:T(8,128)(2,1)S(1)}, u32[]{:S(2)}, u32[]{:S(2)}) collective-permute-start(bf16[1,128,1024]{2,1,0:T(8,128)(2,1)S(1)} %get-tuple-element.76.refs_1_), channel_id=1, source_target_pairs={{0,192},{64,0},{128,64},{192,128},{1,193},{65,1},{129,65},{193,129... | collective-permute-start | bytes 786440 | tf_op jit(solution)/shard_map/ppermute | solution.py:24
  5.5 8.5 %collective-permute-start = (bf16[1,128,1024]{2,1,0:T(8,128)(2,1)S(1)}, bf16[1,128,1024]{2,1,0:T(8,128)(2,1)S(1)}, u32[]{:S(2)}, u32[]{:S(2)}) collective-permute-start(bf16[1,128,1024]{2,1,0:T(8,128)(2,1)S(1)} %get-tuple-element.75), channel_id=1, source_target_pairs={{0,64},{64,128},{128,192},{192,0},{1,65},{65,129},{129,193},{193,1... | collective-permute-start | bytes 786440 | tf_op jit(solution)/shard_map/ppermute | solution.py:24
  14.8 23.5 %collective-permute-start.3 = (bf16[2,128,1024]{2,1,0:T(8,128)(2,1)S(1)}, bf16[2,128,1024]{2,1,0:T(8,128)(2,1)S(1)}, u32[]{:S(2)}, u32[]{:S(2)}) collective-permute-start(bf16[2,128,1024]{2,1,0:T(8,128)(2,1)S(1)} %get-tuple-element.79.refs_1_), channel_id=1, source_target_pairs={{0,192},{64,0},{128,64},{192,128},{1,193},{65,1},{129,65},{193,129... | collective-permute-start | bytes 1572872 | tf_op jit(solution)/shard_map/ppermute | solution.py:24
  14.9 23.4 %collective-permute-start.2 = (bf16[2,128,1024]{2,1,0:T(8,128)(2,1)S(1)}, bf16[2,128,1024]{2,1,0:T(8,128)(2,1)S(1)}, u32[]{:S(2)}, u32[]{:S(2)}) collective-permute-start(bf16[2,128,1024]{2,1,0:T(8,128)(2,1)S(1)} %get-tuple-element.78), channel_id=1, source_target_pairs={{0,64},{64,128},{128,192},{192,0},{1,65},{65,129},{129,193},{193,1... | collective-permute-start | bytes 1572872 | tf_op jit(solution)/shard_map/ppermute | solution.py:24
  18.1 16.4 %collective-permute-start.5 = (bf16[1,128,1024]{2,1,0:T(8,128)(2,1)S(1)}, bf16[1,128,1024]{2,1,0:T(8,128)(2,1)S(1)}, u32[]{:S(2)}, u32[]{:S(2)}) collective-permute-start(bf16[1,128,1024]{2,1,0:T(8,128)(2,1)S(1)} %get-tuple-element.77.refs_3_), channel_id=1, source_target_pairs={{0,192},{64,0},{128,64},{192,128},{1,193},{65,1},{129,65},{193,129... | collective-permute-start | bytes 786440 | tf_op jit(solution)/shard_map/ppermute | solution.py:24
  18.2 16.4 %collective-permute-start.4 = (bf16[1,128,1024]{2,1,0:T(8,128)(2,1)S(1)}, bf16[1,128,1024]{2,1,0:T(8,128)(2,1)S(1)}, u32[]{:S(2)}, u32[]{:S(2)}) collective-permute-start(bf16[1,128,1024]{2,1,0:T(8,128)(2,1)S(1)} %get-tuple-element.80), channel_id=1, source_target_pairs={{0,64},{64,128},{128,192},{192,0},{1,65},{65,129},{129,193},{193,1... | collective-permute-start | bytes 786440 | tf_op jit(solution)/shard_map/ppermute | solution.py:24
  35.3 22.0 %collective-permute-start.10 = (bf16[2,128,1024]{2,1,0:T(8,128)(2,1)S(1)}, bf16[2,128,1024]{2,1,0:T(8,128)(2,1)S(1)}, u32[]{:S(2)}, u32[]{:S(2)}) collective-permute-start(bf16[2,128,1024]{2,1,0:T(8,128)(2,1)S(1)} %get-tuple-element.89), channel_id=1, source_target_pairs={{0,64},{64,128},{128,192},{192,0},{1,65},{65,129},{129,193},{193,1... | collective-permute-start | bytes 1572872 | tf_op jit(solution)/shard_map/ppermute | solution.py:24
  38.4 18.1 %slice-start = ((s8[8388608]{0:T(1024)(128)(4,1)}), s8[4194304]{0:T(1024)(128)(4,1)S(1)}, s32[]{:S(2)}) async-start(s8[8388608]{0:T(1024)(128)(4,1)} %bitcast.2), calls=%async_computation | async-start | bytes 8388608
  38.4 18.1 %slice-start.1 = ((s8[8388608]{0:T(1024)(128)(4,1)}), s8[4194304]{0:T(1024)(128)(4,1)S(1)}, s32[]{:S(2)}) async-start(s8[8388608]{0:T(1024)(128)(4,1)} %bitcast.2), calls=%async_computation.1 | async-start | bytes 8388608
  38.4 19.0 %collective-permute-start.11 = (bf16[2,128,1024]{2,1,0:T(8,128)(2,1)S(1)}, bf16[2,128,1024]{2,1,0:T(8,128)(2,1)S(1)}, u32[]{:S(2)}, u32[]{:S(2)}) collective-permute-start(bf16[2,128,1024]{2,1,0:T(8,128)(2,1)S(1)} %get-tuple-element.82.refs_3_), channel_id=1, source_target_pairs={{0,192},{64,0},{128,64},{192,128},{1,193},{65,1},{129,65},{193,129... | collective-permute-start | bytes 1572872 | tf_op jit(solution)/shard_map/ppermute | solution.py:24
  39.2 6.5 %collective-permute-start.8 = (bf16[2,64,1024]{2,1,0:T(8,128)(2,1)S(1)}, bf16[2,64,1024]{2,1,0:T(8,128)(2,1)S(1)}, u32[]{:S(2)}, u32[]{:S(2)}) collective-permute-start(bf16[2,64,1024]{2,1,0:T(8,128)(2,1)S(1)} %get-tuple-element.83.refs_1_), channel_id=1, source_target_pairs={{0,16},{16,0},{32,48},{48,32},{1,17},{17,1},{33,49},{49,33},{2,18}... | collective-permute-start | bytes 786440 | tf_op jit(solution)/shard_map/ppermute | solution.py:28
  39.4 13.7 %collective-permute-start.12 = (bf16[1,128,1024]{2,1,0:T(8,128)(2,1)S(1)}, bf16[1,128,1024]{2,1,0:T(8,128)(2,1)S(1)}, u32[]{:S(2)}, u32[]{:S(2)}) collective-permute-start(bf16[1,128,1024]{2,1,0:T(8,128)(2,1)S(1)} %get-tuple-element.90), channel_id=1, source_target_pairs={{0,64},{64,128},{128,192},{192,0},{1,65},{65,129},{129,193},{193,1... | collective-permute-start | bytes 786440 | tf_op jit(solution)/shard_map/ppermute | solution.py:24
  42.6 13.9 %collective-permute-start.13 = (bf16[1,128,1024]{2,1,0:T(8,128)(2,1)S(1)}, bf16[1,128,1024]{2,1,0:T(8,128)(2,1)S(1)}, u32[]{:S(2)}, u32[]{:S(2)}) collective-permute-start(bf16[1,128,1024]{2,1,0:T(8,128)(2,1)S(1)} %get-tuple-element.81.refs_3_), channel_id=1, source_target_pairs={{0,192},{64,0},{128,64},{192,128},{1,193},{65,1},{129,65},{193,129... | collective-permute-start | bytes 786440 | tf_op jit(solution)/shard_map/ppermute | solution.py:24
  56.5 11.6 %copy-start.1 = (f32[8,32,1024]{2,1,0:T(8,128)S(1)}, f32[8,32,1024]{2,1,0:T(8,128)}, u32[]{:S(2)}) copy-start(f32[8,32,1024]{2,1,0:T(8,128)} %refs_2_.7) | copy-start | bytes 3145732
  56.5 11.6 %copy-start.2 = (f32[8,32,1024]{2,1,0:T(8,128)S(1)}, f32[8,32,1024]{2,1,0:T(8,128)}, u32[]{:S(2)}) copy-start(f32[8,32,1024]{2,1,0:T(8,128)} %refs_3_.7) | copy-start | bytes 3145732
  58.1 10.7 %collective-permute-start.15 = (bf16[2,64,1024]{2,1,0:T(8,128)(2,1)S(1)}, bf16[2,64,1024]{2,1,0:T(8,128)(2,1)S(1)}, u32[]{:S(2)}, u32[]{:S(2)}) collective-permute-start(bf16[2,64,1024]{2,1,0:T(8,128)(2,1)S(1)} %get-tuple-element.92.refs_4_), channel_id=1, source_target_pairs={{0,16},{16,0},{32,48},{48,32},{1,17},{17,1},{33,49},{49,33},{2,18}... | collective-permute-start | bytes 786440 | tf_op jit(solution)/shard_map/ppermute | solution.py:28
  58.3 9.8 %collective-permute-start.9 = (bf16[2,32,1024]{2,1,0:T(8,128)(2,1)S(1)}, bf16[2,32,1024]{2,1,0:T(8,128)(2,1)S(1)}, u32[]{:S(2)}, u32[]{:S(2)}) collective-permute-start(bf16[2,32,1024]{2,1,0:T(8,128)(2,1)S(1)} %get-tuple-element.88.refs_3_), channel_id=1, source_target_pairs={{0,48},{16,32},{32,16},{48,0},{1,49},{17,33},{33,17},{49,1},{2,50}... | collective-permute-start | bytes 393224 | tf_op jit(solution)/shard_map/ppermute | solution.py:28
  62.0 20.1 %collective-permute-start.19 = (bf16[2,128,1024]{2,1,0:T(8,128)(2,1)S(1)}, bf16[2,128,1024]{2,1,0:T(8,128)(2,1)S(1)}, u32[]{:S(2)}, u32[]{:S(2)}) collective-permute-start(bf16[2,128,1024]{2,1,0:T(8,128)(2,1)S(1)} %get-tuple-element.100), channel_id=1, source_target_pairs={{0,64},{64,128},{128,192},{192,0},{1,65},{65,129},{129,193},{193,1... | collective-permute-start | bytes 1572872 | tf_op jit(solution)/shard_map/ppermute | solution.py:24
  62.3 21.6 %collective-permute-start.20 = (bf16[2,128,1024]{2,1,0:T(8,128)(2,1)S(1)}, bf16[2,128,1024]{2,1,0:T(8,128)(2,1)S(1)}, u32[]{:S(2)}, u32[]{:S(2)}) collective-permute-start(bf16[2,128,1024]{2,1,0:T(8,128)(2,1)S(1)} %get-tuple-element.91.refs_3_), channel_id=1, source_target_pairs={{0,192},{64,0},{128,64},{192,128},{1,193},{65,1},{129,65},{193,129... | collective-permute-start | bytes 1572872 | tf_op jit(solution)/shard_map/ppermute | solution.py:24
  64.1 13.4 %collective-permute-start.6 = (bf16[1,128,1024]{2,1,0:T(8,128)(2,1)S(1)}, bf16[1,128,1024]{2,1,0:T(8,128)(2,1)S(1)}, u32[]{:S(2)}, u32[]{:S(2)}) collective-permute-start(bf16[1,128,1024]{2,1,0:T(8,128)(2,1)S(1)} %get-tuple-element.84), channel_id=1, source_target_pairs={{0,64},{64,128},{128,192},{192,0},{1,65},{65,129},{129,193},{193,1... | collective-permute-start | bytes 786440 | tf_op jit(solution)/shard_map/ppermute | solution.py:24
  68.1 10.9 %collective-permute-start.7 = (bf16[1,128,1024]{2,1,0:T(8,128)(2,1)S(1)}, bf16[1,128,1024]{2,1,0:T(8,128)(2,1)S(1)}, u32[]{:S(2)}, u32[]{:S(2)}) collective-permute-start(bf16[1,128,1024]{2,1,0:T(8,128)(2,1)S(1)} %get-tuple-element.85.refs_2_), channel_id=1, source_target_pairs={{0,192},{64,0},{128,64},{192,128},{1,193},{65,1},{129,65},{193,129... | collective-permute-start | bytes 786440 | tf_op jit(solution)/shard_map/ppermute | solution.py:24
  68.8 6.9 %collective-permute-start.14 = (bf16[2,32,1024]{2,1,0:T(8,128)(2,1)S(1)}, bf16[2,32,1024]{2,1,0:T(8,128)(2,1)S(1)}, u32[]{:S(2)}, u32[]{:S(2)}) collective-permute-start(bf16[2,32,1024]{2,1,0:T(8,128)(2,1)S(1)} %get-tuple-element.93.refs_2_.refs_0_), channel_id=1, source_target_pairs={{0,48},{16,32},{32,16},{48,0},{1,49},{17,33},{33,17},{49,1},{2,50}... | collective-permute-start | bytes 393224 | tf_op jit(solution)/shard_map/ppermute | solution.py:28
  79.8 16.9 %collective-permute-start.16 = (bf16[2,128,1024]{2,1,0:T(8,128)(2,1)S(1)}, bf16[2,128,1024]{2,1,0:T(8,128)(2,1)S(1)}, u32[]{:S(2)}, u32[]{:S(2)}) collective-permute-start(bf16[2,128,1024]{2,1,0:T(8,128)(2,1)S(1)} %get-tuple-element.97), channel_id=1, source_target_pairs={{0,64},{64,128},{128,192},{192,0},{1,65},{65,129},{129,193},{193,1... | collective-permute-start | bytes 1572872 | tf_op jit(solution)/shard_map/ppermute | solution.py:24
  80.4 16.3 %collective-permute-start.17 = (bf16[2,128,1024]{2,1,0:T(8,128)(2,1)S(1)}, bf16[2,128,1024]{2,1,0:T(8,128)(2,1)S(1)}, u32[]{:S(2)}, u32[]{:S(2)}) collective-permute-start(bf16[2,128,1024]{2,1,0:T(8,128)(2,1)S(1)} %get-tuple-element.98.refs_3_), channel_id=1, source_target_pairs={{0,192},{64,0},{128,64},{192,128},{1,193},{65,1},{129,65},{193,129... | collective-permute-start | bytes 1572872 | tf_op jit(solution)/shard_map/ppermute | solution.py:24
  81.9 6.8 %collective-permute-start.18 = (bf16[2,32,1024]{2,1,0:T(8,128)(2,1)S(1)}, bf16[2,32,1024]{2,1,0:T(8,128)(2,1)S(1)}, u32[]{:S(2)}, u32[]{:S(2)}) collective-permute-start(bf16[2,32,1024]{2,1,0:T(8,128)(2,1)S(1)} %get-tuple-element.95.refs_2_), channel_id=1, source_target_pairs={{0,48},{16,32},{32,16},{48,0},{1,49},{17,33},{33,17},{49,1},{2,50}... | collective-permute-start | bytes 393224 | tf_op jit(solution)/shard_map/ppermute | solution.py:28
  82.2 9.7 %collective-permute-start.23 = (bf16[2,64,1024]{2,1,0:T(8,128)(2,1)S(1)}, bf16[2,64,1024]{2,1,0:T(8,128)(2,1)S(1)}, u32[]{:S(2)}, u32[]{:S(2)}) collective-permute-start(bf16[2,64,1024]{2,1,0:T(8,128)(2,1)S(1)} %get-tuple-element.104.refs_0_), channel_id=1, source_target_pairs={{0,16},{16,0},{32,48},{48,32},{1,17},{17,1},{33,49},{49,33},{2,18}... | collective-permute-start | bytes 786440 | tf_op jit(solution)/shard_map/ppermute | solution.py:28
  84.7 9.8 %collective-permute-start.22 = (bf16[2,64,1024]{2,1,0:T(8,128)(2,1)S(1)}, bf16[2,64,1024]{2,1,0:T(8,128)(2,1)S(1)}, u32[]{:S(2)}, u32[]{:S(2)}) collective-permute-start(bf16[2,64,1024]{2,1,0:T(8,128)(2,1)S(1)} %get-tuple-element.101.refs_4_), channel_id=1, source_target_pairs={{0,16},{16,0},{32,48},{48,32},{1,17},{17,1},{33,49},{49,33},{2,18}... | collective-permute-start | bytes 786440 | tf_op jit(solution)/shard_map/ppermute | solution.py:28
  89.3 6.8 %collective-permute-start.21 = (bf16[2,32,1024]{2,1,0:T(8,128)(2,1)S(1)}, bf16[2,32,1024]{2,1,0:T(8,128)(2,1)S(1)}, u32[]{:S(2)}, u32[]{:S(2)}) collective-permute-start(bf16[2,32,1024]{2,1,0:T(8,128)(2,1)S(1)} %get-tuple-element.102.refs_2_.refs_0_), channel_id=1, source_target_pairs={{0,48},{16,32},{32,16},{48,0},{1,49},{17,33},{33,17},{49,1},{2,50}... | collective-permute-start | bytes 393224 | tf_op jit(solution)/shard_map/ppermute | solution.py:28
  97.5 13.4 %collective-permute-start.24 = (bf16[2,64,1024]{2,1,0:T(8,128)(2,1)S(1)}, bf16[2,64,1024]{2,1,0:T(8,128)(2,1)S(1)}, u32[]{:S(2)}, u32[]{:S(2)}) collective-permute-start(bf16[2,64,1024]{2,1,0:T(8,128)(2,1)S(1)} %get-tuple-element.109.refs_4_), channel_id=1, source_target_pairs={{0,16},{16,0},{32,48},{48,32},{1,17},{17,1},{33,49},{49,33},{2,18}... | collective-permute-start | bytes 786440 | tf_op jit(solution)/shard_map/ppermute | solution.py:28
  103.8 8.1 %collective-permute-start.28 = (bf16[2,64,1024]{2,1,0:T(8,128)(2,1)S(1)}, bf16[2,64,1024]{2,1,0:T(8,128)(2,1)S(1)}, u32[]{:S(2)}, u32[]{:S(2)}) collective-permute-start(bf16[2,64,1024]{2,1,0:T(8,128)(2,1)S(1)} %get-tuple-element.114.refs_0_), channel_id=1, source_target_pairs={{0,16},{16,0},{32,48},{48,32},{1,17},{17,1},{33,49},{49,33},{2,18}... | collective-permute-start | bytes 786440 | tf_op jit(solution)/shard_map/ppermute | solution.py:28
  103.9 6.3 %collective-permute-start.25 = (bf16[2,32,1024]{2,1,0:T(8,128)(2,1)S(1)}, bf16[2,32,1024]{2,1,0:T(8,128)(2,1)S(1)}, u32[]{:S(2)}, u32[]{:S(2)}) collective-permute-start(bf16[2,32,1024]{2,1,0:T(8,128)(2,1)S(1)} %get-tuple-element.106.refs_2_), channel_id=1, source_target_pairs={{0,48},{16,32},{32,16},{48,0},{1,49},{17,33},{33,17},{49,1},{2,50}... | collective-permute-start | bytes 393224 | tf_op jit(solution)/shard_map/ppermute | solution.py:28
  103.9 25.7 %collective-permute-start.31 = (bf16[2,128,1024]{2,1,0:T(8,128)(2,1)S(1)}, bf16[2,128,1024]{2,1,0:T(8,128)(2,1)S(1)}, u32[]{:S(2)}, u32[]{:S(2)}) collective-permute-start(bf16[2,128,1024]{2,1,0:T(8,128)(2,1)S(1)} %get-tuple-element.105.refs_2_), channel_id=1, source_target_pairs={{0,64},{64,128},{128,192},{192,0},{1,65},{65,129},{129,193},{193,1... | collective-permute-start | bytes 1572872 | tf_op jit(solution)/shard_map/ppermute | solution.py:24
  106.0 24.2 %collective-permute-start.32 = (bf16[2,128,1024]{2,1,0:T(8,128)(2,1)S(1)}, bf16[2,128,1024]{2,1,0:T(8,128)(2,1)S(1)}, u32[]{:S(2)}, u32[]{:S(2)}) collective-permute-start(bf16[2,128,1024]{2,1,0:T(8,128)(2,1)S(1)} %get-tuple-element.105.refs_2_), channel_id=1, source_target_pairs={{0,192},{64,0},{128,64},{192,128},{1,193},{65,1},{129,65},{193,129... | collective-permute-start | bytes 1572872 | tf_op jit(solution)/shard_map/ppermute | solution.py:24
  113.3 27.0 %collective-permute-start.36 = (bf16[2,128,1024]{2,1,0:T(8,128)(2,1)S(1)}, bf16[2,128,1024]{2,1,0:T(8,128)(2,1)S(1)}, u32[]{:S(2)}, u32[]{:S(2)}) collective-permute-start(bf16[2,128,1024]{2,1,0:T(8,128)(2,1)S(1)} %get-tuple-element.116.refs_2_), channel_id=1, source_target_pairs={{0,64},{64,128},{128,192},{192,0},{1,65},{65,129},{129,193},{193,1... | collective-permute-start | bytes 1572872 | tf_op jit(solution)/shard_map/ppermute | solution.py:24
  118.3 6.5 %collective-permute-start.27 = (bf16[2,32,1024]{2,1,0:T(8,128)(2,1)S(1)}, bf16[2,32,1024]{2,1,0:T(8,128)(2,1)S(1)}, u32[]{:S(2)}, u32[]{:S(2)}) collective-permute-start(bf16[2,32,1024]{2,1,0:T(8,128)(2,1)S(1)} %get-tuple-element.111.refs_2_.refs_0_), channel_id=1, source_target_pairs={{0,48},{16,32},{32,16},{48,0},{1,49},{17,33},{33,17},{49,1},{2,50}... | collective-permute-start | bytes 393224 | tf_op jit(solution)/shard_map/ppermute | solution.py:28
  118.3 10.7 %collective-permute-start.26 = (bf16[2,32,1024]{2,1,0:T(8,128)(2,1)S(1)}, bf16[2,32,1024]{2,1,0:T(8,128)(2,1)S(1)}, u32[]{:S(2)}, u32[]{:S(2)}) collective-permute-start(bf16[2,32,1024]{2,1,0:T(8,128)(2,1)S(1)} %get-tuple-element.113.refs_3_), channel_id=1, source_target_pairs={{0,48},{16,32},{32,16},{48,0},{1,49},{17,33},{33,17},{49,1},{2,50}... | collective-permute-start | bytes 393224 | tf_op jit(solution)/shard_map/ppermute | solution.py:28
  125.3 9.7 %collective-permute-start.30 = (bf16[2,64,1024]{2,1,0:T(8,128)(2,1)S(1)}, bf16[2,64,1024]{2,1,0:T(8,128)(2,1)S(1)}, u32[]{:S(2)}, u32[]{:S(2)}) collective-permute-start(bf16[2,64,1024]{2,1,0:T(8,128)(2,1)S(1)} %get-tuple-element.119.refs_0_), channel_id=1, source_target_pairs={{0,16},{16,0},{32,48},{48,32},{1,17},{17,1},{33,49},{49,33},{2,18}... | collective-permute-start | bytes 786440 | tf_op jit(solution)/shard_map/ppermute | solution.py:28
  129.0 15.1 %collective-permute-start.37 = (bf16[2,128,1024]{2,1,0:T(8,128)(2,1)S(1)}, bf16[2,128,1024]{2,1,0:T(8,128)(2,1)S(1)}, u32[]{:S(2)}, u32[]{:S(2)}) collective-permute-start(bf16[2,128,1024]{2,1,0:T(8,128)(2,1)S(1)} %get-tuple-element.116.refs_2_), channel_id=1, source_target_pairs={{0,192},{64,0},{128,64},{192,128},{1,193},{65,1},{129,65},{193,129... | collective-permute-start | bytes 1572872 | tf_op jit(solution)/shard_map/ppermute | solution.py:24
  129.6 6.8 %collective-permute-start.29 = (bf16[2,32,1024]{2,1,0:T(8,128)(2,1)S(1)}, bf16[2,32,1024]{2,1,0:T(8,128)(2,1)S(1)}, u32[]{:S(2)}, u32[]{:S(2)}) collective-permute-start(bf16[2,32,1024]{2,1,0:T(8,128)(2,1)S(1)} %get-tuple-element.118.refs_3_.refs_0_), channel_id=1, source_target_pairs={{0,48},{16,32},{32,16},{48,0},{1,49},{17,33},{33,17},{49,1},{2,50}... | collective-permute-start | bytes 393224 | tf_op jit(solution)/shard_map/ppermute | solution.py:28
  131.8 13.9 %collective-permute-start.34 = (bf16[1,128,1024]{2,1,0:T(8,128)(2,1)S(1)}, bf16[1,128,1024]{2,1,0:T(8,128)(2,1)S(1)}, u32[]{:S(2)}, u32[]{:S(2)}) collective-permute-start(bf16[1,128,1024]{2,1,0:T(8,128)(2,1)S(1)} %get-tuple-element.125), channel_id=1, source_target_pairs={{0,64},{64,128},{128,192},{192,0},{1,65},{65,129},{129,193},{193,1... | collective-permute-start | bytes 786440 | tf_op jit(solution)/shard_map/ppermute | solution.py:24
  135.1 14.6 %collective-permute-start.35 = (bf16[1,128,1024]{2,1,0:T(8,128)(2,1)S(1)}, bf16[1,128,1024]{2,1,0:T(8,128)(2,1)S(1)}, u32[]{:S(2)}, u32[]{:S(2)}) collective-permute-start(bf16[1,128,1024]{2,1,0:T(8,128)(2,1)S(1)} %get-tuple-element.122.refs_3_), channel_id=1, source_target_pairs={{0,192},{64,0},{128,64},{192,128},{1,193},{65,1},{129,65},{193,129... | collective-permute-start | bytes 786440 | tf_op jit(solution)/shard_map/ppermute | solution.py:24
  136.5 20.4 %collective-permute-start.42 = (bf16[2,128,1024]{2,1,0:T(8,128)(2,1)S(1)}, bf16[2,128,1024]{2,1,0:T(8,128)(2,1)S(1)}, u32[]{:S(2)}, u32[]{:S(2)}) collective-permute-start(bf16[2,128,1024]{2,1,0:T(8,128)(2,1)S(1)} %get-tuple-element.123.refs_2_), channel_id=1, source_target_pairs={{0,64},{64,128},{128,192},{192,0},{1,65},{65,129},{129,193},{193,1... | collective-permute-start | bytes 1572872 | tf_op jit(solution)/shard_map/ppermute | solution.py:24
  140.4 10.7 %collective-permute-start.33 = (bf16[2,64,1024]{2,1,0:T(8,128)(2,1)S(1)}, bf16[2,64,1024]{2,1,0:T(8,128)(2,1)S(1)}, u32[]{:S(2)}, u32[]{:S(2)}) collective-permute-start(bf16[2,64,1024]{2,1,0:T(8,128)(2,1)S(1)} %get-tuple-element.124.refs_0_), channel_id=1, source_target_pairs={{0,16},{16,0},{32,48},{48,32},{1,17},{17,1},{33,49},{49,33},{2,18}... | collective-permute-start | bytes 786440 | tf_op jit(solution)/shard_map/ppermute | solution.py:28
  144.0 16.9 %collective-permute-start.43 = (bf16[2,128,1024]{2,1,0:T(8,128)(2,1)S(1)}, bf16[2,128,1024]{2,1,0:T(8,128)(2,1)S(1)}, u32[]{:S(2)}, u32[]{:S(2)}) collective-permute-start(bf16[2,128,1024]{2,1,0:T(8,128)(2,1)S(1)} %get-tuple-element.123.refs_2_), channel_id=1, source_target_pairs={{0,192},{64,0},{128,64},{192,128},{1,193},{65,1},{129,65},{193,129... | collective-permute-start | bytes 1572872 | tf_op jit(solution)/shard_map/ppermute | solution.py:24
  152.4 24.8 %collective-permute-start.38 = (bf16[2,128,1024]{2,1,0:T(8,128)(2,1)S(1)}, bf16[2,128,1024]{2,1,0:T(8,128)(2,1)S(1)}, u32[]{:S(2)}, u32[]{:S(2)}) collective-permute-start(bf16[2,128,1024]{2,1,0:T(8,128)(2,1)S(1)} %get-tuple-element.130.refs_3_), channel_id=1, source_target_pairs={{0,64},{64,128},{128,192},{192,0},{1,65},{65,129},{129,193},{193,1... | collective-permute-start | bytes 1572872 | tf_op jit(solution)/shard_map/ppermute | solution.py:24
  153.6 23.6 %collective-permute-start.39 = (bf16[2,128,1024]{2,1,0:T(8,128)(2,1)S(1)}, bf16[2,128,1024]{2,1,0:T(8,128)(2,1)S(1)}, u32[]{:S(2)}, u32[]{:S(2)}) collective-permute-start(bf16[2,128,1024]{2,1,0:T(8,128)(2,1)S(1)} %get-tuple-element.130.refs_3_), channel_id=1, source_target_pairs={{0,192},{64,0},{128,64},{192,128},{1,193},{65,1},{129,65},{193,129... | collective-permute-start | bytes 1572872 | tf_op jit(solution)/shard_map/ppermute | solution.py:24
  154.5 10.9 %collective-permute-start.40 = (bf16[1,128,1024]{2,1,0:T(8,128)(2,1)S(1)}, bf16[1,128,1024]{2,1,0:T(8,128)(2,1)S(1)}, u32[]{:S(2)}, u32[]{:S(2)}) collective-permute-start(bf16[1,128,1024]{2,1,0:T(8,128)(2,1)S(1)} %get-tuple-element.131), channel_id=1, source_target_pairs={{0,64},{64,128},{128,192},{192,0},{1,65},{65,129},{129,193},{193,1... | collective-permute-start | bytes 786440 | tf_op jit(solution)/shard_map/ppermute | solution.py:24
  156.9 19.0 %collective-permute-start.41 = (bf16[1,128,1024]{2,1,0:T(8,128)(2,1)S(1)}, bf16[1,128,1024]{2,1,0:T(8,128)(2,1)S(1)}, u32[]{:S(2)}, u32[]{:S(2)}) collective-permute-start(bf16[1,128,1024]{2,1,0:T(8,128)(2,1)S(1)} %get-tuple-element.129.refs_3_), channel_id=1, source_target_pairs={{0,192},{64,0},{128,64},{192,128},{1,193},{65,1},{129,65},{193,129... | collective-permute-start | bytes 786440 | tf_op jit(solution)/shard_map/ppermute | solution.py:24
  162.5 19.9 %collective-permute-start.46 = (bf16[1,128,1024]{2,1,0:T(8,128)(2,1)S(1)}, bf16[1,128,1024]{2,1,0:T(8,128)(2,1)S(1)}, u32[]{:S(2)}, u32[]{:S(2)}) collective-permute-start(bf16[1,128,1024]{2,1,0:T(8,128)(2,1)S(1)} %get-tuple-element.137), channel_id=1, source_target_pairs={{0,64},{64,128},{128,192},{192,0},{1,65},{65,129},{129,193},{193,1... | collective-permute-start | bytes 786440 | tf_op jit(solution)/shard_map/ppermute | solution.py:24
  165.4 17.0 %collective-permute-start.47 = (bf16[1,128,1024]{2,1,0:T(8,128)(2,1)S(1)}, bf16[1,128,1024]{2,1,0:T(8,128)(2,1)S(1)}, u32[]{:S(2)}, u32[]{:S(2)}) collective-permute-start(bf16[1,128,1024]{2,1,0:T(8,128)(2,1)S(1)} %get-tuple-element.134.refs_3_), channel_id=1, source_target_pairs={{0,192},{64,0},{128,64},{192,128},{1,193},{65,1},{129,65},{193,129... | collective-permute-start | bytes 786440 | tf_op jit(solution)/shard_map/ppermute | solution.py:24
  178.9 6.4 %collective-permute-start.44 = (bf16[1,128,1024]{2,1,0:T(8,128)(2,1)S(1)}, bf16[1,128,1024]{2,1,0:T(8,128)(2,1)S(1)}, u32[]{:S(2)}, u32[]{:S(2)}) collective-permute-start(bf16[1,128,1024]{2,1,0:T(8,128)(2,1)S(1)} %get-tuple-element.135), channel_id=1, source_target_pairs={{0,64},{64,128},{128,192},{192,0},{1,65},{65,129},{129,193},{193,1... | collective-permute-start | bytes 786440 | tf_op jit(solution)/shard_map/ppermute | solution.py:24
  179.0 7.6 %collective-permute-start.45 = (bf16[1,128,1024]{2,1,0:T(8,128)(2,1)S(1)}, bf16[1,128,1024]{2,1,0:T(8,128)(2,1)S(1)}, u32[]{:S(2)}, u32[]{:S(2)}) collective-permute-start(bf16[1,128,1024]{2,1,0:T(8,128)(2,1)S(1)} %get-tuple-element.136.refs_3_), channel_id=1, source_target_pairs={{0,192},{64,0},{128,64},{192,128},{1,193},{65,1},{129,65},{193,129... | collective-permute-start | bytes 786440 | tf_op jit(solution)/shard_map/ppermute | solution.py:24
where the time goes:
time: 188 us
  waiting for transfers between devices  80 us (43%)
  starting transfers between devices  68.8 us (37%)
  Pallas kernels  33.2 us (18%)
  local copies, waits for them, and re-layouts  3.4 us (2%)
    ppermute x32, waiting for transfers between devices, shift(): return lax.ppermute(a, 'y', [(i, (i + s) % NY) for i in range(NY)])  55.6 us
    ppermute x32, starting transfers between devices, shift(): return lax.ppermute(a, 'y', [(i, (i + s) % NY) for i in range(NY)])  43.2 us
    pallas_call x36, Pallas kernels, call(): pl.pallas_call(kernel, out_shape=[jax.ShapeDtypeStruct(s, t) for s, t, _...  33.2 us
    ppermute x16, starting transfers between devices, swap(): return lax.ppermute(a, 'z', [(i, i ^ k) for i in range(NZ)])  25.6 us
    ppermute x16, waiting for transfers between devices, swap(): return lax.ppermute(a, 'z', [(i, i ^ k) for i in range(NZ)])  24.4 us
  transfers between devices with their start and end apart: 48, of which 23 were waited for; matrix products, arithmetic and copies ran while one was open for 1% of the time, Pallas kernels for 15%

commit v1 on v0

--- a/solution.py
+++ b/solution.py
@@ -98,18 +98,33 @@
 
     def first(self, c):
         p, h, n, w = self.p, self.h, self.n, self.w
+        if self.last is None:
+            block = (self.where[0] + 2) % NY * n
+            far = [lax.dynamic_slice(self.x, (0, e * p, block, 0), (1, p, n, w))[0] for e in (c, c + 1)]
+            up = jnp.concatenate([t[h:] for t in far])
+            down = jnp.concatenate([t[:h] for t in far])
+            self.last = up
+            return shift(up, 1), shift(down, -1)
 
         def body(where, x, up, down, sems):
             move(
-                (x.at[self.of_x(where, c, 2, h, h)], up, sems.at[0]),
-                (x.at[self.of_x(where, c, 2, 0, h)], down, sems.at[1]),
+                (x.at[self.of_x(where, c, 2, h, h)], up.at[pl.ds(0, h)], sems.at[0]),
+                (x.at[self.of_x(where, c + 1, 2, h, h)], up.at[pl.ds(h, h)], sems.at[1]),
+                (x.at[self.of_x(where, c, 2, 0, h)], down.at[pl.ds(0, h)], sems.at[2]),
+                (x.at[self.of_x(where, c + 1, 2, 0, h)], down.at[pl.ds(h, h)], sems.at[3]),
             )
 
-        up, down = self.call(body, [(self.x, HBM)], [((h, n, w), BF16, ANY)] * 2, scratch=[pltpu.SemaphoreType.DMA((2,))])
+        up, down = self.call(
+            body,
+            [(self.x, HBM)],
+            [((2 * h, n, w), BF16, ANY)] * 2,
+            scratch=[pltpu.SemaphoreType.DMA((4,))],
+        )
         return shift(up, 1), shift(down, -1)
 
     def second(self, c, got):
         p, h, n, w = self.p, self.h, self.n, self.w
+        half = pl.BlockSpec((h, n, w), lambda i, w_: (c % 2, 0, 0))
 
         def body(where, x, below, above, up, down, sems):
             move(
@@ -125,7 +140,7 @@
 
         up, down = self.call(
             body,
-            [(self.x, HBM), (got[0], self.full((h, n, w))), (got[1], self.full((h, n, w)))],
+            [(self.x, HBM), (got[0], half), (got[1], half)],
             [((p, n, w), BF16, self.full((p, n, w)))] * 2,
             scratch=[pltpu.SemaphoreType.DMA((2,))],
         )
@@ -225,43 +240,59 @@
 
     def pass_on(self, c, got):
         p, h, n, w = self.p, self.h, self.n, self.w
-
-        def body(where, below, above, out, up, down, sems):
-            move(
-                (below.at[pl.ds(0, h)], up, sems.at[0]),
-                (above.at[pl.ds(h, h)], down, sems.at[1]),
-                (below, out.at[self.of_out(where, c, 3, 0, p)], sems.at[2]),
-                (above, out.at[self.of_out(where, c, 1, 0, p)], sems.at[3]),
-            )
+        many = len(got) // 2
+
+        def body(where, *refs):
+            came, (out, up, down, sems) = refs[: 2 * many], refs[2 * many :]
+            copies = []
+            for j in range(many):
+                below, above = came[2 * j], came[2 * j + 1]
+                copies += [
+                    (below.at[pl.ds(0, h)], up.at[pl.ds(j * h, h)], sems.at[4 * j]),
+                    (above.at[pl.ds(h, h)], down.at[pl.ds(j * h, h)], sems.at[4 * j + 1]),
+                    (below, out.at[self.of_out(where, c + j, 3, 0, p)], sems.at[4 * j + 2]),
+                    (above, out.at[self.of_out(where, c + j, 1, 0, p)], sems.at[4 * j + 3]),
+                ]
+            move(*copies)
 
         self.out, up, down = self.call(
             body,
             [(a, ANY) for a in got],
-            [(self.out.shape, BF16, HBM), ((h, n, w), BF16, ANY), ((h, n, w), BF16, ANY)],
+            [(self.out.shape, BF16, HBM)] + [((many * h, n, w), BF16, ANY)] * 2,
             alias=[(self.out, 0)],
-            scratch=[pltpu.SemaphoreType.DMA((4,))],
+            scratch=[pltpu.SemaphoreType.DMA((4 * many,))],
         )
         return shift(up, 1), shift(down, -1)
 
     def finish(self, c, got):
-        p, h, n, w = self.p, self.h, self.n, self.w
+        h = self.h
+        many = got[0].shape[0] // h
 
         def body(where, low, high, out, sems):
-            move(
-                (low, out.at[self.of_out(where, c, 2, 0, h)], sems.at[0]),
-                (high, out.at[self.of_out(where, c, 2, h, h)], sems.at[1]),
-            )
+            copies = []
+            for j in range(many):
+                r = pl.ds(j * h, h)
+                copies += [
+                    (low.at[r], out.at[self.of_out(where, c + j, 2, 0, h)], sems.at[2 * j]),
+                    (high.at[r], out.at[self.of_out(where, c + j, 2, h, h)], sems.at[2 * j + 1]),
+                ]
+            move(*copies)
 
         (self.out,) = self.call(
             body,
             [(a, ANY) for a in got],
             [(self.out.shape, BF16, HBM)],
             alias=[(self.out, 0)],
-            scratch=[pltpu.SemaphoreType.DMA((2,))],
-        )
-
-
-PLAN = "a0 a1 m0 a2 m1 s0 a3 h0 m2 s1 u0 h1 p0 m3 s2 u1 g0 h2 p1 s3 u2 h3 g1 p2 u3 o0 g2 p3 o1 f0 g3 o2 f1 o3 f2 f3"
+            scratch=[pltpu.SemaphoreType.DMA((2 * many,))],
+        )
+
+
+PLAN = (
+    "a0", "a2", "m0", "m1", "m2", "s0", "h0", "s1", "u0", "p0",
+    "h1", "s2", "m3", "u1", "h2", "p1", "g0", "u2", "s3", "g1",
+    "p2", "h3", "g2", "o0", "u3", "p3", "f0", "g3", "o2", "o3",
+    "f2", "f3",
+)
 
 
 def on_device(x, master, momentum):
@@ -269,9 +300,14 @@
     s = Steps(x, master, momentum, where)
     held = [None] * CHUNKS
     kinds = dict(a=None, m=s.second, s=s.third, h=s.fourth, u=s.update, p=s.pair, g=s.whole, o=s.pass_on, f=s.finish)
-    for step in PLAN.split():
+    for step in PLAN:
         c = int(step[1:])
-        held[c] = s.first(c) if step[0] == "a" else kinds[step[0]](c, held[c])
+        if step[0] == "a":
+            held[c] = held[c + 1] = s.first(c)
+        elif step == "o0":
+            held[c] = s.pass_on(c, held[c] + held[c + 1])
+        else:
+            held[c] = kinds[step[0]](c, held[c])
     join = lambda d: jnp.concatenate([d[c] for c in range(CHUNKS)])
     return s.out, join(s.new_master), join(s.new_momentum)
 

time: 188 us -> 168 us (0.89)
  waiting for transfers between devices: 80 us -> 70.6 us
  starting transfers between devices: 68.8 us -> 60.5 us
  Pallas kernels: 33.2 us -> 29.1 us
    ppermute x32 -> x26, starting transfers between devices: 43.2 us -> 28.1 us  [shift(): return lax.ppermute(a, 'y', [(i, (i + s) % NY) for i in range(NY)])]
    ppermute x32 -> x26, waiting for transfers between devices: 55.6 us -> 47.8 us  [shift(): return lax.ppermute(a, 'y', [(i, (i + s) % NY) for i in range(NY)])]
    ppermute x16, starting transfers between devices: 25.6 us -> 32.3 us  [swap(): return lax.ppermute(a, 'z', [(i, i ^ k) for i in range(NZ)])]
    pallas_call x36 -> x31, Pallas kernels: 33.2 us -> 29.1 us  [call(): pl.pallas_call(kernel, out_shape=[jax.ShapeDtypeStruct(s, t) for s, t, _...]
  transfers between devices with their start and end apart: 48 -> 42, of which waited for: 23 -> 22; matrix products, arithmetic and copies ran while one was open for 1% -> 1% of each run, Pallas kernels for 15% -> 17%
where the time goes in v1:
time: 168 us
  waiting for transfers between devices  70.6 us (42%)
  starting transfers between devices  60.5 us (36%)
  Pallas kernels  29.1 us (17%)
  local copies, waits for them, and re-layouts  4.68 us (3%)
  other arithmetic  1.74 us (1%)
    ppermute x26, waiting for transfers between devices, shift(): return lax.ppermute(a, 'y', [(i, (i + s) % NY) for i in range(NY)])  47.8 us
    ppermute x16, starting transfers between devices, swap(): return lax.ppermute(a, 'z', [(i, i ^ k) for i in range(NZ)])  32.3 us
    pallas_call x31, Pallas kernels, call(): pl.pallas_call(kernel, out_shape=[jax.ShapeDtypeStruct(s, t) for s, t, _...  29.1 us
    ppermute x26, starting transfers between devices, shift(): return lax.ppermute(a, 'y', [(i, (i + s) % NY) for i in range(NY)])  28.1 us
    ppermute x16, waiting for transfers between devices, swap(): return lax.ppermute(a, 'z', [(i, i ^ k) for i in range(NZ)])  22.8 us
    unnamed x10, local copies, waits for them, and re-layouts  3.4 us
  transfers between devices with their start and end apart: 42, of which 22 were waited for; matrix products, arithmetic and copies ran while one was open for 1% of the time, Pallas kernels for 17%

profile of v1, /device:TPU:56, one launch (start us, length us, event | category | flops | bytes accessed | tf_op | source)
XLA Modules:
  0.0 167.8 jit_solution(16956793463821024725)
XLA Ops:
  0.6 1.3 dynamic-slice_bitcast_fusion.1
  2.4 1.9 %collective-permute-start.3 = (bf16[2,128,1024]{2,1,0:T(8,128)(2,1)S(1)}, bf16[2,128,1024]{2,1,0:T(8,128)(2,1)S(1)}, u32[]{:S(2)}, u32[]{:S(2)}) collective-permute-start(bf16[2,128,1024]{2,1,0:T(8,128)(2,1)S(1)} %pad_maximum_fusion.3), channel_id=1, source_target_pairs={{0,192},{64,0},{128,64},{192,128},{1,193},{65,1},{129,65},{193,129... | collective-permute-start | bytes 1572872 | tf_op jit(solution)/shard_map/ppermute | solution.py:24
  4.3 3.4 %copy-done = bf16[1,8,512,1024]{3,2,1,0:T(8,128)(2,1)S(1)} copy-done((bf16[1,8,512,1024]{3,2,1,0:T(8,128)(2,1)S(1)}, bf16[1,8,512,1024]{3,2,1,0:T(8,128)(2,1)}, u32[]{:S(2)}) %copy-start) | copy-done | bytes 8388632
  8.4 1.5 collective-permute-start
  10.5 6.4 %collective-permute-done.2.refs_1_ = bf16[2,128,1024]{2,1,0:T(8,128)(2,1)S(1)} collective-permute-done((bf16[2,128,1024]{2,1,0:T(8,128)(2,1)S(1)}, bf16[2,128,1024]{2,1,0:T(8,128)(2,1)S(1)}, u32[]{:S(2)}, u32[]{:S(2)}) %collective-permute-start.2) | collective-permute-done | bytes 524320 | tf_op jit(solution)/shard_map/ppermute | solution.py:24
  16.9 1.6 collective-permute-done.3.refs_2_
  19.7 1.6 collective-permute-start.9
  22.2 1.7 collective-permute-start.6
  23.8 4.3 %collective-permute-done.refs_1_ = bf16[2,128,1024]{2,1,0:T(8,128)(2,1)S(1)} collective-permute-done((bf16[2,128,1024]{2,1,0:T(8,128)(2,1)S(1)}, bf16[2,128,1024]{2,1,0:T(8,128)(2,1)S(1)}, u32[]{:S(2)}, u32[]{:S(2)}) %collective-permute-start) | collective-permute-done | bytes 524320 | tf_op jit(solution)/shard_map/ppermute | solution.py:24
  28.9 0.8 collective-permute-done.1.refs_2_
  29.7 0.8 shard_map.61
  30.5 8.9 %collective-permute-done.8.refs_1_ = bf16[2,128,1024]{2,1,0:T(8,128)(2,1)S(1)} collective-permute-done((bf16[2,128,1024]{2,1,0:T(8,128)(2,1)S(1)}, bf16[2,128,1024]{2,1,0:T(8,128)(2,1)S(1)}, u32[]{:S(2)}, u32[]{:S(2)}) %collective-permute-start.8) | collective-permute-done | bytes 524320 | tf_op jit(solution)/shard_map/ppermute | solution.py:24
  39.4 1.6 collective-permute-done.9.refs_2_
  41.0 0.8 shard_map.62
  41.8 2.0 %collective-permute-start.10 = (bf16[2,64,1024]{2,1,0:T(8,128)(2,1)S(1)}, bf16[2,64,1024]{2,1,0:T(8,128)(2,1)S(1)}, u32[]{:S(2)}, u32[]{:S(2)}) collective-permute-start(bf16[2,64,1024]{2,1,0:T(8,128)(2,1)S(1)} %get-tuple-element.75.refs_2_), channel_id=1, source_target_pairs={{0,16},{16,0},{32,48},{48,32},{1,17},{17,1},{33,49},{49,33},{2,18}... | collective-permute-start | bytes 786440 | tf_op jit(solution)/shard_map/ppermute | solution.py:28
  43.7 2.0 %collective-permute-start.5 = (bf16[2,128,1024]{2,1,0:T(8,128)(2,1)S(1)}, bf16[2,128,1024]{2,1,0:T(8,128)(2,1)S(1)}, u32[]{:S(2)}, u32[]{:S(2)}) collective-permute-start(bf16[2,128,1024]{2,1,0:T(8,128)(2,1)S(1)} %get-tuple-element.71.refs_3_), channel_id=1, source_target_pairs={{0,192},{64,0},{128,64},{192,128},{1,193},{65,1},{129,65},{193,129... | collective-permute-start | bytes 1572872 | tf_op jit(solution)/shard_map/ppermute | solution.py:24
  45.8 2.5 %collective-permute-done.10.refs_1_ = bf16[2,64,1024]{2,1,0:T(8,128)(2,1)S(1)} collective-permute-done((bf16[2,64,1024]{2,1,0:T(8,128)(2,1)S(1)}, bf16[2,64,1024]{2,1,0:T(8,128)(2,1)S(1)}, u32[]{:S(2)}, u32[]{:S(2)}) %collective-permute-start.10) | collective-permute-done | bytes 262176 | tf_op jit(solution)/shard_map/ppermute | solution.py:28
  48.8 2.0 %collective-permute-start.12 = (bf16[2,32,1024]{2,1,0:T(8,128)(2,1)S(1)}, bf16[2,32,1024]{2,1,0:T(8,128)(2,1)S(1)}, u32[]{:S(2)}, u32[]{:S(2)}) collective-permute-start(bf16[2,32,1024]{2,1,0:T(8,128)(2,1)S(1)} %get-tuple-element.76.refs_3_), channel_id=1, source_target_pairs={{0,48},{16,32},{32,16},{48,0},{1,49},{17,33},{33,17},{49,1},{2,50}... | collective-permute-start | bytes 393224 | tf_op jit(solution)/shard_map/ppermute | solution.py:28
  50.8 1.3 collective-permute-done.7.refs_2_
  53.0 2.0 %collective-permute-start.11 = (bf16[2,64,1024]{2,1,0:T(8,128)(2,1)S(1)}, bf16[2,64,1024]{2,1,0:T(8,128)(2,1)S(1)}, u32[]{:S(2)}, u32[]{:S(2)}) collective-permute-start(bf16[2,64,1024]{2,1,0:T(8,128)(2,1)S(1)} %get-tuple-element.78.refs_4_), channel_id=1, source_target_pairs={{0,16},{16,0},{32,48},{48,32},{1,17},{17,1},{33,49},{49,33},{2,18}... | collective-permute-start | bytes 786440 | tf_op jit(solution)/shard_map/ppermute | solution.py:28
  55.6 2.0 %collective-permute-start.13 = (bf16[2,32,1024]{2,1,0:T(8,128)(2,1)S(1)}, bf16[2,32,1024]{2,1,0:T(8,128)(2,1)S(1)}, u32[]{:S(2)}, u32[]{:S(2)}) collective-permute-start(bf16[2,32,1024]{2,1,0:T(8,128)(2,1)S(1)} %get-tuple-element.80.refs_0_.refs_2_), channel_id=1, source_target_pairs={{0,48},{16,32},{32,16},{48,0},{1,49},{17,33},{33,17},{49,1},{2,50}... | collective-permute-start | bytes 393224 | tf_op jit(solution)/shard_map/ppermute | solution.py:28
  57.6 4.2 %collective-permute-done.13.refs_1_ = bf16[2,32,1024]{2,1,0:T(8,128)(2,1)S(1)} collective-permute-done((bf16[2,32,1024]{2,1,0:T(8,128)(2,1)S(1)}, bf16[2,32,1024]{2,1,0:T(8,128)(2,1)S(1)}, u32[]{:S(2)}, u32[]{:S(2)}) %collective-permute-start.13) | collective-permute-done | bytes 131104 | tf_op jit(solution)/shard_map/ppermute | solution.py:28
  63.0 1.2 collective-permute-start.17
  64.2 0.8 shard_map.68
  65.0 6.2 %collective-permute-start.16 = (bf16[2,64,1024]{2,1,0:T(8,128)(2,1)S(1)}, bf16[2,64,1024]{2,1,0:T(8,128)(2,1)S(1)}, u32[]{:S(2)}, u32[]{:S(2)}) collective-permute-start(bf16[2,64,1024]{2,1,0:T(8,128)(2,1)S(1)} %get-tuple-element.83.refs_3_), channel_id=1, source_target_pairs={{0,16},{16,0},{32,48},{48,32},{1,17},{17,1},{33,49},{49,33},{2,18}... | collective-permute-start | bytes 786440 | tf_op jit(solution)/shard_map/ppermute | solution.py:28
  71.3 0.8 shard_map.69
  72.6 1.6 collective-permute-start.15
  75.5 4.6 %collective-permute-done.16.refs_1_ = bf16[2,64,1024]{2,1,0:T(8,128)(2,1)S(1)} collective-permute-done((bf16[2,64,1024]{2,1,0:T(8,128)(2,1)S(1)}, bf16[2,64,1024]{2,1,0:T(8,128)(2,1)S(1)}, u32[]{:S(2)}, u32[]{:S(2)}) %collective-permute-start.16) | collective-permute-done | bytes 262176 | tf_op jit(solution)/shard_map/ppermute | solution.py:28
  80.7 1.3 collective-permute-start.18
  82.6 7.8 %collective-permute-start.23 = (bf16[2,64,1024]{2,1,0:T(8,128)(2,1)S(1)}, bf16[2,64,1024]{2,1,0:T(8,128)(2,1)S(1)}, u32[]{:S(2)}, u32[]{:S(2)}) collective-permute-start(bf16[2,64,1024]{2,1,0:T(8,128)(2,1)S(1)} %get-tuple-element.97.refs_0_), channel_id=1, source_target_pairs={{0,16},{16,0},{32,48},{48,32},{1,17},{17,1},{33,49},{49,33},{2,18}... | collective-permute-start | bytes 786440 | tf_op jit(solution)/shard_map/ppermute | solution.py:28
  90.4 1.4 shard_map.73
  92.5 0.8 shard_map.75
  93.3 2.1 %collective-permute-start.21 = (bf16[2,64,1024]{2,1,0:T(8,128)(2,1)S(1)}, bf16[2,64,1024]{2,1,0:T(8,128)(2,1)S(1)}, u32[]{:S(2)}, u32[]{:S(2)}) collective-permute-start(bf16[2,64,1024]{2,1,0:T(8,128)(2,1)S(1)} %get-tuple-element.96.refs_3_), channel_id=1, source_target_pairs={{0,16},{16,0},{32,48},{48,32},{1,17},{17,1},{33,49},{49,33},{2,18}... | collective-permute-start | bytes 786440 | tf_op jit(solution)/shard_map/ppermute | solution.py:28
  95.4 1.5 collective-permute-start.25
  97.4 1.4 shard_map.76
  98.8 2.8 %collective-permute-start.27 = (bf16[2,128,1024]{2,1,0:T(8,128)(2,1)S(1)}, bf16[2,128,1024]{2,1,0:T(8,128)(2,1)S(1)}, u32[]{:S(2)}, u32[]{:S(2)}) collective-permute-start(bf16[2,128,1024]{2,1,0:T(8,128)(2,1)S(1)} %get-tuple-element.99.refs_2_), channel_id=1, source_target_pairs={{0,64},{64,128},{128,192},{192,0},{1,65},{65,129},{129,193},{193,1... | collective-permute-start | bytes 1572872 | tf_op jit(solution)/shard_map/ppermute | solution.py:24
  102.2 1.2 collective-permute-done.21.refs_1_
  103.4 2.5 %collective-permute-start.29 = (bf16[2,64,1024]{2,1,0:T(8,128)(2,1)S(1)}, bf16[2,64,1024]{2,1,0:T(8,128)(2,1)S(1)}, u32[]{:S(2)}, u32[]{:S(2)}) collective-permute-start(bf16[2,64,1024]{2,1,0:T(8,128)(2,1)S(1)} %get-tuple-element.103.refs_0_), channel_id=1, source_target_pairs={{0,16},{16,0},{32,48},{48,32},{1,17},{17,1},{33,49},{49,33},{2,18}... | collective-permute-start | bytes 786440 | tf_op jit(solution)/shard_map/ppermute | solution.py:28
  106.5 5.2 %collective-permute-done.29.refs_1_ = bf16[2,64,1024]{2,1,0:T(8,128)(2,1)S(1)} collective-permute-done((bf16[2,64,1024]{2,1,0:T(8,128)(2,1)S(1)}, bf16[2,64,1024]{2,1,0:T(8,128)(2,1)S(1)}, u32[]{:S(2)}, u32[]{:S(2)}) %collective-permute-start.29) | collective-permute-done | bytes 262176 | tf_op jit(solution)/shard_map/ppermute | solution.py:28
  111.6 1.4 shard_map.79
  113.0 3.0 %collective-permute-done.28.refs_3_ = bf16[2,128,1024]{2,1,0:T(8,128)(2,1)S(1)} collective-permute-done((bf16[2,128,1024]{2,1,0:T(8,128)(2,1)S(1)}, bf16[2,128,1024]{2,1,0:T(8,128)(2,1)S(1)}, u32[]{:S(2)}, u32[]{:S(2)}) %collective-permute-start.28) | collective-permute-done | bytes 524320 | tf_op jit(solution)/shard_map/ppermute | solution.py:24
  116.0 2.0 %shard_map.80 = (bf16[8,512,1024]{2,1,0:T(8,128)(2,1)}, bf16[2,128,1024]{2,1,0:T(8,128)(2,1)S(1)}, bf16[2,128,1024]{2,1,0:T(8,128)(2,1)S(1)}) custom-call(s32[2]{0:T(128)S(1)} %pad_add_fusion.where, bf16[2,128,1024]{2,1,0:T(8,128)(2,1)S(1)} %collective-permute-done.25.refs_0_, ...), custom_call_target="tpu_custom_call", output_to_operand_aliasing={{0}: (5, {})} | custom-call | flops 1000 | bytes 1000 | tf_op jit(solution)/shard_map/pallas_call | solution.py:72
  118.5 1.7 collective-permute-start.33
  120.8 1.6 collective-permute-start.30
  122.4 5.1 %collective-permute-done.30.refs_1_ = bf16[2,32,1024]{2,1,0:T(8,128)(2,1)S(1)} collective-permute-done((bf16[2,32,1024]{2,1,0:T(8,128)(2,1)S(1)}, bf16[2,32,1024]{2,1,0:T(8,128)(2,1)S(1)}, u32[]{:S(2)}, u32[]{:S(2)}) %collective-permute-start.30) | collective-permute-done | bytes 131104 | tf_op jit(solution)/shard_map/ppermute | solution.py:28
  128.0 0.9 collective-permute-start.31
  128.9 1.8 %collective-permute-start.36 = (bf16[2,128,1024]{2,1,0:T(8,128)(2,1)S(1)}, bf16[2,128,1024]{2,1,0:T(8,128)(2,1)S(1)}, u32[]{:S(2)}, u32[]{:S(2)}) collective-permute-start(bf16[2,128,1024]{2,1,0:T(8,128)(2,1)S(1)} %get-tuple-element.106.refs_5_), channel_id=1, source_target_pairs={{0,64},{64,128},{128,192},{192,0},{1,65},{65,129},{129,193},{193,1... | collective-permute-start | bytes 1572872 | tf_op jit(solution)/shard_map/ppermute | solution.py:24
  131.0 1.8 %collective-permute-done.32.refs_0_ = bf16[2,128,1024]{2,1,0:T(8,128)(2,1)S(1)} collective-permute-done((bf16[2,128,1024]{2,1,0:T(8,128)(2,1)S(1)}, bf16[2,128,1024]{2,1,0:T(8,128)(2,1)S(1)}, u32[]{:S(2)}, u32[]{:S(2)}) %collective-permute-start.32) | collective-permute-done | bytes 524320 | tf_op jit(solution)/shard_map/ppermute | solution.py:24
  132.8 1.5 shard_map.83.refs_2_
  134.5 1.4 shard_map.84
  135.9 1.7 collective-permute-start.34
  138.0 6.1 %collective-permute-done.36.refs_0_ = bf16[2,128,1024]{2,1,0:T(8,128)(2,1)S(1)} collective-permute-done((bf16[2,128,1024]{2,1,0:T(8,128)(2,1)S(1)}, bf16[2,128,1024]{2,1,0:T(8,128)(2,1)S(1)}, u32[]{:S(2)}, u32[]{:S(2)}) %collective-permute-start.36) | collective-permute-done | bytes 524320 | tf_op jit(solution)/shard_map/ppermute | solution.py:24
  144.0 2.7 %collective-permute-done.37.refs_1_ = bf16[2,128,1024]{2,1,0:T(8,128)(2,1)S(1)} collective-permute-done((bf16[2,128,1024]{2,1,0:T(8,128)(2,1)S(1)}, bf16[2,128,1024]{2,1,0:T(8,128)(2,1)S(1)}, u32[]{:S(2)}, u32[]{:S(2)}) %collective-permute-start.37) | collective-permute-done | bytes 524320 | tf_op jit(solution)/shard_map/ppermute | solution.py:24
  146.8 1.6 shard_map.85
  148.5 2.0 %collective-permute-start.41 = (bf16[1,128,1024]{2,1,0:T(8,128)(2,1)S(1)}, bf16[1,128,1024]{2,1,0:T(8,128)(2,1)S(1)}, u32[]{:S(2)}, u32[]{:S(2)}) collective-permute-start(bf16[1,128,1024]{2,1,0:T(8,128)(2,1)S(1)} %get-tuple-element.116.refs_3_), channel_id=1, source_target_pairs={{0,192},{64,0},{128,64},{192,128},{1,193},{65,1},{129,65},{193,129... | collective-permute-start | bytes 786440 | tf_op jit(solution)/shard_map/ppermute | solution.py:24
  150.5 4.8 %collective-permute-done.34.refs_0_ = bf16[2,128,1024]{2,1,0:T(8,128)(2,1)S(1)} collective-permute-done((bf16[2,128,1024]{2,1,0:T(8,128)(2,1)S(1)}, bf16[2,128,1024]{2,1,0:T(8,128)(2,1)S(1)}, u32[]{:S(2)}, u32[]{:S(2)}) %collective-permute-start.34) | collective-permute-done | bytes 524320 | tf_op jit(solution)/shard_map/ppermute | solution.py:24
  155.3 1.7 collective-permute-done.35.refs_1_
  156.9 1.6 shard_map.86
  158.6 2.0 %collective-permute-start.39 = (bf16[1,128,1024]{2,1,0:T(8,128)(2,1)S(1)}, bf16[1,128,1024]{2,1,0:T(8,128)(2,1)S(1)}, u32[]{:S(2)}, u32[]{:S(2)}) collective-permute-start(bf16[1,128,1024]{2,1,0:T(8,128)(2,1)S(1)} %get-tuple-element.118.refs_3_), channel_id=1, source_target_pairs={{0,192},{64,0},{128,64},{192,128},{1,193},{65,1},{129,65},{193,129... | collective-permute-start | bytes 786440 | tf_op jit(solution)/shard_map/ppermute | solution.py:24
  160.6 1.6 pad_maximum_fusion
  162.2 1.4 shard_map.87.refs_2_
  163.6 1.4 collective-permute-done.38.refs_0_
  165.0 1.3 collective-permute-done.39.refs_1_
  166.3 1.4 shard_map.88
  (67 shorter events, 15.8 us)
Async XLA Ops:
  2.0 14.9 %collective-permute-start.2 = (bf16[2,128,1024]{2,1,0:T(8,128)(2,1)S(1)}, bf16[2,128,1024]{2,1,0:T(8,128)(2,1)S(1)}, u32[]{:S(2)}, u32[]{:S(2)}) collective-permute-start(bf16[2,128,1024]{2,1,0:T(8,128)(2,1)S(1)} %pad_maximum_fusion.2.refs_1_), channel_id=1, source_target_pairs={{0,64},{64,128},{128,192},{192,0},{1,65},{65,129},{129,193},{193,1... | collective-permute-start | bytes 1572872 | tf_op jit(solution)/shard_map/ppermute | solution.py:24
  2.4 16.1 %collective-permute-start.3 = (bf16[2,128,1024]{2,1,0:T(8,128)(2,1)S(1)}, bf16[2,128,1024]{2,1,0:T(8,128)(2,1)S(1)}, u32[]{:S(2)}, u32[]{:S(2)}) collective-permute-start(bf16[2,128,1024]{2,1,0:T(8,128)(2,1)S(1)} %pad_maximum_fusion.3), channel_id=1, source_target_pairs={{0,192},{64,0},{128,64},{192,128},{1,193},{65,1},{129,65},{193,129... | collective-permute-start | bytes 1572872 | tf_op jit(solution)/shard_map/ppermute | solution.py:24
  4.3 3.4 %copy-start = (bf16[1,8,512,1024]{3,2,1,0:T(8,128)(2,1)S(1)}, bf16[1,8,512,1024]{3,2,1,0:T(8,128)(2,1)}, u32[]{:S(2)}) copy-start(bf16[1,8,512,1024]{3,2,1,0:T(8,128)(2,1)} %refs_0_.17) | copy-start | bytes 25165828
  8.4 19.8 %collective-permute-start = (bf16[2,128,1024]{2,1,0:T(8,128)(2,1)S(1)}, bf16[2,128,1024]{2,1,0:T(8,128)(2,1)S(1)}, u32[]{:S(2)}, u32[]{:S(2)}) collective-permute-start(bf16[2,128,1024]{2,1,0:T(8,128)(2,1)S(1)} %get-tuple-element.66), channel_id=1, source_target_pairs={{0,64},{64,128},{128,192},{192,0},{1,65},{65,129},{129,193},{193,1... | collective-permute-start | bytes 1572872 | tf_op jit(solution)/shard_map/ppermute | solution.py:24
  9.9 19.8 %collective-permute-start.1 = (bf16[2,128,1024]{2,1,0:T(8,128)(2,1)S(1)}, bf16[2,128,1024]{2,1,0:T(8,128)(2,1)S(1)}, u32[]{:S(2)}, u32[]{:S(2)}) collective-permute-start(bf16[2,128,1024]{2,1,0:T(8,128)(2,1)S(1)} %get-tuple-element.67.refs_3_), channel_id=1, source_target_pairs={{0,192},{64,0},{128,64},{192,128},{1,193},{65,1},{129,65},{193,129... | collective-permute-start | bytes 1572872 | tf_op jit(solution)/shard_map/ppermute | solution.py:24
  19.3 20.1 %collective-permute-start.8 = (bf16[2,128,1024]{2,1,0:T(8,128)(2,1)S(1)}, bf16[2,128,1024]{2,1,0:T(8,128)(2,1)S(1)}, u32[]{:S(2)}, u32[]{:S(2)}) collective-permute-start(bf16[2,128,1024]{2,1,0:T(8,128)(2,1)S(1)} %get-tuple-element.73), channel_id=1, source_target_pairs={{0,64},{64,128},{128,192},{192,0},{1,65},{65,129},{129,193},{193,1... | collective-permute-start | bytes 1572872 | tf_op jit(solution)/shard_map/ppermute | solution.py:24
  19.7 21.2 %collective-permute-start.9 = (bf16[2,128,1024]{2,1,0:T(8,128)(2,1)S(1)}, bf16[2,128,1024]{2,1,0:T(8,128)(2,1)S(1)}, u32[]{:S(2)}, u32[]{:S(2)}) collective-permute-start(bf16[2,128,1024]{2,1,0:T(8,128)(2,1)S(1)} %get-tuple-element.68.refs_3_), channel_id=1, source_target_pairs={{0,192},{64,0},{128,64},{192,128},{1,193},{65,1},{129,65},{193,129... | collective-permute-start | bytes 1572872 | tf_op jit(solution)/shard_map/ppermute | solution.py:24
  22.2 28.7 %collective-permute-start.6 = (bf16[2,128,1024]{2,1,0:T(8,128)(2,1)S(1)}, bf16[2,128,1024]{2,1,0:T(8,128)(2,1)S(1)}, u32[]{:S(2)}, u32[]{:S(2)}) collective-permute-start(bf16[2,128,1024]{2,1,0:T(8,128)(2,1)S(1)} %get-tuple-element.72), channel_id=1, source_target_pairs={{0,64},{64,128},{128,192},{192,0},{1,65},{65,129},{129,193},{193,1... | collective-permute-start | bytes 1572872 | tf_op jit(solution)/shard_map/ppermute | solution.py:24
  28.1 24.1 %slice-start = ((s8[8388608]{0:T(1024)(128)(4,1)}), s8[4194304]{0:T(1024)(128)(4,1)S(1)}, s32[]{:S(2)}) async-start(s8[8388608]{0:T(1024)(128)(4,1)} %bitcast.10), calls=%async_computation | async-start | bytes 8388608
  28.1 24.1 %collective-permute-start.7 = (bf16[2,128,1024]{2,1,0:T(8,128)(2,1)S(1)}, bf16[2,128,1024]{2,1,0:T(8,128)(2,1)S(1)}, u32[]{:S(2)}, u32[]{:S(2)}) collective-permute-start(bf16[2,128,1024]{2,1,0:T(8,128)(2,1)S(1)} %get-tuple-element.69.refs_3_), channel_id=1, source_target_pairs={{0,192},{64,0},{128,64},{192,128},{1,193},{65,1},{129,65},{193,129... | collective-permute-start | bytes 1572872 | tf_op jit(solution)/shard_map/ppermute | solution.py:24
  40.9 11.2 %slice-start.1 = ((s8[8388608]{0:T(1024)(128)(4,1)}), s8[4194304]{0:T(1024)(128)(4,1)S(1)}, s32[]{:S(2)}) async-start(s8[8388608]{0:T(1024)(128)(4,1)} %bitcast.10), calls=%async_computation.1 | async-start | bytes 8388608
  40.9 14.0 %copy-start.1 = (f32[8,32,1024]{2,1,0:T(8,128)S(1)}, f32[8,32,1024]{2,1,0:T(8,128)}, u32[]{:S(2)}) copy-start(f32[8,32,1024]{2,1,0:T(8,128)} %refs_2_.7) | copy-start | bytes 3145732
  41.0 14.0 %copy-start.2 = (f32[8,32,1024]{2,1,0:T(8,128)S(1)}, f32[8,32,1024]{2,1,0:T(8,128)}, u32[]{:S(2)}) copy-start(f32[8,32,1024]{2,1,0:T(8,128)} %refs_3_.7) | copy-start | bytes 3145732
  41.8 6.5 %collective-permute-start.10 = (bf16[2,64,1024]{2,1,0:T(8,128)(2,1)S(1)}, bf16[2,64,1024]{2,1,0:T(8,128)(2,1)S(1)}, u32[]{:S(2)}, u32[]{:S(2)}) collective-permute-start(bf16[2,64,1024]{2,1,0:T(8,128)(2,1)S(1)} %get-tuple-element.75.refs_2_), channel_id=1, source_target_pairs={{0,16},{16,0},{32,48},{48,32},{1,17},{17,1},{33,49},{49,33},{2,18}... | collective-permute-start | bytes 786440 | tf_op jit(solution)/shard_map/ppermute | solution.py:28
  43.7 20.5 %collective-permute-start.4 = (bf16[2,128,1024]{2,1,0:T(8,128)(2,1)S(1)}, bf16[2,128,1024]{2,1,0:T(8,128)(2,1)S(1)}, u32[]{:S(2)}, u32[]{:S(2)}) collective-permute-start(bf16[2,128,1024]{2,1,0:T(8,128)(2,1)S(1)} %get-tuple-element.70), channel_id=1, source_target_pairs={{0,64},{64,128},{128,192},{192,0},{1,65},{65,129},{129,193},{193,1... | collective-permute-start | bytes 1572872 | tf_op jit(solution)/shard_map/ppermute | solution.py:24
  43.7 20.5 %collective-permute-start.5 = (bf16[2,128,1024]{2,1,0:T(8,128)(2,1)S(1)}, bf16[2,128,1024]{2,1,0:T(8,128)(2,1)S(1)}, u32[]{:S(2)}, u32[]{:S(2)}) collective-permute-start(bf16[2,128,1024]{2,1,0:T(8,128)(2,1)S(1)} %get-tuple-element.71.refs_3_), channel_id=1, source_target_pairs={{0,192},{64,0},{128,64},{192,128},{1,193},{65,1},{129,65},{193,129... | collective-permute-start | bytes 1572872 | tf_op jit(solution)/shard_map/ppermute | solution.py:24
  48.8 6.1 %collective-permute-start.12 = (bf16[2,32,1024]{2,1,0:T(8,128)(2,1)S(1)}, bf16[2,32,1024]{2,1,0:T(8,128)(2,1)S(1)}, u32[]{:S(2)}, u32[]{:S(2)}) collective-permute-start(bf16[2,32,1024]{2,1,0:T(8,128)(2,1)S(1)} %get-tuple-element.76.refs_3_), channel_id=1, source_target_pairs={{0,48},{16,32},{32,16},{48,0},{1,49},{17,33},{33,17},{49,1},{2,50}... | collective-permute-start | bytes 393224 | tf_op jit(solution)/shard_map/ppermute | solution.py:28
  53.0 9.4 %collective-permute-start.11 = (bf16[2,64,1024]{2,1,0:T(8,128)(2,1)S(1)}, bf16[2,64,1024]{2,1,0:T(8,128)(2,1)S(1)}, u32[]{:S(2)}, u32[]{:S(2)}) collective-permute-start(bf16[2,64,1024]{2,1,0:T(8,128)(2,1)S(1)} %get-tuple-element.78.refs_4_), channel_id=1, source_target_pairs={{0,16},{16,0},{32,48},{48,32},{1,17},{17,1},{33,49},{49,33},{2,18}... | collective-permute-start | bytes 786440 | tf_op jit(solution)/shard_map/ppermute | solution.py:28
  55.6 6.2 %collective-permute-start.13 = (bf16[2,32,1024]{2,1,0:T(8,128)(2,1)S(1)}, bf16[2,32,1024]{2,1,0:T(8,128)(2,1)S(1)}, u32[]{:S(2)}, u32[]{:S(2)}) collective-permute-start(bf16[2,32,1024]{2,1,0:T(8,128)(2,1)S(1)} %get-tuple-element.80.refs_0_.refs_2_), channel_id=1, source_target_pairs={{0,48},{16,32},{32,16},{48,0},{1,49},{17,33},{33,17},{49,1},{2,50}... | collective-permute-start | bytes 393224 | tf_op jit(solution)/shard_map/ppermute | solution.py:28
  63.0 11.2 %collective-permute-start.17 = (bf16[2,32,1024]{2,1,0:T(8,128)(2,1)S(1)}, bf16[2,32,1024]{2,1,0:T(8,128)(2,1)S(1)}, u32[]{:S(2)}, u32[]{:S(2)}) collective-permute-start(bf16[2,32,1024]{2,1,0:T(8,128)(2,1)S(1)} %get-tuple-element.82.refs_3_), channel_id=1, source_target_pairs={{0,48},{16,32},{32,16},{48,0},{1,49},{17,33},{33,17},{49,1},{2,50}... | collective-permute-start | bytes 393224 | tf_op jit(solution)/shard_map/ppermute | solution.py:28
  65.0 15.1 %collective-permute-start.16 = (bf16[2,64,1024]{2,1,0:T(8,128)(2,1)S(1)}, bf16[2,64,1024]{2,1,0:T(8,128)(2,1)S(1)}, u32[]{:S(2)}, u32[]{:S(2)}) collective-permute-start(bf16[2,64,1024]{2,1,0:T(8,128)(2,1)S(1)} %get-tuple-element.83.refs_3_), channel_id=1, source_target_pairs={{0,16},{16,0},{32,48},{48,32},{1,17},{17,1},{33,49},{49,33},{2,18}... | collective-permute-start | bytes 786440 | tf_op jit(solution)/shard_map/ppermute | solution.py:28
  72.1 20.4 %collective-permute-start.14 = (bf16[2,128,1024]{2,1,0:T(8,128)(2,1)S(1)}, bf16[2,128,1024]{2,1,0:T(8,128)(2,1)S(1)}, u32[]{:S(2)}, u32[]{:S(2)}) collective-permute-start(bf16[2,128,1024]{2,1,0:T(8,128)(2,1)S(1)} %get-tuple-element.84), channel_id=1, source_target_pairs={{0,64},{64,128},{128,192},{192,0},{1,65},{65,129},{129,193},{193,1... | collective-permute-start | bytes 1572872 | tf_op jit(solution)/shard_map/ppermute | solution.py:24
  72.6 19.9 %collective-permute-start.15 = (bf16[2,128,1024]{2,1,0:T(8,128)(2,1)S(1)}, bf16[2,128,1024]{2,1,0:T(8,128)(2,1)S(1)}, u32[]{:S(2)}, u32[]{:S(2)}) collective-permute-start(bf16[2,128,1024]{2,1,0:T(8,128)(2,1)S(1)} %get-tuple-element.85.refs_4_), channel_id=1, source_target_pairs={{0,192},{64,0},{128,64},{192,128},{1,193},{65,1},{129,65},{193,129... | collective-permute-start | bytes 1572872 | tf_op jit(solution)/shard_map/ppermute | solution.py:24
  74.2 16.2 %collective-permute-start.19 = (bf16[2,64,1024]{2,1,0:T(8,128)(2,1)S(1)}, bf16[2,64,1024]{2,1,0:T(8,128)(2,1)S(1)}, u32[]{:S(2)}, u32[]{:S(2)}) collective-permute-start(bf16[2,64,1024]{2,1,0:T(8,128)(2,1)S(1)} %get-tuple-element.91.refs_0_), channel_id=1, source_target_pairs={{0,16},{16,0},{32,48},{48,32},{1,17},{17,1},{33,49},{49,33},{2,18}... | collective-permute-start | bytes 786440 | tf_op jit(solution)/shard_map/ppermute | solution.py:28
  74.8 7.2 %collective-permute-start.20 = (bf16[2,32,1024]{2,1,0:T(8,128)(2,1)S(1)}, bf16[2,32,1024]{2,1,0:T(8,128)(2,1)S(1)}, u32[]{:S(2)}, u32[]{:S(2)}) collective-permute-start(bf16[2,32,1024]{2,1,0:T(8,128)(2,1)S(1)} %get-tuple-element.88.refs_2_.refs_0_), channel_id=1, source_target_pairs={{0,48},{16,32},{32,16},{48,0},{1,49},{17,33},{33,17},{49,1},{2,50}... | collective-permute-start | bytes 393224 | tf_op jit(solution)/shard_map/ppermute | solution.py:28
  80.7 11.0 %collective-permute-start.18 = (bf16[2,32,1024]{2,1,0:T(8,128)(2,1)S(1)}, bf16[2,32,1024]{2,1,0:T(8,128)(2,1)S(1)}, u32[]{:S(2)}, u32[]{:S(2)}) collective-permute-start(bf16[2,32,1024]{2,1,0:T(8,128)(2,1)S(1)} %get-tuple-element.90.refs_2_), channel_id=1, source_target_pairs={{0,48},{16,32},{32,16},{48,0},{1,49},{17,33},{33,17},{49,1},{2,50}... | collective-permute-start | bytes 393224 | tf_op jit(solution)/shard_map/ppermute | solution.py:28
  82.6 14.9 %collective-permute-start.23 = (bf16[2,64,1024]{2,1,0:T(8,128)(2,1)S(1)}, bf16[2,64,1024]{2,1,0:T(8,128)(2,1)S(1)}, u32[]{:S(2)}, u32[]{:S(2)}) collective-permute-start(bf16[2,64,1024]{2,1,0:T(8,128)(2,1)S(1)} %get-tuple-element.97.refs_0_), channel_id=1, source_target_pairs={{0,16},{16,0},{32,48},{48,32},{1,17},{17,1},{33,49},{49,33},{2,18}... | collective-permute-start | bytes 786440 | tf_op jit(solution)/shard_map/ppermute | solution.py:28
  92.4 9.2 %collective-permute-start.22 = (bf16[2,32,1024]{2,1,0:T(8,128)(2,1)S(1)}, bf16[2,32,1024]{2,1,0:T(8,128)(2,1)S(1)}, u32[]{:S(2)}, u32[]{:S(2)}) collective-permute-start(bf16[2,32,1024]{2,1,0:T(8,128)(2,1)S(1)} %get-tuple-element.94.refs_3_.refs_0_), channel_id=1, source_target_pairs={{0,48},{16,32},{32,16},{48,0},{1,49},{17,33},{33,17},{49,1},{2,50}... | collective-permute-start | bytes 393224 | tf_op jit(solution)/shard_map/ppermute | solution.py:28
  93.3 10.0 %collective-permute-start.21 = (bf16[2,64,1024]{2,1,0:T(8,128)(2,1)S(1)}, bf16[2,64,1024]{2,1,0:T(8,128)(2,1)S(1)}, u32[]{:S(2)}, u32[]{:S(2)}) collective-permute-start(bf16[2,64,1024]{2,1,0:T(8,128)(2,1)S(1)} %get-tuple-element.96.refs_3_), channel_id=1, source_target_pairs={{0,16},{16,0},{32,48},{48,32},{1,17},{17,1},{33,49},{49,33},{2,18}... | collective-permute-start | bytes 786440 | tf_op jit(solution)/shard_map/ppermute | solution.py:28
  95.4 17.6 %collective-permute-start.25 = (bf16[2,128,1024]{2,1,0:T(8,128)(2,1)S(1)}, bf16[2,128,1024]{2,1,0:T(8,128)(2,1)S(1)}, u32[]{:S(2)}, u32[]{:S(2)}) collective-permute-start(bf16[2,128,1024]{2,1,0:T(8,128)(2,1)S(1)} %get-tuple-element.93.refs_4_), channel_id=1, source_target_pairs={{0,64},{64,128},{128,192},{192,0},{1,65},{65,129},{129,193},{193,1... | collective-permute-start | bytes 1572872 | tf_op jit(solution)/shard_map/ppermute | solution.py:24
  96.9 16.1 %collective-permute-start.26 = (bf16[2,128,1024]{2,1,0:T(8,128)(2,1)S(1)}, bf16[2,128,1024]{2,1,0:T(8,128)(2,1)S(1)}, u32[]{:S(2)}, u32[]{:S(2)}) collective-permute-start(bf16[2,128,1024]{2,1,0:T(8,128)(2,1)S(1)} %get-tuple-element.93.refs_4_), channel_id=1, source_target_pairs={{0,192},{64,0},{128,64},{192,128},{1,193},{65,1},{129,65},{193,129... | collective-permute-start | bytes 1572872 | tf_op jit(solution)/shard_map/ppermute | solution.py:24
  98.8 14.2 %collective-permute-start.27 = (bf16[2,128,1024]{2,1,0:T(8,128)(2,1)S(1)}, bf16[2,128,1024]{2,1,0:T(8,128)(2,1)S(1)}, u32[]{:S(2)}, u32[]{:S(2)}) collective-permute-start(bf16[2,128,1024]{2,1,0:T(8,128)(2,1)S(1)} %get-tuple-element.99.refs_2_), channel_id=1, source_target_pairs={{0,64},{64,128},{128,192},{192,0},{1,65},{65,129},{129,193},{193,1... | collective-permute-start | bytes 1572872 | tf_op jit(solution)/shard_map/ppermute | solution.py:24
  101.6 14.4 %collective-permute-start.28 = (bf16[2,128,1024]{2,1,0:T(8,128)(2,1)S(1)}, bf16[2,128,1024]{2,1,0:T(8,128)(2,1)S(1)}, u32[]{:S(2)}, u32[]{:S(2)}) collective-permute-start(bf16[2,128,1024]{2,1,0:T(8,128)(2,1)S(1)} %get-tuple-element.99.refs_2_), channel_id=1, source_target_pairs={{0,192},{64,0},{128,64},{192,128},{1,193},{65,1},{129,65},{193,129... | collective-permute-start | bytes 1572872 | tf_op jit(solution)/shard_map/ppermute | solution.py:24
  103.4 8.2 %collective-permute-start.29 = (bf16[2,64,1024]{2,1,0:T(8,128)(2,1)S(1)}, bf16[2,64,1024]{2,1,0:T(8,128)(2,1)S(1)}, u32[]{:S(2)}, u32[]{:S(2)}) collective-permute-start(bf16[2,64,1024]{2,1,0:T(8,128)(2,1)S(1)} %get-tuple-element.103.refs_0_), channel_id=1, source_target_pairs={{0,16},{16,0},{32,48},{48,32},{1,17},{17,1},{33,49},{49,33},{2,18}... | collective-permute-start | bytes 786440 | tf_op jit(solution)/shard_map/ppermute | solution.py:28
  111.6 8.5 %collective-permute-start.24 = (bf16[2,32,1024]{2,1,0:T(8,128)(2,1)S(1)}, bf16[2,32,1024]{2,1,0:T(8,128)(2,1)S(1)}, u32[]{:S(2)}, u32[]{:S(2)}) collective-permute-start(bf16[2,32,1024]{2,1,0:T(8,128)(2,1)S(1)} %get-tuple-element.102.refs_3_), channel_id=1, source_target_pairs={{0,48},{16,32},{32,16},{48,0},{1,49},{17,33},{33,17},{49,1},{2,50}... | collective-permute-start | bytes 393224 | tf_op jit(solution)/shard_map/ppermute | solution.py:28
  118.0 14.8 %collective-permute-start.32 = (bf16[2,128,1024]{2,1,0:T(8,128)(2,1)S(1)}, bf16[2,128,1024]{2,1,0:T(8,128)(2,1)S(1)}, u32[]{:S(2)}, u32[]{:S(2)}) collective-permute-start(bf16[2,128,1024]{2,1,0:T(8,128)(2,1)S(1)} %get-tuple-element.110), channel_id=1, source_target_pairs={{0,64},{64,128},{128,192},{192,0},{1,65},{65,129},{129,193},{193,1... | collective-permute-start | bytes 1572872 | tf_op jit(solution)/shard_map/ppermute | solution.py:24
  118.5 14.3 %collective-permute-start.33 = (bf16[2,128,1024]{2,1,0:T(8,128)(2,1)S(1)}, bf16[2,128,1024]{2,1,0:T(8,128)(2,1)S(1)}, u32[]{:S(2)}, u32[]{:S(2)}) collective-permute-start(bf16[2,128,1024]{2,1,0:T(8,128)(2,1)S(1)} %get-tuple-element.107.refs_4_), channel_id=1, source_target_pairs={{0,192},{64,0},{128,64},{192,128},{1,193},{65,1},{129,65},{193,129... | collective-permute-start | bytes 1572872 | tf_op jit(solution)/shard_map/ppermute | solution.py:24
  120.8 6.7 %collective-permute-start.30 = (bf16[2,32,1024]{2,1,0:T(8,128)(2,1)S(1)}, bf16[2,32,1024]{2,1,0:T(8,128)(2,1)S(1)}, u32[]{:S(2)}, u32[]{:S(2)}) collective-permute-start(bf16[2,32,1024]{2,1,0:T(8,128)(2,1)S(1)} %get-tuple-element.108.refs_0_.refs_2_), channel_id=1, source_target_pairs={{0,48},{16,32},{32,16},{48,0},{1,49},{17,33},{33,17},{49,1},{2,50}... | collective-permute-start | bytes 393224 | tf_op jit(solution)/shard_map/ppermute | solution.py:28
  128.0 6.5 %collective-permute-start.31 = (bf16[2,64,1024]{2,1,0:T(8,128)(2,1)S(1)}, bf16[2,64,1024]{2,1,0:T(8,128)(2,1)S(1)}, u32[]{:S(2)}, u32[]{:S(2)}) collective-permute-start(bf16[2,64,1024]{2,1,0:T(8,128)(2,1)S(1)} %get-tuple-element.109.refs_0_), channel_id=1, source_target_pairs={{0,16},{16,0},{32,48},{48,32},{1,17},{17,1},{33,49},{49,33},{2,18}... | collective-permute-start | bytes 786440 | tf_op jit(solution)/shard_map/ppermute | solution.py:28
  128.9 15.1 %collective-permute-start.36 = (bf16[2,128,1024]{2,1,0:T(8,128)(2,1)S(1)}, bf16[2,128,1024]{2,1,0:T(8,128)(2,1)S(1)}, u32[]{:S(2)}, u32[]{:S(2)}) collective-permute-start(bf16[2,128,1024]{2,1,0:T(8,128)(2,1)S(1)} %get-tuple-element.106.refs_5_), channel_id=1, source_target_pairs={{0,64},{64,128},{128,192},{192,0},{1,65},{65,129},{129,193},{193,1... | collective-permute-start | bytes 1572872 | tf_op jit(solution)/shard_map/ppermute | solution.py:24
  130.7 16.1 %collective-permute-start.37 = (bf16[2,128,1024]{2,1,0:T(8,128)(2,1)S(1)}, bf16[2,128,1024]{2,1,0:T(8,128)(2,1)S(1)}, u32[]{:S(2)}, u32[]{:S(2)}) collective-permute-start(bf16[2,128,1024]{2,1,0:T(8,128)(2,1)S(1)} %get-tuple-element.106.refs_5_), channel_id=1, source_target_pairs={{0,192},{64,0},{128,64},{192,128},{1,193},{65,1},{129,65},{193,129... | collective-permute-start | bytes 1572872 | tf_op jit(solution)/shard_map/ppermute | solution.py:24
  135.9 19.4 %collective-permute-start.34 = (bf16[2,128,1024]{2,1,0:T(8,128)(2,1)S(1)}, bf16[2,128,1024]{2,1,0:T(8,128)(2,1)S(1)}, u32[]{:S(2)}, u32[]{:S(2)}) collective-permute-start(bf16[2,128,1024]{2,1,0:T(8,128)(2,1)S(1)} %get-tuple-element.113.refs_3_), channel_id=1, source_target_pairs={{0,64},{64,128},{128,192},{192,0},{1,65},{65,129},{129,193},{193,1... | collective-permute-start | bytes 1572872 | tf_op jit(solution)/shard_map/ppermute | solution.py:24
  137.5 19.4 %collective-permute-start.35 = (bf16[2,128,1024]{2,1,0:T(8,128)(2,1)S(1)}, bf16[2,128,1024]{2,1,0:T(8,128)(2,1)S(1)}, u32[]{:S(2)}, u32[]{:S(2)}) collective-permute-start(bf16[2,128,1024]{2,1,0:T(8,128)(2,1)S(1)} %get-tuple-element.113.refs_3_), channel_id=1, source_target_pairs={{0,192},{64,0},{128,64},{192,128},{1,193},{65,1},{129,65},{193,129... | collective-permute-start | bytes 1572872 | tf_op jit(solution)/shard_map/ppermute | solution.py:24
  148.4 13.8 %collective-permute-start.40 = (bf16[1,128,1024]{2,1,0:T(8,128)(2,1)S(1)}, bf16[1,128,1024]{2,1,0:T(8,128)(2,1)S(1)}, u32[]{:S(2)}, u32[]{:S(2)}) collective-permute-start(bf16[1,128,1024]{2,1,0:T(8,128)(2,1)S(1)} %get-tuple-element.119), channel_id=1, source_target_pairs={{0,64},{64,128},{128,192},{192,0},{1,65},{65,129},{129,193},{193,1... | collective-permute-start | bytes 786440 | tf_op jit(solution)/shard_map/ppermute | solution.py:24
  148.5 13.8 %collective-permute-start.41 = (bf16[1,128,1024]{2,1,0:T(8,128)(2,1)S(1)}, bf16[1,128,1024]{2,1,0:T(8,128)(2,1)S(1)}, u32[]{:S(2)}, u32[]{:S(2)}) collective-permute-start(bf16[1,128,1024]{2,1,0:T(8,128)(2,1)S(1)} %get-tuple-element.116.refs_3_), channel_id=1, source_target_pairs={{0,192},{64,0},{128,64},{192,128},{1,193},{65,1},{129,65},{193,129... | collective-permute-start | bytes 786440 | tf_op jit(solution)/shard_map/ppermute | solution.py:24
  158.5 6.4 %collective-permute-start.38 = (bf16[1,128,1024]{2,1,0:T(8,128)(2,1)S(1)}, bf16[1,128,1024]{2,1,0:T(8,128)(2,1)S(1)}, u32[]{:S(2)}, u32[]{:S(2)}) collective-permute-start(bf16[1,128,1024]{2,1,0:T(8,128)(2,1)S(1)} %get-tuple-element.117), channel_id=1, source_target_pairs={{0,64},{64,128},{128,192},{192,0},{1,65},{65,129},{129,193},{193,1... | collective-permute-start | bytes 786440 | tf_op jit(solution)/shard_map/ppermute | solution.py:24
  158.6 7.7 %collective-permute-start.39 = (bf16[1,128,1024]{2,1,0:T(8,128)(2,1)S(1)}, bf16[1,128,1024]{2,1,0:T(8,128)(2,1)S(1)}, u32[]{:S(2)}, u32[]{:S(2)}) collective-permute-start(bf16[1,128,1024]{2,1,0:T(8,128)(2,1)S(1)} %get-tuple-element.118.refs_3_), channel_id=1, source_target_pairs={{0,192},{64,0},{128,64},{192,128},{1,193},{65,1},{129,65},{193,129... | collective-permute-start | bytes 786440 | tf_op jit(solution)/shard_map/ppermute | solution.py:24

commit v2 on v1

--- a/solution.py
+++ b/solution.py
@@ -96,58 +96,61 @@
     def of_out(self, where, c, d, first, count):
         return (pl.ds(c * self.p + first, count), ds((where[0] + d) % NY, self.n))
 
-    def first(self, c):
+    def first(self, c, many):
         p, h, n, w = self.p, self.h, self.n, self.w
         if self.last is None:
             block = (self.where[0] + 2) % NY * n
-            far = [lax.dynamic_slice(self.x, (0, e * p, block, 0), (1, p, n, w))[0] for e in (c, c + 1)]
-            up = jnp.concatenate([t[h:] for t in far])
-            down = jnp.concatenate([t[:h] for t in far])
-            self.last = up
-            return shift(up, 1), shift(down, -1)
+            far = [lax.dynamic_slice(self.x, (0, (c + j) * p, block, 0), (1, p, n, w))[0] for j in range(many)]
+            self.last = up = jnp.concatenate([t[h:] for t in far])
+            return shift(up, 1), shift(jnp.concatenate([t[:h] for t in far]), -1)
 
         def body(where, x, up, down, sems):
-            move(
-                (x.at[self.of_x(where, c, 2, h, h)], up.at[pl.ds(0, h)], sems.at[0]),
-                (x.at[self.of_x(where, c + 1, 2, h, h)], up.at[pl.ds(h, h)], sems.at[1]),
-                (x.at[self.of_x(where, c, 2, 0, h)], down.at[pl.ds(0, h)], sems.at[2]),
-                (x.at[self.of_x(where, c + 1, 2, 0, h)], down.at[pl.ds(h, h)], sems.at[3]),
-            )
+            copies = []
+            for j in range(many):
+                r = pl.ds(j * h, h)
+                copies += [
+                    (x.at[self.of_x(where, c + j, 2, h, h)], up.at[r], sems.at[2 * j]),
+                    (x.at[self.of_x(where, c + j, 2, 0, h)], down.at[r], sems.at[2 * j + 1]),
+                ]
+            move(*copies)
 
         up, down = self.call(
             body,
             [(self.x, HBM)],
-            [((2 * h, n, w), BF16, ANY)] * 2,
-            scratch=[pltpu.SemaphoreType.DMA((4,))],
+            [((many * h, n, w), BF16, ANY)] * 2,
+            scratch=[pltpu.SemaphoreType.DMA((2 * many,))],
         )
         return shift(up, 1), shift(down, -1)
 
-    def second(self, c, got):
+    def second(self, c, many, got, j):
         p, h, n, w = self.p, self.h, self.n, self.w
-        half = pl.BlockSpec((h, n, w), lambda i, w_: (c % 2, 0, 0))
+        part = pl.BlockSpec((many * h, n, w), lambda i, w_: (j // many, 0, 0))
 
         def body(where, x, below, above, up, down, sems):
             move(
-                (x.at[self.of_x(where, c, 1, 0, p)], up, sems.at[0]),
-                (x.at[self.of_x(where, c, 3, 0, p)], down, sems.at[1]),
+                (x.at[self.of_x(where, c, 1, 0, many * p)], up, sems.at[0]),
+                (x.at[self.of_x(where, c, 3, 0, many * p)], down, sems.at[1]),
             )
 
             @pl.loop(0, n // ROWS)
             def _(i):
                 r = ds(i, ROWS)
-                up[h:, r] = (up[h:, r].astype(F32) + below[:, r].astype(F32)).astype(BF16)
-                down[:h, r] = (down[:h, r].astype(F32) + above[:, r].astype(F32)).astype(BF16)
+                for k in range(many):
+                    came, low, high = pl.ds(k * h, h), pl.ds(k * p, h), pl.ds(k * p + h, h)
+                    up[high, r] = (up[high, r].astype(F32) + below[came, r].astype(F32)).astype(BF16)
+                    down[low, r] = (down[low, r].astype(F32) + above[came, r].astype(F32)).astype(BF16)
 
         up, down = self.call(
             body,
-            [(self.x, HBM), (got[0], half), (got[1], half)],
-            [((p, n, w), BF16, self.full((p, n, w)))] * 2,
+            [(self.x, HBM), (got[0], part), (got[1], part)],
+            [((many * p, n, w), BF16, self.full((many * p, n, w)))] * 2,
             scratch=[pltpu.SemaphoreType.DMA((2,))],
         )
         return shift(up, 1), shift(down, -1)
 
-    def third(self, c, got):
+    def third(self, c, got, j):
         p, n, m, w = self.p, self.n, self.m, self.w
+        part = pl.BlockSpec((p, n, w), lambda i, w_: (j, 0, 0))
 
         def body(where, x, below, above, keep, send, own, sems):
             move((x.at[self.of_x(where, c, 0, 0, p)], own, sems.at[0]))
@@ -159,7 +162,7 @@
 
         keep, send = self.call(
             body,
-            [(self.x, HBM), (got[0], self.full((p, n, w))), (got[1], self.full((p, n, w)))],
+            [(self.x, HBM), (got[0], part), (got[1], part)],
             [
                 ((p, 2 * m, w), F32, self.full((p, 2 * m, w))),
                 ((p, 2 * m, w), BF16, self.full((p, 2 * m, w))),
@@ -288,26 +291,33 @@
 
 
 PLAN = (
-    "a0", "a2", "m0", "m1", "m2", "s0", "h0", "s1", "u0", "p0",
-    "h1", "s2", "m3", "u1", "h2", "p1", "g0", "u2", "s3", "g1",
-    "p2", "h3", "g2", "o0", "u3", "p3", "f0", "g3", "o2", "o3",
-    "f2", "f3",
+    "a0", "a12", "m0", "m1", "m2", "s0", "h0", "s1", "u0", "a3",
+    "h1", "s2", "p0", "m3", "u1", "h2", "p1", "g0", "u2", "s3",
+    "g1", "p2", "h3", "o0", "u3", "o1", "f0", "g2", "p3", "f1",
+    "g3", "o2", "o3", "f2", "f3",
 )
 
 
 def on_device(x, master, momentum):
     where = jnp.stack([lax.axis_index("y"), lax.axis_index("z")]).astype(jnp.int32)
     s = Steps(x, master, momentum, where)
-    held = [None] * CHUNKS
-    kinds = dict(a=None, m=s.second, s=s.third, h=s.fourth, u=s.update, p=s.pair, g=s.whole, o=s.pass_on, f=s.finish)
+    held = {}
+    stages = dict(h=s.fourth, u=s.update, p=s.pair, g=s.whole, f=s.finish)
     for step in PLAN:
-        c = int(step[1:])
-        if step[0] == "a":
-            held[c] = held[c + 1] = s.first(c)
-        elif step == "o0":
-            held[c] = s.pass_on(c, held[c] + held[c + 1])
+        kind, c, last = step[0], int(step[1]), int(step[-1])
+        chunks = range(c, last + 1)
+        if kind == "a":
+            got = s.first(c, len(chunks))
+        elif kind == "m":
+            got = s.second(c, len(chunks), *held[c])
+        elif kind == "s":
+            got = s.third(c, *held[c])
+        elif kind == "o":
+            got = s.pass_on(c, sum((held[e] for e in chunks), ()))
         else:
-            held[c] = kinds[step[0]](c, held[c])
+            got = stages[kind](c, held[c])
+        for j, e in enumerate(chunks):
+            held[e] = (got, j) if kind in "am" else got
     join = lambda d: jnp.concatenate([d[c] for c in range(CHUNKS)])
     return s.out, join(s.new_master), join(s.new_momentum)
 

time: 168 us -> 161 us (0.958)
  waiting for transfers between devices: 70.6 us -> 56.5 us
  starting transfers between devices: 60.5 us -> 63.9 us
  Pallas kernels: 29.1 us -> 32 us
    ppermute x16, waiting for transfers between devices: 22.8 us -> 9.64 us  [swap(): return lax.ppermute(a, 'z', [(i, i ^ k) for i in range(NZ)])]
    ppermute x26 -> x30, starting transfers between devices: 28.1 us -> 35.7 us  [shift(): return lax.ppermute(a, 'y', [(i, (i + s) % NY) for i in range(NY)])]
    ppermute x16, starting transfers between devices: 32.3 us -> 28.3 us  [swap(): return lax.ppermute(a, 'z', [(i, i ^ k) for i in range(NZ)])]
    pallas_call x31 -> x34, Pallas kernels: 29.1 us -> 32 us  [call(): pl.pallas_call(kernel, out_shape=[jax.ShapeDtypeStruct(s, t) for s, t, _...]
    ppermute x26 -> x30, waiting for transfers between devices: 47.8 us -> 46.8 us  [shift(): return lax.ppermute(a, 'y', [(i, (i + s) % NY) for i in range(NY)])]
  transfers between devices with their start and end apart: 42 -> 46, of which waited for: 22 -> 24; matrix products, arithmetic and copies ran while one was open for 1% -> 1% of each run, Pallas kernels for 17% -> 19%
where the time goes in v2:
time: 161 us; the launch traced here: 160 us
  starting transfers between devices  63.9 us (40%)
  waiting for transfers between devices  56.5 us (35%)
  Pallas kernels  32 us (20%)
  local copies, waits for them, and re-layouts  4.47 us (3%)
    ppermute x30, waiting for transfers between devices, shift(): return lax.ppermute(a, 'y', [(i, (i + s) % NY) for i in range(NY)])  46.8 us
    ppermute x30, starting transfers between devices, shift(): return lax.ppermute(a, 'y', [(i, (i + s) % NY) for i in range(NY)])  35.7 us
    pallas_call x34, Pallas kernels, call(): pl.pallas_call(kernel, out_shape=[jax.ShapeDtypeStruct(s, t) for s, t, _...  32 us
    ppermute x16, starting transfers between devices, swap(): return lax.ppermute(a, 'z', [(i, i ^ k) for i in range(NZ)])  28.3 us
    ppermute x16, waiting for transfers between devices, swap(): return lax.ppermute(a, 'z', [(i, i ^ k) for i in range(NZ)])  9.64 us
    unnamed x10, local copies, waits for them, and re-layouts  3.4 us
  transfers between devices with their start and end apart: 46, of which 24 were waited for; matrix products, arithmetic and copies ran while one was open for 1% of the time, Pallas kernels for 19%

profile of v2, /device:TPU:56, one launch (start us, length us, event | category | flops | bytes accessed | tf_op | source)
XLA Modules:
  0.0 159.6 jit_solution(14924218002574136800)
XLA Ops:
  0.6 1.1 dynamic-slice_bitcast_fusion
  2.0 1.8 %collective-permute-start.1 = (bf16[1,128,1024]{2,1,0:T(8,128)(2,1)S(1)}, bf16[1,128,1024]{2,1,0:T(8,128)(2,1)S(1)}, u32[]{:S(2)}, u32[]{:S(2)}) collective-permute-start(bf16[1,128,1024]{2,1,0:T(8,128)(2,1)S(1)} %get-tuple-element.139), channel_id=1, source_target_pairs={{0,192},{64,0},{128,64},{192,128},{1,193},{65,1},{129,65},{193,129... | collective-permute-start | bytes 786440 | tf_op jit(solution)/shard_map/ppermute | solution.py:24
  3.9 3.4 %copy-done = bf16[1,8,512,1024]{3,2,1,0:T(8,128)(2,1)S(1)} copy-done((bf16[1,8,512,1024]{3,2,1,0:T(8,128)(2,1)S(1)}, bf16[1,8,512,1024]{3,2,1,0:T(8,128)(2,1)}, u32[]{:S(2)}) %copy-start) | copy-done | bytes 8388632
  8.0 1.5 collective-permute-start.4
  10.1 1.1 collective-permute-done.1.refs_2_
  11.9 1.6 %collective-permute-start.2 = (bf16[2,128,1024]{2,1,0:T(8,128)(2,1)S(1)}, bf16[2,128,1024]{2,1,0:T(8,128)(2,1)S(1)}, u32[]{:S(2)}, u32[]{:S(2)}) collective-permute-start(bf16[2,128,1024]{2,1,0:T(8,128)(2,1)S(1)} %get-tuple-element.72), channel_id=1, source_target_pairs={{0,64},{64,128},{128,192},{192,0},{1,65},{65,129},{129,193},{193,1... | collective-permute-start | bytes 1572872 | tf_op jit(solution)/shard_map/ppermute | solution.py:24
  14.0 8.9 %collective-permute-done.4.refs_1_ = bf16[2,128,1024]{2,1,0:T(8,128)(2,1)S(1)} collective-permute-done((bf16[2,128,1024]{2,1,0:T(8,128)(2,1)S(1)}, bf16[2,128,1024]{2,1,0:T(8,128)(2,1)S(1)}, u32[]{:S(2)}, u32[]{:S(2)}) %collective-permute-start.4) | collective-permute-done | bytes 524320 | tf_op jit(solution)/shard_map/ppermute | solution.py:24
  22.9 2.6 %collective-permute-done.5.refs_2_ = bf16[2,128,1024]{2,1,0:T(8,128)(2,1)S(1)} collective-permute-done((bf16[2,128,1024]{2,1,0:T(8,128)(2,1)S(1)}, bf16[2,128,1024]{2,1,0:T(8,128)(2,1)S(1)}, u32[]{:S(2)}, u32[]{:S(2)}) %collective-permute-start.5) | collective-permute-done | bytes 524320 | tf_op jit(solution)/shard_map/ppermute | solution.py:24
  26.4 2.0 %collective-permute-start.9 = (bf16[2,128,1024]{2,1,0:T(8,128)(2,1)S(1)}, bf16[2,128,1024]{2,1,0:T(8,128)(2,1)S(1)}, u32[]{:S(2)}, u32[]{:S(2)}) collective-permute-start(bf16[2,128,1024]{2,1,0:T(8,128)(2,1)S(1)} %get-tuple-element.75.refs_3_), channel_id=1, source_target_pairs={{0,192},{64,0},{128,64},{192,128},{1,193},{65,1},{129,65},{193,129... | collective-permute-start | bytes 1572872 | tf_op jit(solution)/shard_map/ppermute | solution.py:24
  29.2 4.9 %collective-permute-done.2.refs_1_ = bf16[2,128,1024]{2,1,0:T(8,128)(2,1)S(1)} collective-permute-done((bf16[2,128,1024]{2,1,0:T(8,128)(2,1)S(1)}, bf16[2,128,1024]{2,1,0:T(8,128)(2,1)S(1)}, u32[]{:S(2)}, u32[]{:S(2)}) %collective-permute-start.2) | collective-permute-done | bytes 524320 | tf_op jit(solution)/shard_map/ppermute | solution.py:24
  34.1 2.6 %collective-permute-done.3.refs_2_ = bf16[2,128,1024]{2,1,0:T(8,128)(2,1)S(1)} collective-permute-done((bf16[2,128,1024]{2,1,0:T(8,128)(2,1)S(1)}, bf16[2,128,1024]{2,1,0:T(8,128)(2,1)S(1)}, u32[]{:S(2)}, u32[]{:S(2)}) %collective-permute-start.3) | collective-permute-done | bytes 524320 | tf_op jit(solution)/shard_map/ppermute | solution.py:24
  37.6 1.9 %collective-permute-start.6 = (bf16[2,64,1024]{2,1,0:T(8,128)(2,1)S(1)}, bf16[2,64,1024]{2,1,0:T(8,128)(2,1)S(1)}, u32[]{:S(2)}, u32[]{:S(2)}) collective-permute-start(bf16[2,64,1024]{2,1,0:T(8,128)(2,1)S(1)} %get-tuple-element.78.refs_2_), channel_id=1, source_target_pairs={{0,16},{16,0},{32,48},{48,32},{1,17},{17,1},{33,49},{49,33},{2,18}... | collective-permute-start | bytes 786440 | tf_op jit(solution)/shard_map/ppermute | solution.py:28
  39.5 2.0 %collective-permute-start.14 = (bf16[2,128,1024]{2,1,0:T(8,128)(2,1)S(1)}, bf16[2,128,1024]{2,1,0:T(8,128)(2,1)S(1)}, u32[]{:S(2)}, u32[]{:S(2)}) collective-permute-start(bf16[2,128,1024]{2,1,0:T(8,128)(2,1)S(1)} %get-tuple-element.76.refs_3_), channel_id=1, source_target_pairs={{0,192},{64,0},{128,64},{192,128},{1,193},{65,1},{129,65},{193,129... | collective-permute-start | bytes 1572872 | tf_op jit(solution)/shard_map/ppermute | solution.py:24
  41.5 2.5 %collective-permute-done.6.refs_1_ = bf16[2,64,1024]{2,1,0:T(8,128)(2,1)S(1)} collective-permute-done((bf16[2,64,1024]{2,1,0:T(8,128)(2,1)S(1)}, bf16[2,64,1024]{2,1,0:T(8,128)(2,1)S(1)}, u32[]{:S(2)}, u32[]{:S(2)}) %collective-permute-start.6) | collective-permute-done | bytes 262176 | tf_op jit(solution)/shard_map/ppermute | solution.py:28
  44.6 3.0 %collective-permute-start.7 = (bf16[2,32,1024]{2,1,0:T(8,128)(2,1)S(1)}, bf16[2,32,1024]{2,1,0:T(8,128)(2,1)S(1)}, u32[]{:S(2)}, u32[]{:S(2)}) collective-permute-start(bf16[2,32,1024]{2,1,0:T(8,128)(2,1)S(1)} %get-tuple-element.80.refs_3_), channel_id=1, source_target_pairs={{0,48},{16,32},{32,16},{48,0},{1,49},{17,33},{33,17},{49,1},{2,50}... | collective-permute-start | bytes 393224 | tf_op jit(solution)/shard_map/ppermute | solution.py:28
  48.8 1.9 %collective-permute-start.15 = (bf16[2,64,1024]{2,1,0:T(8,128)(2,1)S(1)}, bf16[2,64,1024]{2,1,0:T(8,128)(2,1)S(1)}, u32[]{:S(2)}, u32[]{:S(2)}) collective-permute-start(bf16[2,64,1024]{2,1,0:T(8,128)(2,1)S(1)} %get-tuple-element.82.refs_4_), channel_id=1, source_target_pairs={{0,16},{16,0},{32,48},{48,32},{1,17},{17,1},{33,49},{49,33},{2,18}... | collective-permute-start | bytes 786440 | tf_op jit(solution)/shard_map/ppermute | solution.py:28
  52.1 2.0 %collective-permute-start.11 = (bf16[1,128,1024]{2,1,0:T(8,128)(2,1)S(1)}, bf16[1,128,1024]{2,1,0:T(8,128)(2,1)S(1)}, u32[]{:S(2)}, u32[]{:S(2)}) collective-permute-start(bf16[1,128,1024]{2,1,0:T(8,128)(2,1)S(1)} %get-tuple-element.85.refs_2_), channel_id=1, source_target_pairs={{0,192},{64,0},{128,64},{192,128},{1,193},{65,1},{129,65},{193,129... | collective-permute-start | bytes 786440 | tf_op jit(solution)/shard_map/ppermute | solution.py:24
  54.1 1.1 collective-permute-done.15.refs_1_
  55.3 2.2 %collective-permute-start.12 = (bf16[2,32,1024]{2,1,0:T(8,128)(2,1)S(1)}, bf16[2,32,1024]{2,1,0:T(8,128)(2,1)S(1)}, u32[]{:S(2)}, u32[]{:S(2)}) collective-permute-start(bf16[2,32,1024]{2,1,0:T(8,128)(2,1)S(1)} %get-tuple-element.83.refs_1_.refs_0_), channel_id=1, source_target_pairs={{0,48},{16,32},{32,16},{48,0},{1,49},{17,33},{33,17},{49,1},{2,50}... | collective-permute-start | bytes 393224 | tf_op jit(solution)/shard_map/ppermute | solution.py:28
  58.1 1.2 collective-permute-done.14.refs_2_
  60.0 1.5 collective-permute-start.18
  62.1 0.9 collective-permute-done.11.refs_2_
  64.1 1.9 %collective-permute-start.19 = (bf16[2,32,1024]{2,1,0:T(8,128)(2,1)S(1)}, bf16[2,32,1024]{2,1,0:T(8,128)(2,1)S(1)}, u32[]{:S(2)}, u32[]{:S(2)}) collective-permute-start(bf16[2,32,1024]{2,1,0:T(8,128)(2,1)S(1)} %get-tuple-element.88.refs_3_), channel_id=1, source_target_pairs={{0,48},{16,32},{32,16},{48,0},{1,49},{17,33},{33,17},{49,1},{2,50}... | collective-permute-start | bytes 393224 | tf_op jit(solution)/shard_map/ppermute | solution.py:28
  66.0 1.7 %collective-permute-start.17 = (bf16[2,128,1024]{2,1,0:T(8,128)(2,1)S(1)}, bf16[2,128,1024]{2,1,0:T(8,128)(2,1)S(1)}, u32[]{:S(2)}, u32[]{:S(2)}) collective-permute-start(bf16[2,128,1024]{2,1,0:T(8,128)(2,1)S(1)} %get-tuple-element.92.refs_4_), channel_id=1, source_target_pairs={{0,192},{64,0},{128,64},{192,128},{1,193},{65,1},{129,65},{193,129... | collective-permute-start | bytes 1572872 | tf_op jit(solution)/shard_map/ppermute | solution.py:24
  67.8 2.9 %collective-permute-start.21 = (bf16[2,64,1024]{2,1,0:T(8,128)(2,1)S(1)}, bf16[2,64,1024]{2,1,0:T(8,128)(2,1)S(1)}, u32[]{:S(2)}, u32[]{:S(2)}) collective-permute-start(bf16[2,64,1024]{2,1,0:T(8,128)(2,1)S(1)} %get-tuple-element.98.refs_0_), channel_id=1, source_target_pairs={{0,16},{16,0},{32,48},{48,32},{1,17},{17,1},{33,49},{49,33},{2,18}... | collective-permute-start | bytes 786440 | tf_op jit(solution)/shard_map/ppermute | solution.py:28
  71.3 2.2 %collective-permute-start.22 = (bf16[2,32,1024]{2,1,0:T(8,128)(2,1)S(1)}, bf16[2,32,1024]{2,1,0:T(8,128)(2,1)S(1)}, u32[]{:S(2)}, u32[]{:S(2)}) collective-permute-start(bf16[2,32,1024]{2,1,0:T(8,128)(2,1)S(1)} %get-tuple-element.95.refs_2_.refs_0_), channel_id=1, source_target_pairs={{0,48},{16,32},{32,16},{48,0},{1,49},{17,33},{33,17},{49,1},{2,50}... | collective-permute-start | bytes 393224 | tf_op jit(solution)/shard_map/ppermute | solution.py:28
  74.2 5.2 %collective-permute-done.22.refs_1_ = bf16[2,32,1024]{2,1,0:T(8,128)(2,1)S(1)} collective-permute-done((bf16[2,32,1024]{2,1,0:T(8,128)(2,1)S(1)}, bf16[2,32,1024]{2,1,0:T(8,128)(2,1)S(1)}, u32[]{:S(2)}, u32[]{:S(2)}) %collective-permute-start.22) | collective-permute-done | bytes 131104 | tf_op jit(solution)/shard_map/ppermute | solution.py:28
  80.0 4.1 %collective-permute-start.25 = (bf16[2,64,1024]{2,1,0:T(8,128)(2,1)S(1)}, bf16[2,64,1024]{2,1,0:T(8,128)(2,1)S(1)}, u32[]{:S(2)}, u32[]{:S(2)}) collective-permute-start(bf16[2,64,1024]{2,1,0:T(8,128)(2,1)S(1)} %get-tuple-element.104.refs_0_), channel_id=1, source_target_pairs={{0,16},{16,0},{32,48},{48,32},{1,17},{17,1},{33,49},{49,33},{2,18}... | collective-permute-start | bytes 786440 | tf_op jit(solution)/shard_map/ppermute | solution.py:28
  84.1 1.4 shard_map.74
  85.6 3.0 %collective-permute-start.28 = (bf16[2,128,1024]{2,1,0:T(8,128)(2,1)S(1)}, bf16[2,128,1024]{2,1,0:T(8,128)(2,1)S(1)}, u32[]{:S(2)}, u32[]{:S(2)}) collective-permute-start(bf16[2,128,1024]{2,1,0:T(8,128)(2,1)S(1)} %get-tuple-element.100.refs_4_), channel_id=1, source_target_pairs={{0,192},{64,0},{128,64},{192,128},{1,193},{65,1},{129,65},{193,129... | collective-permute-start | bytes 1572872 | tf_op jit(solution)/shard_map/ppermute | solution.py:24
  90.6 1.0 collective-permute-start.23
  91.7 1.4 shard_map.77
  93.1 2.1 %collective-permute-start.33 = (bf16[2,128,1024]{2,1,0:T(8,128)(2,1)S(1)}, bf16[2,128,1024]{2,1,0:T(8,128)(2,1)S(1)}, u32[]{:S(2)}, u32[]{:S(2)}) collective-permute-start(bf16[2,128,1024]{2,1,0:T(8,128)(2,1)S(1)} %get-tuple-element.106.refs_2_), channel_id=1, source_target_pairs={{0,64},{64,128},{128,192},{192,0},{1,65},{65,129},{129,193},{193,1... | collective-permute-start | bytes 1572872 | tf_op jit(solution)/shard_map/ppermute | solution.py:24
  95.7 2.2 %collective-permute-start.34 = (bf16[2,128,1024]{2,1,0:T(8,128)(2,1)S(1)}, bf16[2,128,1024]{2,1,0:T(8,128)(2,1)S(1)}, u32[]{:S(2)}, u32[]{:S(2)}) collective-permute-start(bf16[2,128,1024]{2,1,0:T(8,128)(2,1)S(1)} %get-tuple-element.106.refs_2_), channel_id=1, source_target_pairs={{0,192},{64,0},{128,64},{192,128},{1,193},{65,1},{129,65},{193,129... | collective-permute-start | bytes 1572872 | tf_op jit(solution)/shard_map/ppermute | solution.py:24
  99.5 1.8 %collective-permute-done.27.refs_0_ = bf16[2,128,1024]{2,1,0:T(8,128)(2,1)S(1)} collective-permute-done((bf16[2,128,1024]{2,1,0:T(8,128)(2,1)S(1)}, bf16[2,128,1024]{2,1,0:T(8,128)(2,1)S(1)}, u32[]{:S(2)}, u32[]{:S(2)}) %collective-permute-start.27) | collective-permute-done | bytes 524320 | tf_op jit(solution)/shard_map/ppermute | solution.py:24
  101.3 1.6 shard_map.80
  102.9 2.7 %collective-permute-start.31 = (bf16[1,128,1024]{2,1,0:T(8,128)(2,1)S(1)}, bf16[1,128,1024]{2,1,0:T(8,128)(2,1)S(1)}, u32[]{:S(2)}, u32[]{:S(2)}) collective-permute-start(bf16[1,128,1024]{2,1,0:T(8,128)(2,1)S(1)} %get-tuple-element.114), channel_id=1, source_target_pairs={{0,64},{64,128},{128,192},{192,0},{1,65},{65,129},{129,193},{193,1... | collective-permute-start | bytes 786440 | tf_op jit(solution)/shard_map/ppermute | solution.py:24
  105.5 2.8 %collective-permute-start.30 = (bf16[2,64,1024]{2,1,0:T(8,128)(2,1)S(1)}, bf16[2,64,1024]{2,1,0:T(8,128)(2,1)S(1)}, u32[]{:S(2)}, u32[]{:S(2)}) collective-permute-start(bf16[2,64,1024]{2,1,0:T(8,128)(2,1)S(1)} %get-tuple-element.113.refs_0_), channel_id=1, source_target_pairs={{0,16},{16,0},{32,48},{48,32},{1,17},{17,1},{33,49},{49,33},{2,18}... | collective-permute-start | bytes 786440 | tf_op jit(solution)/shard_map/ppermute | solution.py:28
  109.0 1.8 %collective-permute-done.33.refs_0_ = bf16[2,128,1024]{2,1,0:T(8,128)(2,1)S(1)} collective-permute-done((bf16[2,128,1024]{2,1,0:T(8,128)(2,1)S(1)}, bf16[2,128,1024]{2,1,0:T(8,128)(2,1)S(1)}, u32[]{:S(2)}, u32[]{:S(2)}) %collective-permute-start.33) | collective-permute-done | bytes 524320 | tf_op jit(solution)/shard_map/ppermute | solution.py:24
  110.8 1.1 collective-permute-start.29
  112.1 1.6 shard_map.82
  113.6 2.0 %collective-permute-start.36 = (bf16[1,128,1024]{2,1,0:T(8,128)(2,1)S(1)}, bf16[1,128,1024]{2,1,0:T(8,128)(2,1)S(1)}, u32[]{:S(2)}, u32[]{:S(2)}) collective-permute-start(bf16[1,128,1024]{2,1,0:T(8,128)(2,1)S(1)} %get-tuple-element.120), channel_id=1, source_target_pairs={{0,64},{64,128},{128,192},{192,0},{1,65},{65,129},{129,193},{193,1... | collective-permute-start | bytes 786440 | tf_op jit(solution)/shard_map/ppermute | solution.py:24
  116.3 1.4 shard_map.83.refs_2_
  117.7 1.4 shard_map.84
  120.4 2.0 %collective-permute-start.40 = (bf16[2,128,1024]{2,1,0:T(8,128)(2,1)S(1)}, bf16[2,128,1024]{2,1,0:T(8,128)(2,1)S(1)}, u32[]{:S(2)}, u32[]{:S(2)}) collective-permute-start(bf16[2,128,1024]{2,1,0:T(8,128)(2,1)S(1)} %get-tuple-element.118.refs_2_), channel_id=1, source_target_pairs={{0,64},{64,128},{128,192},{192,0},{1,65},{65,129},{129,193},{193,1... | collective-permute-start | bytes 1572872 | tf_op jit(solution)/shard_map/ppermute | solution.py:24
  122.4 1.0 collective-permute-done.36.refs_0_
  123.4 2.7 %collective-permute-done.37.refs_1_ = bf16[1,128,1024]{2,1,0:T(8,128)(2,1)S(1)} collective-permute-done((bf16[1,128,1024]{2,1,0:T(8,128)(2,1)S(1)}, bf16[1,128,1024]{2,1,0:T(8,128)(2,1)S(1)}, u32[]{:S(2)}, u32[]{:S(2)}) %collective-permute-start.37) | collective-permute-done | bytes 262176 | tf_op jit(solution)/shard_map/ppermute | solution.py:24
  126.1 1.4 shard_map.86.refs_2_
  127.5 1.4 shard_map.87
  128.9 1.3 collective-permute-start.38
  130.1 0.8 collective-permute-start.39
  131.0 4.3 %collective-permute-done.40.refs_0_ = bf16[2,128,1024]{2,1,0:T(8,128)(2,1)S(1)} collective-permute-done((bf16[2,128,1024]{2,1,0:T(8,128)(2,1)S(1)}, bf16[2,128,1024]{2,1,0:T(8,128)(2,1)S(1)}, u32[]{:S(2)}, u32[]{:S(2)}) %collective-permute-start.40) | collective-permute-done | bytes 524320 | tf_op jit(solution)/shard_map/ppermute | solution.py:24
  135.2 3.2 %collective-permute-done.41.refs_1_ = bf16[2,128,1024]{2,1,0:T(8,128)(2,1)S(1)} collective-permute-done((bf16[2,128,1024]{2,1,0:T(8,128)(2,1)S(1)}, bf16[2,128,1024]{2,1,0:T(8,128)(2,1)S(1)}, u32[]{:S(2)}, u32[]{:S(2)}) %collective-permute-start.41) | collective-permute-done | bytes 524320 | tf_op jit(solution)/shard_map/ppermute | solution.py:24
  138.5 1.6 shard_map.88
  140.6 1.6 collective-permute-start.45
  142.2 4.2 %collective-permute-done.38.refs_0_ = bf16[2,128,1024]{2,1,0:T(8,128)(2,1)S(1)} collective-permute-done((bf16[2,128,1024]{2,1,0:T(8,128)(2,1)S(1)}, bf16[2,128,1024]{2,1,0:T(8,128)(2,1)S(1)}, u32[]{:S(2)}, u32[]{:S(2)}) %collective-permute-start.38) | collective-permute-done | bytes 524320 | tf_op jit(solution)/shard_map/ppermute | solution.py:24
  146.3 2.2 %collective-permute-done.39.refs_1_ = bf16[2,128,1024]{2,1,0:T(8,128)(2,1)S(1)} collective-permute-done((bf16[2,128,1024]{2,1,0:T(8,128)(2,1)S(1)}, bf16[2,128,1024]{2,1,0:T(8,128)(2,1)S(1)}, u32[]{:S(2)}, u32[]{:S(2)}) %collective-permute-start.39) | collective-permute-done | bytes 524320 | tf_op jit(solution)/shard_map/ppermute | solution.py:24
  148.5 1.6 shard_map.89
  150.5 1.7 %collective-permute-start.43 = (bf16[1,128,1024]{2,1,0:T(8,128)(2,1)S(1)}, bf16[1,128,1024]{2,1,0:T(8,128)(2,1)S(1)}, u32[]{:S(2)}, u32[]{:S(2)}) collective-permute-start(bf16[1,128,1024]{2,1,0:T(8,128)(2,1)S(1)} %get-tuple-element.128.refs_3_), channel_id=1, source_target_pairs={{0,192},{64,0},{128,64},{192,128},{1,193},{65,1},{129,65},{193,129... | collective-permute-start | bytes 786440 | tf_op jit(solution)/shard_map/ppermute | solution.py:24
  152.2 1.5 pad_maximum_fusion
  153.7 1.4 shard_map.90.refs_2_
  155.1 1.5 collective-permute-done.42.refs_0_
  156.6 1.5 collective-permute-done.43.refs_1_
  158.0 1.4 shard_map.91
  (76 shorter events, 21.2 us)
Async XLA Ops:
  1.7 8.3 %collective-permute-start = (bf16[1,128,1024]{2,1,0:T(8,128)(2,1)S(1)}, bf16[1,128,1024]{2,1,0:T(8,128)(2,1)S(1)}, u32[]{:S(2)}, u32[]{:S(2)}) collective-permute-start(bf16[1,128,1024]{2,1,0:T(8,128)(2,1)S(1)} %get-tuple-element.140.refs_1_), channel_id=1, source_target_pairs={{0,64},{64,128},{128,192},{192,0},{1,65},{65,129},{129,193},{193,1... | collective-permute-start | bytes 786440 | tf_op jit(solution)/shard_map/ppermute | solution.py:24
  2.0 9.1 %collective-permute-start.1 = (bf16[1,128,1024]{2,1,0:T(8,128)(2,1)S(1)}, bf16[1,128,1024]{2,1,0:T(8,128)(2,1)S(1)}, u32[]{:S(2)}, u32[]{:S(2)}) collective-permute-start(bf16[1,128,1024]{2,1,0:T(8,128)(2,1)S(1)} %get-tuple-element.139), channel_id=1, source_target_pairs={{0,192},{64,0},{128,64},{192,128},{1,193},{65,1},{129,65},{193,129... | collective-permute-start | bytes 786440 | tf_op jit(solution)/shard_map/ppermute | solution.py:24
  3.9 3.4 %copy-start = (bf16[1,8,512,1024]{3,2,1,0:T(8,128)(2,1)S(1)}, bf16[1,8,512,1024]{3,2,1,0:T(8,128)(2,1)}, u32[]{:S(2)}) copy-start(bf16[1,8,512,1024]{3,2,1,0:T(8,128)(2,1)} %refs_0_.19) | copy-start | bytes 25165828
  8.0 14.9 %collective-permute-start.4 = (bf16[2,128,1024]{2,1,0:T(8,128)(2,1)S(1)}, bf16[2,128,1024]{2,1,0:T(8,128)(2,1)S(1)}, u32[]{:S(2)}, u32[]{:S(2)}) collective-permute-start(bf16[2,128,1024]{2,1,0:T(8,128)(2,1)S(1)} %get-tuple-element.74), channel_id=1, source_target_pairs={{0,64},{64,128},{128,192},{192,0},{1,65},{65,129},{129,193},{193,1... | collective-permute-start | bytes 1572872 | tf_op jit(solution)/shard_map/ppermute | solution.py:24
  9.5 16.1 %collective-permute-start.5 = (bf16[2,128,1024]{2,1,0:T(8,128)(2,1)S(1)}, bf16[2,128,1024]{2,1,0:T(8,128)(2,1)S(1)}, u32[]{:S(2)}, u32[]{:S(2)}) collective-permute-start(bf16[2,128,1024]{2,1,0:T(8,128)(2,1)S(1)} %get-tuple-element.71.refs_3_), channel_id=1, source_target_pairs={{0,192},{64,0},{128,64},{192,128},{1,193},{65,1},{129,65},{193,129... | collective-permute-start | bytes 1572872 | tf_op jit(solution)/shard_map/ppermute | solution.py:24
  11.9 22.2 %collective-permute-start.2 = (bf16[2,128,1024]{2,1,0:T(8,128)(2,1)S(1)}, bf16[2,128,1024]{2,1,0:T(8,128)(2,1)S(1)}, u32[]{:S(2)}, u32[]{:S(2)}) collective-permute-start(bf16[2,128,1024]{2,1,0:T(8,128)(2,1)S(1)} %get-tuple-element.72), channel_id=1, source_target_pairs={{0,64},{64,128},{128,192},{192,0},{1,65},{65,129},{129,193},{193,1... | collective-permute-start | bytes 1572872 | tf_op jit(solution)/shard_map/ppermute | solution.py:24
  13.6 23.2 %collective-permute-start.3 = (bf16[2,128,1024]{2,1,0:T(8,128)(2,1)S(1)}, bf16[2,128,1024]{2,1,0:T(8,128)(2,1)S(1)}, u32[]{:S(2)}, u32[]{:S(2)}) collective-permute-start(bf16[2,128,1024]{2,1,0:T(8,128)(2,1)S(1)} %get-tuple-element.73.refs_3_), channel_id=1, source_target_pairs={{0,192},{64,0},{128,64},{192,128},{1,193},{65,1},{129,65},{193,129... | collective-permute-start | bytes 1572872 | tf_op jit(solution)/shard_map/ppermute | solution.py:24
  26.3 21.3 %collective-permute-start.8 = (bf16[2,128,1024]{2,1,0:T(8,128)(2,1)S(1)}, bf16[2,128,1024]{2,1,0:T(8,128)(2,1)S(1)}, u32[]{:S(2)}, u32[]{:S(2)}) collective-permute-start(bf16[2,128,1024]{2,1,0:T(8,128)(2,1)S(1)} %get-tuple-element.81), channel_id=1, source_target_pairs={{0,64},{64,128},{128,192},{192,0},{1,65},{65,129},{129,193},{193,1... | collective-permute-start | bytes 1572872 | tf_op jit(solution)/shard_map/ppermute | solution.py:24
  26.4 21.6 %slice-start = ((s8[8388608]{0:T(1024)(128)(4,1)}), s8[4194304]{0:T(1024)(128)(4,1)S(1)}, s32[]{:S(2)}) async-start(s8[8388608]{0:T(1024)(128)(4,1)} %bitcast.6), calls=%async_computation | async-start | bytes 8388608
  26.4 21.6 %collective-permute-start.9 = (bf16[2,128,1024]{2,1,0:T(8,128)(2,1)S(1)}, bf16[2,128,1024]{2,1,0:T(8,128)(2,1)S(1)}, u32[]{:S(2)}, u32[]{:S(2)}) collective-permute-start(bf16[2,128,1024]{2,1,0:T(8,128)(2,1)S(1)} %get-tuple-element.75.refs_3_), channel_id=1, source_target_pairs={{0,192},{64,0},{128,64},{192,128},{1,193},{65,1},{129,65},{193,129... | collective-permute-start | bytes 1572872 | tf_op jit(solution)/shard_map/ppermute | solution.py:24
  36.8 11.2 %slice-start.1 = ((s8[8388608]{0:T(1024)(128)(4,1)}), s8[4194304]{0:T(1024)(128)(4,1)S(1)}, s32[]{:S(2)}) async-start(s8[8388608]{0:T(1024)(128)(4,1)} %bitcast.6), calls=%async_computation.1 | async-start | bytes 8388608
  36.8 14.0 %copy-start.1 = (f32[8,32,1024]{2,1,0:T(8,128)S(1)}, f32[8,32,1024]{2,1,0:T(8,128)}, u32[]{:S(2)}) copy-start(f32[8,32,1024]{2,1,0:T(8,128)} %refs_2_.7) | copy-start | bytes 3145732
  36.8 14.0 %copy-start.2 = (f32[8,32,1024]{2,1,0:T(8,128)S(1)}, f32[8,32,1024]{2,1,0:T(8,128)}, u32[]{:S(2)}) copy-start(f32[8,32,1024]{2,1,0:T(8,128)} %refs_3_.7) | copy-start | bytes 3145732
  37.6 6.5 %collective-permute-start.6 = (bf16[2,64,1024]{2,1,0:T(8,128)(2,1)S(1)}, bf16[2,64,1024]{2,1,0:T(8,128)(2,1)S(1)}, u32[]{:S(2)}, u32[]{:S(2)}) collective-permute-start(bf16[2,64,1024]{2,1,0:T(8,128)(2,1)S(1)} %get-tuple-element.78.refs_2_), channel_id=1, source_target_pairs={{0,16},{16,0},{32,48},{48,32},{1,17},{17,1},{33,49},{49,33},{2,18}... | collective-permute-start | bytes 786440 | tf_op jit(solution)/shard_map/ppermute | solution.py:28
  39.5 18.6 %collective-permute-start.13 = (bf16[2,128,1024]{2,1,0:T(8,128)(2,1)S(1)}, bf16[2,128,1024]{2,1,0:T(8,128)(2,1)S(1)}, u32[]{:S(2)}, u32[]{:S(2)}) collective-permute-start(bf16[2,128,1024]{2,1,0:T(8,128)(2,1)S(1)} %get-tuple-element.86), channel_id=1, source_target_pairs={{0,64},{64,128},{128,192},{192,0},{1,65},{65,129},{129,193},{193,1... | collective-permute-start | bytes 1572872 | tf_op jit(solution)/shard_map/ppermute | solution.py:24
  39.5 19.7 %collective-permute-start.14 = (bf16[2,128,1024]{2,1,0:T(8,128)(2,1)S(1)}, bf16[2,128,1024]{2,1,0:T(8,128)(2,1)S(1)}, u32[]{:S(2)}, u32[]{:S(2)}) collective-permute-start(bf16[2,128,1024]{2,1,0:T(8,128)(2,1)S(1)} %get-tuple-element.76.refs_3_), channel_id=1, source_target_pairs={{0,192},{64,0},{128,64},{192,128},{1,193},{65,1},{129,65},{193,129... | collective-permute-start | bytes 1572872 | tf_op jit(solution)/shard_map/ppermute | solution.py:24
  44.6 6.1 %collective-permute-start.7 = (bf16[2,32,1024]{2,1,0:T(8,128)(2,1)S(1)}, bf16[2,32,1024]{2,1,0:T(8,128)(2,1)S(1)}, u32[]{:S(2)}, u32[]{:S(2)}) collective-permute-start(bf16[2,32,1024]{2,1,0:T(8,128)(2,1)S(1)} %get-tuple-element.80.refs_3_), channel_id=1, source_target_pairs={{0,48},{16,32},{32,16},{48,0},{1,49},{17,33},{33,17},{49,1},{2,50}... | collective-permute-start | bytes 393224 | tf_op jit(solution)/shard_map/ppermute | solution.py:28
  48.8 6.5 %collective-permute-start.15 = (bf16[2,64,1024]{2,1,0:T(8,128)(2,1)S(1)}, bf16[2,64,1024]{2,1,0:T(8,128)(2,1)S(1)}, u32[]{:S(2)}, u32[]{:S(2)}) collective-permute-start(bf16[2,64,1024]{2,1,0:T(8,128)(2,1)S(1)} %get-tuple-element.82.refs_4_), channel_id=1, source_target_pairs={{0,16},{16,0},{32,48},{48,32},{1,17},{17,1},{33,49},{49,33},{2,18}... | collective-permute-start | bytes 786440 | tf_op jit(solution)/shard_map/ppermute | solution.py:28
  52.0 10.0 %collective-permute-start.10 = (bf16[1,128,1024]{2,1,0:T(8,128)(2,1)S(1)}, bf16[1,128,1024]{2,1,0:T(8,128)(2,1)S(1)}, u32[]{:S(2)}, u32[]{:S(2)}) collective-permute-start(bf16[1,128,1024]{2,1,0:T(8,128)(2,1)S(1)} %get-tuple-element.84), channel_id=1, source_target_pairs={{0,64},{64,128},{128,192},{192,0},{1,65},{65,129},{129,193},{193,1... | collective-permute-start | bytes 786440 | tf_op jit(solution)/shard_map/ppermute | solution.py:24
  52.1 10.9 %collective-permute-start.11 = (bf16[1,128,1024]{2,1,0:T(8,128)(2,1)S(1)}, bf16[1,128,1024]{2,1,0:T(8,128)(2,1)S(1)}, u32[]{:S(2)}, u32[]{:S(2)}) collective-permute-start(bf16[1,128,1024]{2,1,0:T(8,128)(2,1)S(1)} %get-tuple-element.85.refs_2_), channel_id=1, source_target_pairs={{0,192},{64,0},{128,64},{192,128},{1,193},{65,1},{129,65},{193,129... | collective-permute-start | bytes 786440 | tf_op jit(solution)/shard_map/ppermute | solution.py:24
  55.3 6.2 %collective-permute-start.12 = (bf16[2,32,1024]{2,1,0:T(8,128)(2,1)S(1)}, bf16[2,32,1024]{2,1,0:T(8,128)(2,1)S(1)}, u32[]{:S(2)}, u32[]{:S(2)}) collective-permute-start(bf16[2,32,1024]{2,1,0:T(8,128)(2,1)S(1)} %get-tuple-element.83.refs_1_.refs_0_), channel_id=1, source_target_pairs={{0,48},{16,32},{32,16},{48,0},{1,49},{17,33},{33,17},{49,1},{2,50}... | collective-permute-start | bytes 393224 | tf_op jit(solution)/shard_map/ppermute | solution.py:28
  60.0 13.5 %collective-permute-start.18 = (bf16[2,64,1024]{2,1,0:T(8,128)(2,1)S(1)}, bf16[2,64,1024]{2,1,0:T(8,128)(2,1)S(1)}, u32[]{:S(2)}, u32[]{:S(2)}) collective-permute-start(bf16[2,64,1024]{2,1,0:T(8,128)(2,1)S(1)} %get-tuple-element.89.refs_2_), channel_id=1, source_target_pairs={{0,16},{16,0},{32,48},{48,32},{1,17},{17,1},{33,49},{49,33},{2,18}... | collective-permute-start | bytes 786440 | tf_op jit(solution)/shard_map/ppermute | solution.py:28
  63.8 25.5 %collective-permute-start.16 = (bf16[2,128,1024]{2,1,0:T(8,128)(2,1)S(1)}, bf16[2,128,1024]{2,1,0:T(8,128)(2,1)S(1)}, u32[]{:S(2)}, u32[]{:S(2)}) collective-permute-start(bf16[2,128,1024]{2,1,0:T(8,128)(2,1)S(1)} %get-tuple-element.91), channel_id=1, source_target_pairs={{0,64},{64,128},{128,192},{192,0},{1,65},{65,129},{129,193},{193,1... | collective-permute-start | bytes 1572872 | tf_op jit(solution)/shard_map/ppermute | solution.py:24
  64.1 6.5 %collective-permute-start.19 = (bf16[2,32,1024]{2,1,0:T(8,128)(2,1)S(1)}, bf16[2,32,1024]{2,1,0:T(8,128)(2,1)S(1)}, u32[]{:S(2)}, u32[]{:S(2)}) collective-permute-start(bf16[2,32,1024]{2,1,0:T(8,128)(2,1)S(1)} %get-tuple-element.88.refs_3_), channel_id=1, source_target_pairs={{0,48},{16,32},{32,16},{48,0},{1,49},{17,33},{33,17},{49,1},{2,50}... | collective-permute-start | bytes 393224 | tf_op jit(solution)/shard_map/ppermute | solution.py:28
  66.0 23.7 %collective-permute-start.17 = (bf16[2,128,1024]{2,1,0:T(8,128)(2,1)S(1)}, bf16[2,128,1024]{2,1,0:T(8,128)(2,1)S(1)}, u32[]{:S(2)}, u32[]{:S(2)}) collective-permute-start(bf16[2,128,1024]{2,1,0:T(8,128)(2,1)S(1)} %get-tuple-element.92.refs_4_), channel_id=1, source_target_pairs={{0,192},{64,0},{128,64},{192,128},{1,193},{65,1},{129,65},{193,129... | collective-permute-start | bytes 1572872 | tf_op jit(solution)/shard_map/ppermute | solution.py:24
  67.8 16.4 %collective-permute-start.21 = (bf16[2,64,1024]{2,1,0:T(8,128)(2,1)S(1)}, bf16[2,64,1024]{2,1,0:T(8,128)(2,1)S(1)}, u32[]{:S(2)}, u32[]{:S(2)}) collective-permute-start(bf16[2,64,1024]{2,1,0:T(8,128)(2,1)S(1)} %get-tuple-element.98.refs_0_), channel_id=1, source_target_pairs={{0,16},{16,0},{32,48},{48,32},{1,17},{17,1},{33,49},{49,33},{2,18}... | collective-permute-start | bytes 786440 | tf_op jit(solution)/shard_map/ppermute | solution.py:28
  71.3 8.1 %collective-permute-start.22 = (bf16[2,32,1024]{2,1,0:T(8,128)(2,1)S(1)}, bf16[2,32,1024]{2,1,0:T(8,128)(2,1)S(1)}, u32[]{:S(2)}, u32[]{:S(2)}) collective-permute-start(bf16[2,32,1024]{2,1,0:T(8,128)(2,1)S(1)} %get-tuple-element.95.refs_2_.refs_0_), channel_id=1, source_target_pairs={{0,48},{16,32},{32,16},{48,0},{1,49},{17,33},{33,17},{49,1},{2,50}... | collective-permute-start | bytes 393224 | tf_op jit(solution)/shard_map/ppermute | solution.py:28
  74.1 11.5 %collective-permute-start.20 = (bf16[2,32,1024]{2,1,0:T(8,128)(2,1)S(1)}, bf16[2,32,1024]{2,1,0:T(8,128)(2,1)S(1)}, u32[]{:S(2)}, u32[]{:S(2)}) collective-permute-start(bf16[2,32,1024]{2,1,0:T(8,128)(2,1)S(1)} %get-tuple-element.97.refs_2_), channel_id=1, source_target_pairs={{0,48},{16,32},{32,16},{48,0},{1,49},{17,33},{33,17},{49,1},{2,50}... | collective-permute-start | bytes 393224 | tf_op jit(solution)/shard_map/ppermute | solution.py:28
  80.0 11.7 %collective-permute-start.25 = (bf16[2,64,1024]{2,1,0:T(8,128)(2,1)S(1)}, bf16[2,64,1024]{2,1,0:T(8,128)(2,1)S(1)}, u32[]{:S(2)}, u32[]{:S(2)}) collective-permute-start(bf16[2,64,1024]{2,1,0:T(8,128)(2,1)S(1)} %get-tuple-element.104.refs_0_), channel_id=1, source_target_pairs={{0,16},{16,0},{32,48},{48,32},{1,17},{17,1},{33,49},{49,33},{2,18}... | collective-permute-start | bytes 786440 | tf_op jit(solution)/shard_map/ppermute | solution.py:28
  85.5 15.7 %collective-permute-start.27 = (bf16[2,128,1024]{2,1,0:T(8,128)(2,1)S(1)}, bf16[2,128,1024]{2,1,0:T(8,128)(2,1)S(1)}, u32[]{:S(2)}, u32[]{:S(2)}) collective-permute-start(bf16[2,128,1024]{2,1,0:T(8,128)(2,1)S(1)} %get-tuple-element.100.refs_4_), channel_id=1, source_target_pairs={{0,64},{64,128},{128,192},{192,0},{1,65},{65,129},{129,193},{193,1... | collective-permute-start | bytes 1572872 | tf_op jit(solution)/shard_map/ppermute | solution.py:24
  85.6 15.6 %collective-permute-start.28 = (bf16[2,128,1024]{2,1,0:T(8,128)(2,1)S(1)}, bf16[2,128,1024]{2,1,0:T(8,128)(2,1)S(1)}, u32[]{:S(2)}, u32[]{:S(2)}) collective-permute-start(bf16[2,128,1024]{2,1,0:T(8,128)(2,1)S(1)} %get-tuple-element.100.refs_4_), channel_id=1, source_target_pairs={{0,192},{64,0},{128,64},{192,128},{1,193},{65,1},{129,65},{193,129... | collective-permute-start | bytes 1572872 | tf_op jit(solution)/shard_map/ppermute | solution.py:24
  89.3 6.5 %collective-permute-start.24 = (bf16[2,32,1024]{2,1,0:T(8,128)(2,1)S(1)}, bf16[2,32,1024]{2,1,0:T(8,128)(2,1)S(1)}, u32[]{:S(2)}, u32[]{:S(2)}) collective-permute-start(bf16[2,32,1024]{2,1,0:T(8,128)(2,1)S(1)} %get-tuple-element.101.refs_3_.refs_0_), channel_id=1, source_target_pairs={{0,48},{16,32},{32,16},{48,0},{1,49},{17,33},{33,17},{49,1},{2,50}... | collective-permute-start | bytes 393224 | tf_op jit(solution)/shard_map/ppermute | solution.py:28
  90.6 8.0 %collective-permute-start.23 = (bf16[2,64,1024]{2,1,0:T(8,128)(2,1)S(1)}, bf16[2,64,1024]{2,1,0:T(8,128)(2,1)S(1)}, u32[]{:S(2)}, u32[]{:S(2)}) collective-permute-start(bf16[2,64,1024]{2,1,0:T(8,128)(2,1)S(1)} %get-tuple-element.103.refs_3_), channel_id=1, source_target_pairs={{0,16},{16,0},{32,48},{48,32},{1,17},{17,1},{33,49},{49,33},{2,18}... | collective-permute-start | bytes 786440 | tf_op jit(solution)/shard_map/ppermute | solution.py:28
  93.1 17.8 %collective-permute-start.33 = (bf16[2,128,1024]{2,1,0:T(8,128)(2,1)S(1)}, bf16[2,128,1024]{2,1,0:T(8,128)(2,1)S(1)}, u32[]{:S(2)}, u32[]{:S(2)}) collective-permute-start(bf16[2,128,1024]{2,1,0:T(8,128)(2,1)S(1)} %get-tuple-element.106.refs_2_), channel_id=1, source_target_pairs={{0,64},{64,128},{128,192},{192,0},{1,65},{65,129},{129,193},{193,1... | collective-permute-start | bytes 1572872 | tf_op jit(solution)/shard_map/ppermute | solution.py:24
  95.7 16.3 %collective-permute-start.34 = (bf16[2,128,1024]{2,1,0:T(8,128)(2,1)S(1)}, bf16[2,128,1024]{2,1,0:T(8,128)(2,1)S(1)}, u32[]{:S(2)}, u32[]{:S(2)}) collective-permute-start(bf16[2,128,1024]{2,1,0:T(8,128)(2,1)S(1)} %get-tuple-element.106.refs_2_), channel_id=1, source_target_pairs={{0,192},{64,0},{128,64},{192,128},{1,193},{65,1},{129,65},{193,129... | collective-permute-start | bytes 1572872 | tf_op jit(solution)/shard_map/ppermute | solution.py:24
  99.1 6.4 %collective-permute-start.26 = (bf16[2,32,1024]{2,1,0:T(8,128)(2,1)S(1)}, bf16[2,32,1024]{2,1,0:T(8,128)(2,1)S(1)}, u32[]{:S(2)}, u32[]{:S(2)}) collective-permute-start(bf16[2,32,1024]{2,1,0:T(8,128)(2,1)S(1)} %get-tuple-element.109.refs_3_), channel_id=1, source_target_pairs={{0,48},{16,32},{32,16},{48,0},{1,49},{17,33},{33,17},{49,1},{2,50}... | collective-permute-start | bytes 393224 | tf_op jit(solution)/shard_map/ppermute | solution.py:28
  102.9 12.8 %collective-permute-start.31 = (bf16[1,128,1024]{2,1,0:T(8,128)(2,1)S(1)}, bf16[1,128,1024]{2,1,0:T(8,128)(2,1)S(1)}, u32[]{:S(2)}, u32[]{:S(2)}) collective-permute-start(bf16[1,128,1024]{2,1,0:T(8,128)(2,1)S(1)} %get-tuple-element.114), channel_id=1, source_target_pairs={{0,64},{64,128},{128,192},{192,0},{1,65},{65,129},{129,193},{193,1... | collective-permute-start | bytes 786440 | tf_op jit(solution)/shard_map/ppermute | solution.py:24
  105.5 10.8 %collective-permute-start.32 = (bf16[1,128,1024]{2,1,0:T(8,128)(2,1)S(1)}, bf16[1,128,1024]{2,1,0:T(8,128)(2,1)S(1)}, u32[]{:S(2)}, u32[]{:S(2)}) collective-permute-start(bf16[1,128,1024]{2,1,0:T(8,128)(2,1)S(1)} %get-tuple-element.111.refs_4_), channel_id=1, source_target_pairs={{0,192},{64,0},{128,64},{192,128},{1,193},{65,1},{129,65},{193,129... | collective-permute-start | bytes 786440 | tf_op jit(solution)/shard_map/ppermute | solution.py:24
  105.5 12.1 %collective-permute-start.30 = (bf16[2,64,1024]{2,1,0:T(8,128)(2,1)S(1)}, bf16[2,64,1024]{2,1,0:T(8,128)(2,1)S(1)}, u32[]{:S(2)}, u32[]{:S(2)}) collective-permute-start(bf16[2,64,1024]{2,1,0:T(8,128)(2,1)S(1)} %get-tuple-element.113.refs_0_), channel_id=1, source_target_pairs={{0,16},{16,0},{32,48},{48,32},{1,17},{17,1},{33,49},{49,33},{2,18}... | collective-permute-start | bytes 786440 | tf_op jit(solution)/shard_map/ppermute | solution.py:28
  110.8 8.2 %collective-permute-start.29 = (bf16[2,32,1024]{2,1,0:T(8,128)(2,1)S(1)}, bf16[2,32,1024]{2,1,0:T(8,128)(2,1)S(1)}, u32[]{:S(2)}, u32[]{:S(2)}) collective-permute-start(bf16[2,32,1024]{2,1,0:T(8,128)(2,1)S(1)} %get-tuple-element.112.refs_3_.refs_0_), channel_id=1, source_target_pairs={{0,48},{16,32},{32,16},{48,0},{1,49},{17,33},{33,17},{49,1},{2,50}... | collective-permute-start | bytes 393224 | tf_op jit(solution)/shard_map/ppermute | solution.py:28
  113.6 9.8 %collective-permute-start.36 = (bf16[1,128,1024]{2,1,0:T(8,128)(2,1)S(1)}, bf16[1,128,1024]{2,1,0:T(8,128)(2,1)S(1)}, u32[]{:S(2)}, u32[]{:S(2)}) collective-permute-start(bf16[1,128,1024]{2,1,0:T(8,128)(2,1)S(1)} %get-tuple-element.120), channel_id=1, source_target_pairs={{0,64},{64,128},{128,192},{192,0},{1,65},{65,129},{129,193},{193,1... | collective-permute-start | bytes 786440 | tf_op jit(solution)/shard_map/ppermute | solution.py:24
  115.6 10.5 %collective-permute-start.37 = (bf16[1,128,1024]{2,1,0:T(8,128)(2,1)S(1)}, bf16[1,128,1024]{2,1,0:T(8,128)(2,1)S(1)}, u32[]{:S(2)}, u32[]{:S(2)}) collective-permute-start(bf16[1,128,1024]{2,1,0:T(8,128)(2,1)S(1)} %get-tuple-element.117.refs_3_), channel_id=1, source_target_pairs={{0,192},{64,0},{128,64},{192,128},{1,193},{65,1},{129,65},{193,129... | collective-permute-start | bytes 786440 | tf_op jit(solution)/shard_map/ppermute | solution.py:24
  119.7 7.8 %collective-permute-start.35 = (bf16[2,64,1024]{2,1,0:T(8,128)(2,1)S(1)}, bf16[2,64,1024]{2,1,0:T(8,128)(2,1)S(1)}, u32[]{:S(2)}, u32[]{:S(2)}) collective-permute-start(bf16[2,64,1024]{2,1,0:T(8,128)(2,1)S(1)} %get-tuple-element.119.refs_0_), channel_id=1, source_target_pairs={{0,16},{16,0},{32,48},{48,32},{1,17},{17,1},{33,49},{49,33},{2,18}... | collective-permute-start | bytes 786440 | tf_op jit(solution)/shard_map/ppermute | solution.py:28
  120.4 14.9 %collective-permute-start.40 = (bf16[2,128,1024]{2,1,0:T(8,128)(2,1)S(1)}, bf16[2,128,1024]{2,1,0:T(8,128)(2,1)S(1)}, u32[]{:S(2)}, u32[]{:S(2)}) collective-permute-start(bf16[2,128,1024]{2,1,0:T(8,128)(2,1)S(1)} %get-tuple-element.118.refs_2_), channel_id=1, source_target_pairs={{0,64},{64,128},{128,192},{192,0},{1,65},{65,129},{129,193},{193,1... | collective-permute-start | bytes 1572872 | tf_op jit(solution)/shard_map/ppermute | solution.py:24
  122.4 16.1 %collective-permute-start.41 = (bf16[2,128,1024]{2,1,0:T(8,128)(2,1)S(1)}, bf16[2,128,1024]{2,1,0:T(8,128)(2,1)S(1)}, u32[]{:S(2)}, u32[]{:S(2)}) collective-permute-start(bf16[2,128,1024]{2,1,0:T(8,128)(2,1)S(1)} %get-tuple-element.118.refs_2_), channel_id=1, source_target_pairs={{0,192},{64,0},{128,64},{192,128},{1,193},{65,1},{129,65},{193,129... | collective-permute-start | bytes 1572872 | tf_op jit(solution)/shard_map/ppermute | solution.py:24
  128.9 17.5 %collective-permute-start.38 = (bf16[2,128,1024]{2,1,0:T(8,128)(2,1)S(1)}, bf16[2,128,1024]{2,1,0:T(8,128)(2,1)S(1)}, u32[]{:S(2)}, u32[]{:S(2)}) collective-permute-start(bf16[2,128,1024]{2,1,0:T(8,128)(2,1)S(1)} %get-tuple-element.123.refs_3_), channel_id=1, source_target_pairs={{0,64},{64,128},{128,192},{192,0},{1,65},{65,129},{129,193},{193,1... | collective-permute-start | bytes 1572872 | tf_op jit(solution)/shard_map/ppermute | solution.py:24
  130.1 18.4 %collective-permute-start.39 = (bf16[2,128,1024]{2,1,0:T(8,128)(2,1)S(1)}, bf16[2,128,1024]{2,1,0:T(8,128)(2,1)S(1)}, u32[]{:S(2)}, u32[]{:S(2)}) collective-permute-start(bf16[2,128,1024]{2,1,0:T(8,128)(2,1)S(1)} %get-tuple-element.123.refs_3_), channel_id=1, source_target_pairs={{0,192},{64,0},{128,64},{192,128},{1,193},{65,1},{129,65},{193,129... | collective-permute-start | bytes 1572872 | tf_op jit(solution)/shard_map/ppermute | solution.py:24
  140.1 13.6 %collective-permute-start.44 = (bf16[1,128,1024]{2,1,0:T(8,128)(2,1)S(1)}, bf16[1,128,1024]{2,1,0:T(8,128)(2,1)S(1)}, u32[]{:S(2)}, u32[]{:S(2)}) collective-permute-start(bf16[1,128,1024]{2,1,0:T(8,128)(2,1)S(1)} %get-tuple-element.129), channel_id=1, source_target_pairs={{0,64},{64,128},{128,192},{192,0},{1,65},{65,129},{129,193},{193,1... | collective-permute-start | bytes 786440 | tf_op jit(solution)/shard_map/ppermute | solution.py:24
  140.6 13.1 %collective-permute-start.45 = (bf16[1,128,1024]{2,1,0:T(8,128)(2,1)S(1)}, bf16[1,128,1024]{2,1,0:T(8,128)(2,1)S(1)}, u32[]{:S(2)}, u32[]{:S(2)}) collective-permute-start(bf16[1,128,1024]{2,1,0:T(8,128)(2,1)S(1)} %get-tuple-element.126.refs_3_), channel_id=1, source_target_pairs={{0,192},{64,0},{128,64},{192,128},{1,193},{65,1},{129,65},{193,129... | collective-permute-start | bytes 786440 | tf_op jit(solution)/shard_map/ppermute | solution.py:24
  150.1 6.4 %collective-permute-start.42 = (bf16[1,128,1024]{2,1,0:T(8,128)(2,1)S(1)}, bf16[1,128,1024]{2,1,0:T(8,128)(2,1)S(1)}, u32[]{:S(2)}, u32[]{:S(2)}) collective-permute-start(bf16[1,128,1024]{2,1,0:T(8,128)(2,1)S(1)} %get-tuple-element.127), channel_id=1, source_target_pairs={{0,64},{64,128},{128,192},{192,0},{1,65},{65,129},{129,193},{193,1... | collective-permute-start | bytes 786440 | tf_op jit(solution)/shard_map/ppermute | solution.py:24
  150.5 7.6 %collective-permute-start.43 = (bf16[1,128,1024]{2,1,0:T(8,128)(2,1)S(1)}, bf16[1,128,1024]{2,1,0:T(8,128)(2,1)S(1)}, u32[]{:S(2)}, u32[]{:S(2)}) collective-permute-start(bf16[1,128,1024]{2,1,0:T(8,128)(2,1)S(1)} %get-tuple-element.128.refs_3_), channel_id=1, source_target_pairs={{0,192},{64,0},{128,64},{192,128},{1,193},{65,1},{129,65},{193,129... | collective-permute-start | bytes 786440 | tf_op jit(solution)/shard_map/ppermute | solution.py:24

commit v3 on v2

--- a/solution.py
+++ b/solution.py
@@ -292,7 +292,7 @@
 
 PLAN = (
     "a0", "a12", "m0", "m1", "m2", "s0", "h0", "s1", "u0", "a3",
-    "h1", "s2", "p0", "m3", "u1", "h2", "p1", "g0", "u2", "s3",
+    "h1", "s2", "m3", "p0", "u1", "h2", "g0", "p1", "u2", "s3",
     "g1", "p2", "h3", "o0", "u3", "o1", "f0", "g2", "p3", "f1",
     "g3", "o2", "o3", "f2", "f3",
 )

time: 161 us -> 161 us (level)
    ppermute x16, starting transfers between devices: 28.3 us -> 31.1 us  [swap(): return lax.ppermute(a, 'z', [(i, i ^ k) for i in range(NZ)])]
    ppermute x30, starting transfers between devices: 35.7 us -> 33.2 us  [shift(): return lax.ppermute(a, 'y', [(i, (i + s) % NY) for i in range(NY)])]
  transfers between devices with their start and end apart: 46 -> 46, of which waited for: 24 -> 23; matrix products, arithmetic and copies ran while one was open for 1% -> 1% of each run, Pallas kernels for 19% -> 19%
where the time goes in v3:
time: 161 us; the launch traced here: 160 us
  starting transfers between devices  64.3 us (40%)
  waiting for transfers between devices  56 us (35%)
  Pallas kernels  32 us (20%)
  local copies, waits for them, and re-layouts  4.47 us (3%)
    ppermute x30, waiting for transfers between devices, shift(): return lax.ppermute(a, 'y', [(i, (i + s) % NY) for i in range(NY)])  46.4 us
    ppermute x30, starting transfers between devices, shift(): return lax.ppermute(a, 'y', [(i, (i + s) % NY) for i in range(NY)])  33.2 us
    pallas_call x34, Pallas kernels, call(): pl.pallas_call(kernel, out_shape=[jax.ShapeDtypeStruct(s, t) for s, t, _...  32 us
    ppermute x16, starting transfers between devices, swap(): return lax.ppermute(a, 'z', [(i, i ^ k) for i in range(NZ)])  31.1 us
    ppermute x16, waiting for transfers between devices, swap(): return lax.ppermute(a, 'z', [(i, i ^ k) for i in range(NZ)])  9.65 us
    unnamed x10, local copies, waits for them, and re-layouts  3.4 us
  transfers between devices with their start and end apart: 46, of which 23 were waited for; matrix products, arithmetic and copies ran while one was open for 1% of the time, Pallas kernels for 19%

profile of v3, /device:TPU:56, one launch (start us, length us, event | category | flops | bytes accessed | tf_op | source)
XLA Modules:
  0.0 159.6 jit_solution(6134860964826670733)
XLA Ops:
  0.6 1.1 dynamic-slice_bitcast_fusion
  2.0 1.8 %collective-permute-start.1 = (bf16[1,128,1024]{2,1,0:T(8,128)(2,1)S(1)}, bf16[1,128,1024]{2,1,0:T(8,128)(2,1)S(1)}, u32[]{:S(2)}, u32[]{:S(2)}) collective-permute-start(bf16[1,128,1024]{2,1,0:T(8,128)(2,1)S(1)} %get-tuple-element.139), channel_id=1, source_target_pairs={{0,192},{64,0},{128,64},{192,128},{1,193},{65,1},{129,65},{193,129... | collective-permute-start | bytes 786440 | tf_op jit(solution)/shard_map/ppermute | solution.py:24
  3.9 3.4 %copy-done = bf16[1,8,512,1024]{3,2,1,0:T(8,128)(2,1)S(1)} copy-done((bf16[1,8,512,1024]{3,2,1,0:T(8,128)(2,1)S(1)}, bf16[1,8,512,1024]{3,2,1,0:T(8,128)(2,1)}, u32[]{:S(2)}) %copy-start) | copy-done | bytes 8388632
  8.0 1.5 collective-permute-start.4
  10.1 1.1 collective-permute-done.1.refs_2_
  11.1 0.8 shard_map.59
  11.9 1.6 %collective-permute-start.2 = (bf16[2,128,1024]{2,1,0:T(8,128)(2,1)S(1)}, bf16[2,128,1024]{2,1,0:T(8,128)(2,1)S(1)}, u32[]{:S(2)}, u32[]{:S(2)}) collective-permute-start(bf16[2,128,1024]{2,1,0:T(8,128)(2,1)S(1)} %get-tuple-element.72), channel_id=1, source_target_pairs={{0,64},{64,128},{128,192},{192,0},{1,65},{65,129},{129,193},{193,1... | collective-permute-start | bytes 1572872 | tf_op jit(solution)/shard_map/ppermute | solution.py:24
  14.0 8.9 %collective-permute-done.4.refs_1_ = bf16[2,128,1024]{2,1,0:T(8,128)(2,1)S(1)} collective-permute-done((bf16[2,128,1024]{2,1,0:T(8,128)(2,1)S(1)}, bf16[2,128,1024]{2,1,0:T(8,128)(2,1)S(1)}, u32[]{:S(2)}, u32[]{:S(2)}) %collective-permute-start.4) | collective-permute-done | bytes 524320 | tf_op jit(solution)/shard_map/ppermute | solution.py:24
  22.9 2.6 %collective-permute-done.5.refs_2_ = bf16[2,128,1024]{2,1,0:T(8,128)(2,1)S(1)} collective-permute-done((bf16[2,128,1024]{2,1,0:T(8,128)(2,1)S(1)}, bf16[2,128,1024]{2,1,0:T(8,128)(2,1)S(1)}, u32[]{:S(2)}, u32[]{:S(2)}) %collective-permute-start.5) | collective-permute-done | bytes 524320 | tf_op jit(solution)/shard_map/ppermute | solution.py:24
  25.5 0.8 shard_map.60
  26.4 2.0 %collective-permute-start.9 = (bf16[2,128,1024]{2,1,0:T(8,128)(2,1)S(1)}, bf16[2,128,1024]{2,1,0:T(8,128)(2,1)S(1)}, u32[]{:S(2)}, u32[]{:S(2)}) collective-permute-start(bf16[2,128,1024]{2,1,0:T(8,128)(2,1)S(1)} %get-tuple-element.75.refs_3_), channel_id=1, source_target_pairs={{0,192},{64,0},{128,64},{192,128},{1,193},{65,1},{129,65},{193,129... | collective-permute-start | bytes 1572872 | tf_op jit(solution)/shard_map/ppermute | solution.py:24
  29.2 4.9 %collective-permute-done.2.refs_1_ = bf16[2,128,1024]{2,1,0:T(8,128)(2,1)S(1)} collective-permute-done((bf16[2,128,1024]{2,1,0:T(8,128)(2,1)S(1)}, bf16[2,128,1024]{2,1,0:T(8,128)(2,1)S(1)}, u32[]{:S(2)}, u32[]{:S(2)}) %collective-permute-start.2) | collective-permute-done | bytes 524320 | tf_op jit(solution)/shard_map/ppermute | solution.py:24
  34.1 2.6 %collective-permute-done.3.refs_2_ = bf16[2,128,1024]{2,1,0:T(8,128)(2,1)S(1)} collective-permute-done((bf16[2,128,1024]{2,1,0:T(8,128)(2,1)S(1)}, bf16[2,128,1024]{2,1,0:T(8,128)(2,1)S(1)}, u32[]{:S(2)}, u32[]{:S(2)}) %collective-permute-start.3) | collective-permute-done | bytes 524320 | tf_op jit(solution)/shard_map/ppermute | solution.py:24
  37.6 1.9 %collective-permute-start.6 = (bf16[2,64,1024]{2,1,0:T(8,128)(2,1)S(1)}, bf16[2,64,1024]{2,1,0:T(8,128)(2,1)S(1)}, u32[]{:S(2)}, u32[]{:S(2)}) collective-permute-start(bf16[2,64,1024]{2,1,0:T(8,128)(2,1)S(1)} %get-tuple-element.78.refs_2_), channel_id=1, source_target_pairs={{0,16},{16,0},{32,48},{48,32},{1,17},{17,1},{33,49},{49,33},{2,18}... | collective-permute-start | bytes 786440 | tf_op jit(solution)/shard_map/ppermute | solution.py:28
  39.5 2.0 %collective-permute-start.13 = (bf16[2,128,1024]{2,1,0:T(8,128)(2,1)S(1)}, bf16[2,128,1024]{2,1,0:T(8,128)(2,1)S(1)}, u32[]{:S(2)}, u32[]{:S(2)}) collective-permute-start(bf16[2,128,1024]{2,1,0:T(8,128)(2,1)S(1)} %get-tuple-element.76.refs_3_), channel_id=1, source_target_pairs={{0,192},{64,0},{128,64},{192,128},{1,193},{65,1},{129,65},{193,129... | collective-permute-start | bytes 1572872 | tf_op jit(solution)/shard_map/ppermute | solution.py:24
  41.5 2.5 %collective-permute-done.6.refs_1_ = bf16[2,64,1024]{2,1,0:T(8,128)(2,1)S(1)} collective-permute-done((bf16[2,64,1024]{2,1,0:T(8,128)(2,1)S(1)}, bf16[2,64,1024]{2,1,0:T(8,128)(2,1)S(1)}, u32[]{:S(2)}, u32[]{:S(2)}) %collective-permute-start.6) | collective-permute-done | bytes 262176 | tf_op jit(solution)/shard_map/ppermute | solution.py:28
  44.6 3.0 %collective-permute-start.7 = (bf16[2,32,1024]{2,1,0:T(8,128)(2,1)S(1)}, bf16[2,32,1024]{2,1,0:T(8,128)(2,1)S(1)}, u32[]{:S(2)}, u32[]{:S(2)}) collective-permute-start(bf16[2,32,1024]{2,1,0:T(8,128)(2,1)S(1)} %get-tuple-element.80.refs_3_), channel_id=1, source_target_pairs={{0,48},{16,32},{32,16},{48,0},{1,49},{17,33},{33,17},{49,1},{2,50}... | collective-permute-start | bytes 393224 | tf_op jit(solution)/shard_map/ppermute | solution.py:28
  48.0 0.8 shard_map.64
  48.8 1.9 %collective-permute-start.14 = (bf16[2,64,1024]{2,1,0:T(8,128)(2,1)S(1)}, bf16[2,64,1024]{2,1,0:T(8,128)(2,1)S(1)}, u32[]{:S(2)}, u32[]{:S(2)}) collective-permute-start(bf16[2,64,1024]{2,1,0:T(8,128)(2,1)S(1)} %get-tuple-element.82.refs_4_), channel_id=1, source_target_pairs={{0,16},{16,0},{32,48},{48,32},{1,17},{17,1},{33,49},{49,33},{2,18}... | collective-permute-start | bytes 786440 | tf_op jit(solution)/shard_map/ppermute | solution.py:28
  52.1 2.0 %collective-permute-start.11 = (bf16[1,128,1024]{2,1,0:T(8,128)(2,1)S(1)}, bf16[1,128,1024]{2,1,0:T(8,128)(2,1)S(1)}, u32[]{:S(2)}, u32[]{:S(2)}) collective-permute-start(bf16[1,128,1024]{2,1,0:T(8,128)(2,1)S(1)} %get-tuple-element.85.refs_2_), channel_id=1, source_target_pairs={{0,192},{64,0},{128,64},{192,128},{1,193},{65,1},{129,65},{193,129... | collective-permute-start | bytes 786440 | tf_op jit(solution)/shard_map/ppermute | solution.py:24
  54.1 1.1 collective-permute-done.14.refs_1_
  55.3 2.2 %collective-permute-start.19 = (bf16[2,32,1024]{2,1,0:T(8,128)(2,1)S(1)}, bf16[2,32,1024]{2,1,0:T(8,128)(2,1)S(1)}, u32[]{:S(2)}, u32[]{:S(2)}) collective-permute-start(bf16[2,32,1024]{2,1,0:T(8,128)(2,1)S(1)} %get-tuple-element.83.refs_1_.refs_0_), channel_id=1, source_target_pairs={{0,48},{16,32},{32,16},{48,0},{1,49},{17,33},{33,17},{49,1},{2,50}... | collective-permute-start | bytes 393224 | tf_op jit(solution)/shard_map/ppermute | solution.py:28
  60.0 3.5 %collective-permute-start.17 = (bf16[2,64,1024]{2,1,0:T(8,128)(2,1)S(1)}, bf16[2,64,1024]{2,1,0:T(8,128)(2,1)S(1)}, u32[]{:S(2)}, u32[]{:S(2)}) collective-permute-start(bf16[2,64,1024]{2,1,0:T(8,128)(2,1)S(1)} %get-tuple-element.89.refs_3_), channel_id=1, source_target_pairs={{0,16},{16,0},{32,48},{48,32},{1,17},{17,1},{33,49},{49,33},{2,18}... | collective-permute-start | bytes 786440 | tf_op jit(solution)/shard_map/ppermute | solution.py:28
  63.6 0.8 shard_map.69
  64.3 1.4 collective-permute-start.15
  68.0 3.1 %collective-permute-start.21 = (bf16[2,32,1024]{2,1,0:T(8,128)(2,1)S(1)}, bf16[2,32,1024]{2,1,0:T(8,128)(2,1)S(1)}, u32[]{:S(2)}, u32[]{:S(2)}) collective-permute-start(bf16[2,32,1024]{2,1,0:T(8,128)(2,1)S(1)} %get-tuple-element.95.refs_2_.refs_0_), channel_id=1, source_target_pairs={{0,48},{16,32},{32,16},{48,0},{1,49},{17,33},{33,17},{49,1},{2,50}... | collective-permute-start | bytes 393224 | tf_op jit(solution)/shard_map/ppermute | solution.py:28
  71.9 1.2 collective-permute-start.20
  73.0 3.3 %collective-permute-done.22.refs_1_ = bf16[2,64,1024]{2,1,0:T(8,128)(2,1)S(1)} collective-permute-done((bf16[2,64,1024]{2,1,0:T(8,128)(2,1)S(1)}, bf16[2,64,1024]{2,1,0:T(8,128)(2,1)S(1)}, u32[]{:S(2)}, u32[]{:S(2)}) %collective-permute-start.22) | collective-permute-done | bytes 262176 | tf_op jit(solution)/shard_map/ppermute | solution.py:28
  76.3 1.4 shard_map.73
  78.3 4.1 %collective-permute-start.25 = (bf16[2,64,1024]{2,1,0:T(8,128)(2,1)S(1)}, bf16[2,64,1024]{2,1,0:T(8,128)(2,1)S(1)}, u32[]{:S(2)}, u32[]{:S(2)}) collective-permute-start(bf16[2,64,1024]{2,1,0:T(8,128)(2,1)S(1)} %get-tuple-element.104.refs_0_), channel_id=1, source_target_pairs={{0,16},{16,0},{32,48},{48,32},{1,17},{17,1},{33,49},{49,33},{2,18}... | collective-permute-start | bytes 786440 | tf_op jit(solution)/shard_map/ppermute | solution.py:28
  82.4 2.9 %collective-permute-start.27 = (bf16[2,128,1024]{2,1,0:T(8,128)(2,1)S(1)}, bf16[2,128,1024]{2,1,0:T(8,128)(2,1)S(1)}, u32[]{:S(2)}, u32[]{:S(2)}) collective-permute-start(bf16[2,128,1024]{2,1,0:T(8,128)(2,1)S(1)} %get-tuple-element.99.refs_2_), channel_id=1, source_target_pairs={{0,64},{64,128},{128,192},{192,0},{1,65},{65,129},{129,193},{193,1... | collective-permute-start | bytes 1572872 | tf_op jit(solution)/shard_map/ppermute | solution.py:24
  86.8 0.8 shard_map.76
  87.6 1.1 collective-permute-start.23
  88.7 2.5 %collective-permute-done.25.refs_1_ = bf16[2,64,1024]{2,1,0:T(8,128)(2,1)S(1)} collective-permute-done((bf16[2,64,1024]{2,1,0:T(8,128)(2,1)S(1)}, bf16[2,64,1024]{2,1,0:T(8,128)(2,1)S(1)}, u32[]{:S(2)}, u32[]{:S(2)}) %collective-permute-start.25) | collective-permute-done | bytes 262176 | tf_op jit(solution)/shard_map/ppermute | solution.py:28
  91.2 1.4 shard_map.77
  92.6 2.7 %collective-permute-start.33 = (bf16[2,128,1024]{2,1,0:T(8,128)(2,1)S(1)}, bf16[2,128,1024]{2,1,0:T(8,128)(2,1)S(1)}, u32[]{:S(2)}, u32[]{:S(2)}) collective-permute-start(bf16[2,128,1024]{2,1,0:T(8,128)(2,1)S(1)} %get-tuple-element.106.refs_2_), channel_id=1, source_target_pairs={{0,64},{64,128},{128,192},{192,0},{1,65},{65,129},{129,193},{193,1... | collective-permute-start | bytes 1572872 | tf_op jit(solution)/shard_map/ppermute | solution.py:24
  97.0 3.3 %collective-permute-done.28.refs_1_ = bf16[2,128,1024]{2,1,0:T(8,128)(2,1)S(1)} collective-permute-done((bf16[2,128,1024]{2,1,0:T(8,128)(2,1)S(1)}, bf16[2,128,1024]{2,1,0:T(8,128)(2,1)S(1)}, u32[]{:S(2)}, u32[]{:S(2)}) %collective-permute-start.28) | collective-permute-done | bytes 524320 | tf_op jit(solution)/shard_map/ppermute | solution.py:24
  100.3 1.6 shard_map.80
  102.0 2.0 %collective-permute-start.32 = (bf16[1,128,1024]{2,1,0:T(8,128)(2,1)S(1)}, bf16[1,128,1024]{2,1,0:T(8,128)(2,1)S(1)}, u32[]{:S(2)}, u32[]{:S(2)}) collective-permute-start(bf16[1,128,1024]{2,1,0:T(8,128)(2,1)S(1)} %get-tuple-element.111.refs_4_), channel_id=1, source_target_pairs={{0,192},{64,0},{128,64},{192,128},{1,193},{65,1},{129,65},{193,129... | collective-permute-start | bytes 786440 | tf_op jit(solution)/shard_map/ppermute | solution.py:24
  104.0 4.1 %collective-permute-start.30 = (bf16[2,64,1024]{2,1,0:T(8,128)(2,1)S(1)}, bf16[2,64,1024]{2,1,0:T(8,128)(2,1)S(1)}, u32[]{:S(2)}, u32[]{:S(2)}) collective-permute-start(bf16[2,64,1024]{2,1,0:T(8,128)(2,1)S(1)} %get-tuple-element.113.refs_0_), channel_id=1, source_target_pairs={{0,16},{16,0},{32,48},{48,32},{1,17},{17,1},{33,49},{49,33},{2,18}... | collective-permute-start | bytes 786440 | tf_op jit(solution)/shard_map/ppermute | solution.py:28
  108.9 0.8 collective-permute-done.34.refs_1_
  109.8 1.6 shard_map.82
  111.4 2.5 %collective-permute-start.36 = (bf16[1,128,1024]{2,1,0:T(8,128)(2,1)S(1)}, bf16[1,128,1024]{2,1,0:T(8,128)(2,1)S(1)}, u32[]{:S(2)}, u32[]{:S(2)}) collective-permute-start(bf16[1,128,1024]{2,1,0:T(8,128)(2,1)S(1)} %get-tuple-element.120), channel_id=1, source_target_pairs={{0,64},{64,128},{128,192},{192,0},{1,65},{65,129},{129,193},{193,1... | collective-permute-start | bytes 786440 | tf_op jit(solution)/shard_map/ppermute | solution.py:24
  114.5 1.4 shard_map.83.refs_2_
  115.9 1.4 shard_map.84
  117.8 3.1 %collective-permute-start.35 = (bf16[2,64,1024]{2,1,0:T(8,128)(2,1)S(1)}, bf16[2,64,1024]{2,1,0:T(8,128)(2,1)S(1)}, u32[]{:S(2)}, u32[]{:S(2)}) collective-permute-start(bf16[2,64,1024]{2,1,0:T(8,128)(2,1)S(1)} %get-tuple-element.119.refs_0_), channel_id=1, source_target_pairs={{0,16},{16,0},{32,48},{48,32},{1,17},{17,1},{33,49},{49,33},{2,18}... | collective-permute-start | bytes 786440 | tf_op jit(solution)/shard_map/ppermute | solution.py:28
  121.6 1.3 collective-permute-start.41
  123.0 1.3 collective-permute-done.37.refs_1_
  124.3 1.4 shard_map.86.refs_2_
  125.6 1.4 shard_map.87
  127.0 1.3 collective-permute-start.38
  129.1 6.7 %collective-permute-done.40.refs_0_ = bf16[2,128,1024]{2,1,0:T(8,128)(2,1)S(1)} collective-permute-done((bf16[2,128,1024]{2,1,0:T(8,128)(2,1)S(1)}, bf16[2,128,1024]{2,1,0:T(8,128)(2,1)S(1)}, u32[]{:S(2)}, u32[]{:S(2)}) %collective-permute-start.40) | collective-permute-done | bytes 524320 | tf_op jit(solution)/shard_map/ppermute | solution.py:24
  135.8 1.9 %collective-permute-done.41.refs_1_ = bf16[2,128,1024]{2,1,0:T(8,128)(2,1)S(1)} collective-permute-done((bf16[2,128,1024]{2,1,0:T(8,128)(2,1)S(1)}, bf16[2,128,1024]{2,1,0:T(8,128)(2,1)S(1)}, u32[]{:S(2)}, u32[]{:S(2)}) %collective-permute-start.41) | collective-permute-done | bytes 524320 | tf_op jit(solution)/shard_map/ppermute | solution.py:24
  137.7 1.6 shard_map.88
  139.4 2.0 %collective-permute-start.45 = (bf16[1,128,1024]{2,1,0:T(8,128)(2,1)S(1)}, bf16[1,128,1024]{2,1,0:T(8,128)(2,1)S(1)}, u32[]{:S(2)}, u32[]{:S(2)}) collective-permute-start(bf16[1,128,1024]{2,1,0:T(8,128)(2,1)S(1)} %get-tuple-element.126.refs_3_), channel_id=1, source_target_pairs={{0,192},{64,0},{128,64},{192,128},{1,193},{65,1},{129,65},{193,129... | collective-permute-start | bytes 786440 | tf_op jit(solution)/shard_map/ppermute | solution.py:24
  141.4 3.7 %collective-permute-done.38.refs_0_ = bf16[2,128,1024]{2,1,0:T(8,128)(2,1)S(1)} collective-permute-done((bf16[2,128,1024]{2,1,0:T(8,128)(2,1)S(1)}, bf16[2,128,1024]{2,1,0:T(8,128)(2,1)S(1)}, u32[]{:S(2)}, u32[]{:S(2)}) %collective-permute-start.38) | collective-permute-done | bytes 524320 | tf_op jit(solution)/shard_map/ppermute | solution.py:24
  145.1 3.4 %collective-permute-done.39.refs_1_ = bf16[2,128,1024]{2,1,0:T(8,128)(2,1)S(1)} collective-permute-done((bf16[2,128,1024]{2,1,0:T(8,128)(2,1)S(1)}, bf16[2,128,1024]{2,1,0:T(8,128)(2,1)S(1)}, u32[]{:S(2)}, u32[]{:S(2)}) %collective-permute-start.39) | collective-permute-done | bytes 524320 | tf_op jit(solution)/shard_map/ppermute | solution.py:24
  148.5 1.6 shard_map.89
  150.5 1.7 %collective-permute-start.43 = (bf16[1,128,1024]{2,1,0:T(8,128)(2,1)S(1)}, bf16[1,128,1024]{2,1,0:T(8,128)(2,1)S(1)}, u32[]{:S(2)}, u32[]{:S(2)}) collective-permute-start(bf16[1,128,1024]{2,1,0:T(8,128)(2,1)S(1)} %get-tuple-element.128.refs_3_), channel_id=1, source_target_pairs={{0,192},{64,0},{128,64},{192,128},{1,193},{65,1},{129,65},{193,129... | collective-permute-start | bytes 786440 | tf_op jit(solution)/shard_map/ppermute | solution.py:24
  152.2 1.5 pad_maximum_fusion
  153.7 1.4 shard_map.90.refs_2_
  155.1 1.5 collective-permute-done.42.refs_0_
  156.6 1.5 collective-permute-done.43.refs_1_
  158.0 1.4 shard_map.91
  (76 shorter events, 19.3 us)
Async XLA Ops:
  1.7 8.3 %collective-permute-start = (bf16[1,128,1024]{2,1,0:T(8,128)(2,1)S(1)}, bf16[1,128,1024]{2,1,0:T(8,128)(2,1)S(1)}, u32[]{:S(2)}, u32[]{:S(2)}) collective-permute-start(bf16[1,128,1024]{2,1,0:T(8,128)(2,1)S(1)} %get-tuple-element.140.refs_1_), channel_id=1, source_target_pairs={{0,64},{64,128},{128,192},{192,0},{1,65},{65,129},{129,193},{193,1... | collective-permute-start | bytes 786440 | tf_op jit(solution)/shard_map/ppermute | solution.py:24
  2.0 9.1 %collective-permute-start.1 = (bf16[1,128,1024]{2,1,0:T(8,128)(2,1)S(1)}, bf16[1,128,1024]{2,1,0:T(8,128)(2,1)S(1)}, u32[]{:S(2)}, u32[]{:S(2)}) collective-permute-start(bf16[1,128,1024]{2,1,0:T(8,128)(2,1)S(1)} %get-tuple-element.139), channel_id=1, source_target_pairs={{0,192},{64,0},{128,64},{192,128},{1,193},{65,1},{129,65},{193,129... | collective-permute-start | bytes 786440 | tf_op jit(solution)/shard_map/ppermute | solution.py:24
  3.9 3.4 %copy-start = (bf16[1,8,512,1024]{3,2,1,0:T(8,128)(2,1)S(1)}, bf16[1,8,512,1024]{3,2,1,0:T(8,128)(2,1)}, u32[]{:S(2)}) copy-start(bf16[1,8,512,1024]{3,2,1,0:T(8,128)(2,1)} %refs_0_.19) | copy-start | bytes 25165828
  8.0 14.9 %collective-permute-start.4 = (bf16[2,128,1024]{2,1,0:T(8,128)(2,1)S(1)}, bf16[2,128,1024]{2,1,0:T(8,128)(2,1)S(1)}, u32[]{:S(2)}, u32[]{:S(2)}) collective-permute-start(bf16[2,128,1024]{2,1,0:T(8,128)(2,1)S(1)} %get-tuple-element.74), channel_id=1, source_target_pairs={{0,64},{64,128},{128,192},{192,0},{1,65},{65,129},{129,193},{193,1... | collective-permute-start | bytes 1572872 | tf_op jit(solution)/shard_map/ppermute | solution.py:24
  9.5 16.1 %collective-permute-start.5 = (bf16[2,128,1024]{2,1,0:T(8,128)(2,1)S(1)}, bf16[2,128,1024]{2,1,0:T(8,128)(2,1)S(1)}, u32[]{:S(2)}, u32[]{:S(2)}) collective-permute-start(bf16[2,128,1024]{2,1,0:T(8,128)(2,1)S(1)} %get-tuple-element.71.refs_3_), channel_id=1, source_target_pairs={{0,192},{64,0},{128,64},{192,128},{1,193},{65,1},{129,65},{193,129... | collective-permute-start | bytes 1572872 | tf_op jit(solution)/shard_map/ppermute | solution.py:24
  11.9 22.2 %collective-permute-start.2 = (bf16[2,128,1024]{2,1,0:T(8,128)(2,1)S(1)}, bf16[2,128,1024]{2,1,0:T(8,128)(2,1)S(1)}, u32[]{:S(2)}, u32[]{:S(2)}) collective-permute-start(bf16[2,128,1024]{2,1,0:T(8,128)(2,1)S(1)} %get-tuple-element.72), channel_id=1, source_target_pairs={{0,64},{64,128},{128,192},{192,0},{1,65},{65,129},{129,193},{193,1... | collective-permute-start | bytes 1572872 | tf_op jit(solution)/shard_map/ppermute | solution.py:24
  13.6 23.2 %collective-permute-start.3 = (bf16[2,128,1024]{2,1,0:T(8,128)(2,1)S(1)}, bf16[2,128,1024]{2,1,0:T(8,128)(2,1)S(1)}, u32[]{:S(2)}, u32[]{:S(2)}) collective-permute-start(bf16[2,128,1024]{2,1,0:T(8,128)(2,1)S(1)} %get-tuple-element.73.refs_3_), channel_id=1, source_target_pairs={{0,192},{64,0},{128,64},{192,128},{1,193},{65,1},{129,65},{193,129... | collective-permute-start | bytes 1572872 | tf_op jit(solution)/shard_map/ppermute | solution.py:24
  26.3 21.3 %collective-permute-start.8 = (bf16[2,128,1024]{2,1,0:T(8,128)(2,1)S(1)}, bf16[2,128,1024]{2,1,0:T(8,128)(2,1)S(1)}, u32[]{:S(2)}, u32[]{:S(2)}) collective-permute-start(bf16[2,128,1024]{2,1,0:T(8,128)(2,1)S(1)} %get-tuple-element.81), channel_id=1, source_target_pairs={{0,64},{64,128},{128,192},{192,0},{1,65},{65,129},{129,193},{193,1... | collective-permute-start | bytes 1572872 | tf_op jit(solution)/shard_map/ppermute | solution.py:24
  26.4 21.6 %slice-start = ((s8[8388608]{0:T(1024)(128)(4,1)}), s8[4194304]{0:T(1024)(128)(4,1)S(1)}, s32[]{:S(2)}) async-start(s8[8388608]{0:T(1024)(128)(4,1)} %bitcast.6), calls=%async_computation | async-start | bytes 8388608
  26.4 21.6 %collective-permute-start.9 = (bf16[2,128,1024]{2,1,0:T(8,128)(2,1)S(1)}, bf16[2,128,1024]{2,1,0:T(8,128)(2,1)S(1)}, u32[]{:S(2)}, u32[]{:S(2)}) collective-permute-start(bf16[2,128,1024]{2,1,0:T(8,128)(2,1)S(1)} %get-tuple-element.75.refs_3_), channel_id=1, source_target_pairs={{0,192},{64,0},{128,64},{192,128},{1,193},{65,1},{129,65},{193,129... | collective-permute-start | bytes 1572872 | tf_op jit(solution)/shard_map/ppermute | solution.py:24
  36.8 11.2 %slice-start.1 = ((s8[8388608]{0:T(1024)(128)(4,1)}), s8[4194304]{0:T(1024)(128)(4,1)S(1)}, s32[]{:S(2)}) async-start(s8[8388608]{0:T(1024)(128)(4,1)} %bitcast.6), calls=%async_computation.1 | async-start | bytes 8388608
  36.8 14.0 %copy-start.1 = (f32[8,32,1024]{2,1,0:T(8,128)S(1)}, f32[8,32,1024]{2,1,0:T(8,128)}, u32[]{:S(2)}) copy-start(f32[8,32,1024]{2,1,0:T(8,128)} %refs_2_.7) | copy-start | bytes 3145732
  36.8 14.0 %copy-start.2 = (f32[8,32,1024]{2,1,0:T(8,128)S(1)}, f32[8,32,1024]{2,1,0:T(8,128)}, u32[]{:S(2)}) copy-start(f32[8,32,1024]{2,1,0:T(8,128)} %refs_3_.7) | copy-start | bytes 3145732
  37.6 6.5 %collective-permute-start.6 = (bf16[2,64,1024]{2,1,0:T(8,128)(2,1)S(1)}, bf16[2,64,1024]{2,1,0:T(8,128)(2,1)S(1)}, u32[]{:S(2)}, u32[]{:S(2)}) collective-permute-start(bf16[2,64,1024]{2,1,0:T(8,128)(2,1)S(1)} %get-tuple-element.78.refs_2_), channel_id=1, source_target_pairs={{0,16},{16,0},{32,48},{48,32},{1,17},{17,1},{33,49},{49,33},{2,18}... | collective-permute-start | bytes 786440 | tf_op jit(solution)/shard_map/ppermute | solution.py:28
  39.5 18.6 %collective-permute-start.12 = (bf16[2,128,1024]{2,1,0:T(8,128)(2,1)S(1)}, bf16[2,128,1024]{2,1,0:T(8,128)(2,1)S(1)}, u32[]{:S(2)}, u32[]{:S(2)}) collective-permute-start(bf16[2,128,1024]{2,1,0:T(8,128)(2,1)S(1)} %get-tuple-element.86), channel_id=1, source_target_pairs={{0,64},{64,128},{128,192},{192,0},{1,65},{65,129},{129,193},{193,1... | collective-permute-start | bytes 1572872 | tf_op jit(solution)/shard_map/ppermute | solution.py:24
  39.5 19.7 %collective-permute-start.13 = (bf16[2,128,1024]{2,1,0:T(8,128)(2,1)S(1)}, bf16[2,128,1024]{2,1,0:T(8,128)(2,1)S(1)}, u32[]{:S(2)}, u32[]{:S(2)}) collective-permute-start(bf16[2,128,1024]{2,1,0:T(8,128)(2,1)S(1)} %get-tuple-element.76.refs_3_), channel_id=1, source_target_pairs={{0,192},{64,0},{128,64},{192,128},{1,193},{65,1},{129,65},{193,129... | collective-permute-start | bytes 1572872 | tf_op jit(solution)/shard_map/ppermute | solution.py:24
  44.6 6.1 %collective-permute-start.7 = (bf16[2,32,1024]{2,1,0:T(8,128)(2,1)S(1)}, bf16[2,32,1024]{2,1,0:T(8,128)(2,1)S(1)}, u32[]{:S(2)}, u32[]{:S(2)}) collective-permute-start(bf16[2,32,1024]{2,1,0:T(8,128)(2,1)S(1)} %get-tuple-element.80.refs_3_), channel_id=1, source_target_pairs={{0,48},{16,32},{32,16},{48,0},{1,49},{17,33},{33,17},{49,1},{2,50}... | collective-permute-start | bytes 393224 | tf_op jit(solution)/shard_map/ppermute | solution.py:28
  48.8 6.5 %collective-permute-start.14 = (bf16[2,64,1024]{2,1,0:T(8,128)(2,1)S(1)}, bf16[2,64,1024]{2,1,0:T(8,128)(2,1)S(1)}, u32[]{:S(2)}, u32[]{:S(2)}) collective-permute-start(bf16[2,64,1024]{2,1,0:T(8,128)(2,1)S(1)} %get-tuple-element.82.refs_4_), channel_id=1, source_target_pairs={{0,16},{16,0},{32,48},{48,32},{1,17},{17,1},{33,49},{49,33},{2,18}... | collective-permute-start | bytes 786440 | tf_op jit(solution)/shard_map/ppermute | solution.py:28
  52.0 11.5 %collective-permute-start.10 = (bf16[1,128,1024]{2,1,0:T(8,128)(2,1)S(1)}, bf16[1,128,1024]{2,1,0:T(8,128)(2,1)S(1)}, u32[]{:S(2)}, u32[]{:S(2)}) collective-permute-start(bf16[1,128,1024]{2,1,0:T(8,128)(2,1)S(1)} %get-tuple-element.84), channel_id=1, source_target_pairs={{0,64},{64,128},{128,192},{192,0},{1,65},{65,129},{129,193},{193,1... | collective-permute-start | bytes 786440 | tf_op jit(solution)/shard_map/ppermute | solution.py:24
  52.1 11.4 %collective-permute-start.11 = (bf16[1,128,1024]{2,1,0:T(8,128)(2,1)S(1)}, bf16[1,128,1024]{2,1,0:T(8,128)(2,1)S(1)}, u32[]{:S(2)}, u32[]{:S(2)}) collective-permute-start(bf16[1,128,1024]{2,1,0:T(8,128)(2,1)S(1)} %get-tuple-element.85.refs_2_), channel_id=1, source_target_pairs={{0,192},{64,0},{128,64},{192,128},{1,193},{65,1},{129,65},{193,129... | collective-permute-start | bytes 786440 | tf_op jit(solution)/shard_map/ppermute | solution.py:24
  55.3 11.2 %collective-permute-start.19 = (bf16[2,32,1024]{2,1,0:T(8,128)(2,1)S(1)}, bf16[2,32,1024]{2,1,0:T(8,128)(2,1)S(1)}, u32[]{:S(2)}, u32[]{:S(2)}) collective-permute-start(bf16[2,32,1024]{2,1,0:T(8,128)(2,1)S(1)} %get-tuple-element.83.refs_1_.refs_0_), channel_id=1, source_target_pairs={{0,48},{16,32},{32,16},{48,0},{1,49},{17,33},{33,17},{49,1},{2,50}... | collective-permute-start | bytes 393224 | tf_op jit(solution)/shard_map/ppermute | solution.py:28
  58.1 9.3 %collective-permute-start.18 = (bf16[2,32,1024]{2,1,0:T(8,128)(2,1)S(1)}, bf16[2,32,1024]{2,1,0:T(8,128)(2,1)S(1)}, u32[]{:S(2)}, u32[]{:S(2)}) collective-permute-start(bf16[2,32,1024]{2,1,0:T(8,128)(2,1)S(1)} %get-tuple-element.88.refs_3_), channel_id=1, source_target_pairs={{0,48},{16,32},{32,16},{48,0},{1,49},{17,33},{33,17},{49,1},{2,50}... | collective-permute-start | bytes 393224 | tf_op jit(solution)/shard_map/ppermute | solution.py:28
  60.0 11.2 %collective-permute-start.17 = (bf16[2,64,1024]{2,1,0:T(8,128)(2,1)S(1)}, bf16[2,64,1024]{2,1,0:T(8,128)(2,1)S(1)}, u32[]{:S(2)}, u32[]{:S(2)}) collective-permute-start(bf16[2,64,1024]{2,1,0:T(8,128)(2,1)S(1)} %get-tuple-element.89.refs_3_), channel_id=1, source_target_pairs={{0,16},{16,0},{32,48},{48,32},{1,17},{17,1},{33,49},{49,33},{2,18}... | collective-permute-start | bytes 786440 | tf_op jit(solution)/shard_map/ppermute | solution.py:28
  64.3 21.6 %collective-permute-start.15 = (bf16[2,128,1024]{2,1,0:T(8,128)(2,1)S(1)}, bf16[2,128,1024]{2,1,0:T(8,128)(2,1)S(1)}, u32[]{:S(2)}, u32[]{:S(2)}) collective-permute-start(bf16[2,128,1024]{2,1,0:T(8,128)(2,1)S(1)} %get-tuple-element.90), channel_id=1, source_target_pairs={{0,64},{64,128},{128,192},{192,0},{1,65},{65,129},{129,193},{193,1... | collective-permute-start | bytes 1572872 | tf_op jit(solution)/shard_map/ppermute | solution.py:24
  65.7 21.0 %collective-permute-start.16 = (bf16[2,128,1024]{2,1,0:T(8,128)(2,1)S(1)}, bf16[2,128,1024]{2,1,0:T(8,128)(2,1)S(1)}, u32[]{:S(2)}, u32[]{:S(2)}) collective-permute-start(bf16[2,128,1024]{2,1,0:T(8,128)(2,1)S(1)} %get-tuple-element.91.refs_2_), channel_id=1, source_target_pairs={{0,192},{64,0},{128,64},{192,128},{1,193},{65,1},{129,65},{193,129... | collective-permute-start | bytes 1572872 | tf_op jit(solution)/shard_map/ppermute | solution.py:24
  67.0 9.3 %collective-permute-start.22 = (bf16[2,64,1024]{2,1,0:T(8,128)(2,1)S(1)}, bf16[2,64,1024]{2,1,0:T(8,128)(2,1)S(1)}, u32[]{:S(2)}, u32[]{:S(2)}) collective-permute-start(bf16[2,64,1024]{2,1,0:T(8,128)(2,1)S(1)} %get-tuple-element.98.refs_0_), channel_id=1, source_target_pairs={{0,16},{16,0},{32,48},{48,32},{1,17},{17,1},{33,49},{49,33},{2,18}... | collective-permute-start | bytes 786440 | tf_op jit(solution)/shard_map/ppermute | solution.py:28
  68.0 9.7 %collective-permute-start.21 = (bf16[2,32,1024]{2,1,0:T(8,128)(2,1)S(1)}, bf16[2,32,1024]{2,1,0:T(8,128)(2,1)S(1)}, u32[]{:S(2)}, u32[]{:S(2)}) collective-permute-start(bf16[2,32,1024]{2,1,0:T(8,128)(2,1)S(1)} %get-tuple-element.95.refs_2_.refs_0_), channel_id=1, source_target_pairs={{0,48},{16,32},{32,16},{48,0},{1,49},{17,33},{33,17},{49,1},{2,50}... | collective-permute-start | bytes 393224 | tf_op jit(solution)/shard_map/ppermute | solution.py:28
  71.9 13.5 %collective-permute-start.20 = (bf16[2,32,1024]{2,1,0:T(8,128)(2,1)S(1)}, bf16[2,32,1024]{2,1,0:T(8,128)(2,1)S(1)}, u32[]{:S(2)}, u32[]{:S(2)}) collective-permute-start(bf16[2,32,1024]{2,1,0:T(8,128)(2,1)S(1)} %get-tuple-element.97.refs_2_), channel_id=1, source_target_pairs={{0,48},{16,32},{32,16},{48,0},{1,49},{17,33},{33,17},{49,1},{2,50}... | collective-permute-start | bytes 393224 | tf_op jit(solution)/shard_map/ppermute | solution.py:28
  78.3 12.9 %collective-permute-start.25 = (bf16[2,64,1024]{2,1,0:T(8,128)(2,1)S(1)}, bf16[2,64,1024]{2,1,0:T(8,128)(2,1)S(1)}, u32[]{:S(2)}, u32[]{:S(2)}) collective-permute-start(bf16[2,64,1024]{2,1,0:T(8,128)(2,1)S(1)} %get-tuple-element.104.refs_0_), channel_id=1, source_target_pairs={{0,16},{16,0},{32,48},{48,32},{1,17},{17,1},{33,49},{49,33},{2,18}... | collective-permute-start | bytes 786440 | tf_op jit(solution)/shard_map/ppermute | solution.py:28
  82.4 14.7 %collective-permute-start.27 = (bf16[2,128,1024]{2,1,0:T(8,128)(2,1)S(1)}, bf16[2,128,1024]{2,1,0:T(8,128)(2,1)S(1)}, u32[]{:S(2)}, u32[]{:S(2)}) collective-permute-start(bf16[2,128,1024]{2,1,0:T(8,128)(2,1)S(1)} %get-tuple-element.99.refs_2_), channel_id=1, source_target_pairs={{0,64},{64,128},{128,192},{192,0},{1,65},{65,129},{129,193},{193,1... | collective-permute-start | bytes 1572872 | tf_op jit(solution)/shard_map/ppermute | solution.py:24
  85.3 15.0 %collective-permute-start.28 = (bf16[2,128,1024]{2,1,0:T(8,128)(2,1)S(1)}, bf16[2,128,1024]{2,1,0:T(8,128)(2,1)S(1)}, u32[]{:S(2)}, u32[]{:S(2)}) collective-permute-start(bf16[2,128,1024]{2,1,0:T(8,128)(2,1)S(1)} %get-tuple-element.99.refs_2_), channel_id=1, source_target_pairs={{0,192},{64,0},{128,64},{192,128},{1,193},{65,1},{129,65},{193,129... | collective-permute-start | bytes 1572872 | tf_op jit(solution)/shard_map/ppermute | solution.py:24
  86.0 9.3 %collective-permute-start.24 = (bf16[2,32,1024]{2,1,0:T(8,128)(2,1)S(1)}, bf16[2,32,1024]{2,1,0:T(8,128)(2,1)S(1)}, u32[]{:S(2)}, u32[]{:S(2)}) collective-permute-start(bf16[2,32,1024]{2,1,0:T(8,128)(2,1)S(1)} %get-tuple-element.101.refs_3_.refs_0_), channel_id=1, source_target_pairs={{0,48},{16,32},{32,16},{48,0},{1,49},{17,33},{33,17},{49,1},{2,50}... | collective-permute-start | bytes 393224 | tf_op jit(solution)/shard_map/ppermute | solution.py:28
  87.6 8.3 %collective-permute-start.23 = (bf16[2,64,1024]{2,1,0:T(8,128)(2,1)S(1)}, bf16[2,64,1024]{2,1,0:T(8,128)(2,1)S(1)}, u32[]{:S(2)}, u32[]{:S(2)}) collective-permute-start(bf16[2,64,1024]{2,1,0:T(8,128)(2,1)S(1)} %get-tuple-element.103.refs_3_), channel_id=1, source_target_pairs={{0,16},{16,0},{32,48},{48,32},{1,17},{17,1},{33,49},{49,33},{2,18}... | collective-permute-start | bytes 786440 | tf_op jit(solution)/shard_map/ppermute | solution.py:28
  92.6 16.2 %collective-permute-start.33 = (bf16[2,128,1024]{2,1,0:T(8,128)(2,1)S(1)}, bf16[2,128,1024]{2,1,0:T(8,128)(2,1)S(1)}, u32[]{:S(2)}, u32[]{:S(2)}) collective-permute-start(bf16[2,128,1024]{2,1,0:T(8,128)(2,1)S(1)} %get-tuple-element.106.refs_2_), channel_id=1, source_target_pairs={{0,64},{64,128},{128,192},{192,0},{1,65},{65,129},{129,193},{193,1... | collective-permute-start | bytes 1572872 | tf_op jit(solution)/shard_map/ppermute | solution.py:24
  95.3 14.5 %collective-permute-start.34 = (bf16[2,128,1024]{2,1,0:T(8,128)(2,1)S(1)}, bf16[2,128,1024]{2,1,0:T(8,128)(2,1)S(1)}, u32[]{:S(2)}, u32[]{:S(2)}) collective-permute-start(bf16[2,128,1024]{2,1,0:T(8,128)(2,1)S(1)} %get-tuple-element.106.refs_2_), channel_id=1, source_target_pairs={{0,192},{64,0},{128,64},{192,128},{1,193},{65,1},{129,65},{193,129... | collective-permute-start | bytes 1572872 | tf_op jit(solution)/shard_map/ppermute | solution.py:24
  96.5 7.6 %collective-permute-start.26 = (bf16[2,32,1024]{2,1,0:T(8,128)(2,1)S(1)}, bf16[2,32,1024]{2,1,0:T(8,128)(2,1)S(1)}, u32[]{:S(2)}, u32[]{:S(2)}) collective-permute-start(bf16[2,32,1024]{2,1,0:T(8,128)(2,1)S(1)} %get-tuple-element.109.refs_3_), channel_id=1, source_target_pairs={{0,48},{16,32},{32,16},{48,0},{1,49},{17,33},{33,17},{49,1},{2,50}... | collective-permute-start | bytes 393224 | tf_op jit(solution)/shard_map/ppermute | solution.py:28
  101.9 11.9 %collective-permute-start.31 = (bf16[1,128,1024]{2,1,0:T(8,128)(2,1)S(1)}, bf16[1,128,1024]{2,1,0:T(8,128)(2,1)S(1)}, u32[]{:S(2)}, u32[]{:S(2)}) collective-permute-start(bf16[1,128,1024]{2,1,0:T(8,128)(2,1)S(1)} %get-tuple-element.114), channel_id=1, source_target_pairs={{0,64},{64,128},{128,192},{192,0},{1,65},{65,129},{129,193},{193,1... | collective-permute-start | bytes 786440 | tf_op jit(solution)/shard_map/ppermute | solution.py:24
  102.0 12.5 %collective-permute-start.32 = (bf16[1,128,1024]{2,1,0:T(8,128)(2,1)S(1)}, bf16[1,128,1024]{2,1,0:T(8,128)(2,1)S(1)}, u32[]{:S(2)}, u32[]{:S(2)}) collective-permute-start(bf16[1,128,1024]{2,1,0:T(8,128)(2,1)S(1)} %get-tuple-element.111.refs_4_), channel_id=1, source_target_pairs={{0,192},{64,0},{128,64},{192,128},{1,193},{65,1},{129,65},{193,129... | collective-permute-start | bytes 786440 | tf_op jit(solution)/shard_map/ppermute | solution.py:24
  104.0 11.8 %collective-permute-start.30 = (bf16[2,64,1024]{2,1,0:T(8,128)(2,1)S(1)}, bf16[2,64,1024]{2,1,0:T(8,128)(2,1)S(1)}, u32[]{:S(2)}, u32[]{:S(2)}) collective-permute-start(bf16[2,64,1024]{2,1,0:T(8,128)(2,1)S(1)} %get-tuple-element.113.refs_0_), channel_id=1, source_target_pairs={{0,16},{16,0},{32,48},{48,32},{1,17},{17,1},{33,49},{49,33},{2,18}... | collective-permute-start | bytes 786440 | tf_op jit(solution)/shard_map/ppermute | solution.py:28
  108.8 8.4 %collective-permute-start.29 = (bf16[2,32,1024]{2,1,0:T(8,128)(2,1)S(1)}, bf16[2,32,1024]{2,1,0:T(8,128)(2,1)S(1)}, u32[]{:S(2)}, u32[]{:S(2)}) collective-permute-start(bf16[2,32,1024]{2,1,0:T(8,128)(2,1)S(1)} %get-tuple-element.112.refs_3_.refs_0_), channel_id=1, source_target_pairs={{0,48},{16,32},{32,16},{48,0},{1,49},{17,33},{33,17},{49,1},{2,50}... | collective-permute-start | bytes 393224 | tf_op jit(solution)/shard_map/ppermute | solution.py:28
  111.4 11.6 %collective-permute-start.36 = (bf16[1,128,1024]{2,1,0:T(8,128)(2,1)S(1)}, bf16[1,128,1024]{2,1,0:T(8,128)(2,1)S(1)}, u32[]{:S(2)}, u32[]{:S(2)}) collective-permute-start(bf16[1,128,1024]{2,1,0:T(8,128)(2,1)S(1)} %get-tuple-element.120), channel_id=1, source_target_pairs={{0,64},{64,128},{128,192},{192,0},{1,65},{65,129},{129,193},{193,1... | collective-permute-start | bytes 786440 | tf_op jit(solution)/shard_map/ppermute | solution.py:24
  113.9 10.4 %collective-permute-start.37 = (bf16[1,128,1024]{2,1,0:T(8,128)(2,1)S(1)}, bf16[1,128,1024]{2,1,0:T(8,128)(2,1)S(1)}, u32[]{:S(2)}, u32[]{:S(2)}) collective-permute-start(bf16[1,128,1024]{2,1,0:T(8,128)(2,1)S(1)} %get-tuple-element.117.refs_3_), channel_id=1, source_target_pairs={{0,192},{64,0},{128,64},{192,128},{1,193},{65,1},{129,65},{193,129... | collective-permute-start | bytes 786440 | tf_op jit(solution)/shard_map/ppermute | solution.py:24
  117.8 7.8 %collective-permute-start.35 = (bf16[2,64,1024]{2,1,0:T(8,128)(2,1)S(1)}, bf16[2,64,1024]{2,1,0:T(8,128)(2,1)S(1)}, u32[]{:S(2)}, u32[]{:S(2)}) collective-permute-start(bf16[2,64,1024]{2,1,0:T(8,128)(2,1)S(1)} %get-tuple-element.119.refs_0_), channel_id=1, source_target_pairs={{0,16},{16,0},{32,48},{48,32},{1,17},{17,1},{33,49},{49,33},{2,18}... | collective-permute-start | bytes 786440 | tf_op jit(solution)/shard_map/ppermute | solution.py:28
  120.9 14.9 %collective-permute-start.40 = (bf16[2,128,1024]{2,1,0:T(8,128)(2,1)S(1)}, bf16[2,128,1024]{2,1,0:T(8,128)(2,1)S(1)}, u32[]{:S(2)}, u32[]{:S(2)}) collective-permute-start(bf16[2,128,1024]{2,1,0:T(8,128)(2,1)S(1)} %get-tuple-element.118.refs_2_), channel_id=1, source_target_pairs={{0,64},{64,128},{128,192},{192,0},{1,65},{65,129},{129,193},{193,1... | collective-permute-start | bytes 1572872 | tf_op jit(solution)/shard_map/ppermute | solution.py:24
  121.6 16.1 %collective-permute-start.41 = (bf16[2,128,1024]{2,1,0:T(8,128)(2,1)S(1)}, bf16[2,128,1024]{2,1,0:T(8,128)(2,1)S(1)}, u32[]{:S(2)}, u32[]{:S(2)}) collective-permute-start(bf16[2,128,1024]{2,1,0:T(8,128)(2,1)S(1)} %get-tuple-element.118.refs_2_), channel_id=1, source_target_pairs={{0,192},{64,0},{128,64},{192,128},{1,193},{65,1},{129,65},{193,129... | collective-permute-start | bytes 1572872 | tf_op jit(solution)/shard_map/ppermute | solution.py:24
  127.0 18.1 %collective-permute-start.38 = (bf16[2,128,1024]{2,1,0:T(8,128)(2,1)S(1)}, bf16[2,128,1024]{2,1,0:T(8,128)(2,1)S(1)}, u32[]{:S(2)}, u32[]{:S(2)}) collective-permute-start(bf16[2,128,1024]{2,1,0:T(8,128)(2,1)S(1)} %get-tuple-element.123.refs_3_), channel_id=1, source_target_pairs={{0,64},{64,128},{128,192},{192,0},{1,65},{65,129},{129,193},{193,1... | collective-permute-start | bytes 1572872 | tf_op jit(solution)/shard_map/ppermute | solution.py:24
  128.4 20.1 %collective-permute-start.39 = (bf16[2,128,1024]{2,1,0:T(8,128)(2,1)S(1)}, bf16[2,128,1024]{2,1,0:T(8,128)(2,1)S(1)}, u32[]{:S(2)}, u32[]{:S(2)}) collective-permute-start(bf16[2,128,1024]{2,1,0:T(8,128)(2,1)S(1)} %get-tuple-element.123.refs_3_), channel_id=1, source_target_pairs={{0,192},{64,0},{128,64},{192,128},{1,193},{65,1},{129,65},{193,129... | collective-permute-start | bytes 1572872 | tf_op jit(solution)/shard_map/ppermute | solution.py:24
  139.3 14.4 %collective-permute-start.44 = (bf16[1,128,1024]{2,1,0:T(8,128)(2,1)S(1)}, bf16[1,128,1024]{2,1,0:T(8,128)(2,1)S(1)}, u32[]{:S(2)}, u32[]{:S(2)}) collective-permute-start(bf16[1,128,1024]{2,1,0:T(8,128)(2,1)S(1)} %get-tuple-element.129), channel_id=1, source_target_pairs={{0,64},{64,128},{128,192},{192,0},{1,65},{65,129},{129,193},{193,1... | collective-permute-start | bytes 786440 | tf_op jit(solution)/shard_map/ppermute | solution.py:24
  139.4 14.3 %collective-permute-start.45 = (bf16[1,128,1024]{2,1,0:T(8,128)(2,1)S(1)}, bf16[1,128,1024]{2,1,0:T(8,128)(2,1)S(1)}, u32[]{:S(2)}, u32[]{:S(2)}) collective-permute-start(bf16[1,128,1024]{2,1,0:T(8,128)(2,1)S(1)} %get-tuple-element.126.refs_3_), channel_id=1, source_target_pairs={{0,192},{64,0},{128,64},{192,128},{1,193},{65,1},{129,65},{193,129... | collective-permute-start | bytes 786440 | tf_op jit(solution)/shard_map/ppermute | solution.py:24
  150.1 6.4 %collective-permute-start.42 = (bf16[1,128,1024]{2,1,0:T(8,128)(2,1)S(1)}, bf16[1,128,1024]{2,1,0:T(8,128)(2,1)S(1)}, u32[]{:S(2)}, u32[]{:S(2)}) collective-permute-start(bf16[1,128,1024]{2,1,0:T(8,128)(2,1)S(1)} %get-tuple-element.127), channel_id=1, source_target_pairs={{0,64},{64,128},{128,192},{192,0},{1,65},{65,129},{129,193},{193,1... | collective-permute-start | bytes 786440 | tf_op jit(solution)/shard_map/ppermute | solution.py:24
  150.5 7.6 %collective-permute-start.43 = (bf16[1,128,1024]{2,1,0:T(8,128)(2,1)S(1)}, bf16[1,128,1024]{2,1,0:T(8,128)(2,1)S(1)}, u32[]{:S(2)}, u32[]{:S(2)}) collective-permute-start(bf16[1,128,1024]{2,1,0:T(8,128)(2,1)S(1)} %get-tuple-element.128.refs_3_), channel_id=1, source_target_pairs={{0,192},{64,0},{128,64},{192,128},{1,193},{65,1},{129,65},{193,129... | collective-permute-start | bytes 786440 | tf_op jit(solution)/shard_map/ppermute | solution.py:24

commit v4 on v2

--- a/solution.py
+++ b/solution.py
@@ -49,7 +49,7 @@
         self.n = rows // NY
         self.m = self.n // NZ
         self.last = None
-        self.out, self.new_master, self.new_momentum = None, {}, {}
+        self.out, self.new_master, self.new_momentum, self.block = None, {}, {}, {}
 
     def call(self, body, ins, outs, alias=(), scratch=()):
         arrays = [a for a, _ in ins]
@@ -226,67 +226,76 @@
     def whole(self, c, got):
         p, n, m, w = self.p, self.n, self.m, self.w
 
-        def body(where, mine, came, out, block, sems):
+        def body(where, mine, came, block, mark):
             z = where[1]
             for src, at, k in ((mine, 0, 0), (mine, m, 3), (came, 0, 1), (came, m, 2)):
                 block[:, ds(z ^ k, m)] = src[:, at : at + m]
-            move((block, out.at[self.of_out(where, c, 0, 0, p)], sems.at[0]))
-
-        self.out, block = self.call(
+
+        block, _ = self.call(
             body,
             [(a, self.full((p, 2 * m, w))) for a in got],
-            [((self.projs, NY * n, w), BF16, HBM), ((p, n, w), BF16, self.full((p, n, w)))],
-            alias=[(self.out, 0)],
-            scratch=[pltpu.SemaphoreType.DMA((1,))],
-        )
+            [((p, n, w), BF16, self.full((p, n, w))), ((8, 128), F32, self.full((8, 128)))],
+        )
+        self.block[c] = block
         return shift(block, 1), shift(block, -1)
+
+    def blocks_out(self, where, c, refs, out, sems, at):
+        return [
+            (ref, out.at[self.of_out(where, c, d, 0, self.p)], sems.at[at + k])
+            for k, (ref, d) in enumerate(zip(refs, (0, 3, 1)))
+        ]
 
     def pass_on(self, c, got):
         p, h, n, w = self.p, self.h, self.n, self.w
-        many = len(got) // 2
+        late = c == CHUNKS - 1
+        blocks = (self.block[c],) + tuple(got)
+        if late:
+            self.late = blocks
 
         def body(where, *refs):
-            came, (out, up, down, sems) = refs[: 2 * many], refs[2 * many :]
-            copies = []
-            for j in range(many):
-                below, above = came[2 * j], came[2 * j + 1]
-                copies += [
-                    (below.at[pl.ds(0, h)], up.at[pl.ds(j * h, h)], sems.at[4 * j]),
-                    (above.at[pl.ds(h, h)], down.at[pl.ds(j * h, h)], sems.at[4 * j + 1]),
-                    (below, out.at[self.of_out(where, c + j, 3, 0, p)], sems.at[4 * j + 2]),
-                    (above, out.at[self.of_out(where, c + j, 1, 0, p)], sems.at[4 * j + 3]),
-                ]
+            (_, below, above), (up, down, sems) = refs[:3], refs[-3:]
+            copies = [
+                (below.at[pl.ds(0, h)], up, sems.at[0]),
+                (above.at[pl.ds(h, h)], down, sems.at[1]),
+            ]
+            if not late:
+                copies += self.blocks_out(where, c, refs[:3], refs[3], sems, 2)
             move(*copies)
 
-        self.out, up, down = self.call(
-            body,
-            [(a, ANY) for a in got],
-            [(self.out.shape, BF16, HBM)] + [((many * h, n, w), BF16, ANY)] * 2,
-            alias=[(self.out, 0)],
-            scratch=[pltpu.SemaphoreType.DMA((4 * many,))],
-        )
-        return shift(up, 1), shift(down, -1)
+        outs = [((h, n, w), BF16, ANY)] * 2
+        if not late:
+            outs = [((self.projs, NY * n, w), BF16, HBM)] + outs
+        made = self.call(
+            body,
+            [(a, ANY) for a in blocks],
+            outs,
+            alias=[] if late else [(self.out, 0)],
+            scratch=[pltpu.SemaphoreType.DMA((5,))],
+        )
+        if not late:
+            self.out = made[0]
+        return shift(made[-2], 1), shift(made[-1], -1)
 
     def finish(self, c, got):
         h = self.h
-        many = got[0].shape[0] // h
-
-        def body(where, low, high, out, sems):
-            copies = []
-            for j in range(many):
-                r = pl.ds(j * h, h)
-                copies += [
-                    (low.at[r], out.at[self.of_out(where, c + j, 2, 0, h)], sems.at[2 * j]),
-                    (high.at[r], out.at[self.of_out(where, c + j, 2, h, h)], sems.at[2 * j + 1]),
-                ]
+        more = self.late if c == CHUNKS - 2 else ()
+
+        def body(where, low, high, *refs):
+            out, sems = refs[-2:]
+            copies = [
+                (low, out.at[self.of_out(where, c, 2, 0, h)], sems.at[0]),
+                (high, out.at[self.of_out(where, c, 2, h, h)], sems.at[1]),
+            ]
+            if more:
+                copies += self.blocks_out(where, c + 1, refs[:3], out, sems, 2)
             move(*copies)
 
         (self.out,) = self.call(
             body,
-            [(a, ANY) for a in got],
+            [(a, ANY) for a in tuple(got) + more],
             [(self.out.shape, BF16, HBM)],
             alias=[(self.out, 0)],
-            scratch=[pltpu.SemaphoreType.DMA((2 * many,))],
+            scratch=[pltpu.SemaphoreType.DMA((5,))],
         )
 
 
@@ -313,7 +322,7 @@
         elif kind == "s":
             got = s.third(c, *held[c])
         elif kind == "o":
-            got = s.pass_on(c, sum((held[e] for e in chunks), ()))
+            got = s.pass_on(c, held[c])
         else:
             got = stages[kind](c, held[c])
         for j, e in enumerate(chunks):

time: 161 us -> 171 us (1.062)
  starting transfers between devices: 63.9 us -> 73.3 us
  waiting for transfers between devices: 56.5 us -> 61.7 us
  Pallas kernels: 32 us -> 29 us
    ppermute x16, starting transfers between devices: 28.3 us -> 36 us  [swap(): return lax.ppermute(a, 'z', [(i, i ^ k) for i in range(NZ)])]
    ppermute x16, waiting for transfers between devices: 9.64 us -> 16.7 us  [swap(): return lax.ppermute(a, 'z', [(i, i ^ k) for i in range(NZ)])]
    pallas_call x34, Pallas kernels: 32 us -> 29 us  [call(): pl.pallas_call(kernel, out_shape=[jax.ShapeDtypeStruct(s, t) for s, t, _...]
    ppermute x30, waiting for transfers between devices: 46.8 us -> 45 us  [shift(): return lax.ppermute(a, 'y', [(i, (i + s) % NY) for i in range(NY)])]
  transfers between devices with their start and end apart: 46 -> 46, of which waited for: 24 -> 24; matrix products, arithmetic and copies ran while one was open for 1% -> 1% of each run, Pallas kernels for 19% -> 15%
where the time goes in v4:
time: 171 us
  starting transfers between devices  73.3 us (43%)
  waiting for transfers between devices  61.7 us (36%)
  Pallas kernels  29 us (17%)
  local copies, waits for them, and re-layouts  4.47 us (3%)
    ppermute x30, waiting for transfers between devices, shift(): return lax.ppermute(a, 'y', [(i, (i + s) % NY) for i in range(NY)])  45 us
    ppermute x30, starting transfers between devices, shift(): return lax.ppermute(a, 'y', [(i, (i + s) % NY) for i in range(NY)])  37.3 us
    ppermute x16, starting transfers between devices, swap(): return lax.ppermute(a, 'z', [(i, i ^ k) for i in range(NZ)])  36 us
    pallas_call x34, Pallas kernels, call(): pl.pallas_call(kernel, out_shape=[jax.ShapeDtypeStruct(s, t) for s, t, _...  29 us
    ppermute x16, waiting for transfers between devices, swap(): return lax.ppermute(a, 'z', [(i, i ^ k) for i in range(NZ)])  16.7 us
  transfers between devices with their start and end apart: 46, of which 24 were waited for; matrix products, arithmetic and copies ran while one was open for 1% of the time, Pallas kernels for 15%

profile of v4, /device:TPU:56, one launch (start us, length us, event | category | flops | bytes accessed | tf_op | source)
XLA Modules:
  0.0 171.2 jit_solution(9825314689382640087)
XLA Ops:
  0.6 1.1 dynamic-slice_bitcast_fusion
  2.0 1.8 %collective-permute-start.1 = (bf16[1,128,1024]{2,1,0:T(8,128)(2,1)S(1)}, bf16[1,128,1024]{2,1,0:T(8,128)(2,1)S(1)}, u32[]{:S(2)}, u32[]{:S(2)}) collective-permute-start(bf16[1,128,1024]{2,1,0:T(8,128)(2,1)S(1)} %get-tuple-element.137), channel_id=1, source_target_pairs={{0,192},{64,0},{128,64},{192,128},{1,193},{65,1},{129,65},{193,129... | collective-permute-start | bytes 786440 | tf_op jit(solution)/shard_map/ppermute | solution.py:24
  3.9 3.4 %copy-done = bf16[1,8,512,1024]{3,2,1,0:T(8,128)(2,1)S(1)} copy-done((bf16[1,8,512,1024]{3,2,1,0:T(8,128)(2,1)S(1)}, bf16[1,8,512,1024]{3,2,1,0:T(8,128)(2,1)}, u32[]{:S(2)}) %copy-start) | copy-done | bytes 8388632
  8.0 1.5 collective-permute-start.4
  10.1 1.1 collective-permute-done.1.refs_2_
  11.1 0.8 shard_map.59
  11.9 1.6 collective-permute-start.2
  14.0 8.9 %collective-permute-done.4.refs_1_ = bf16[2,128,1024]{2,1,0:T(8,128)(2,1)S(1)} collective-permute-done((bf16[2,128,1024]{2,1,0:T(8,128)(2,1)S(1)}, bf16[2,128,1024]{2,1,0:T(8,128)(2,1)S(1)}, u32[]{:S(2)}, u32[]{:S(2)}) %collective-permute-start.4) | collective-permute-done | bytes 524320 | tf_op jit(solution)/shard_map/ppermute | solution.py:24
  22.9 2.6 %collective-permute-done.5.refs_2_ = bf16[2,128,1024]{2,1,0:T(8,128)(2,1)S(1)} collective-permute-done((bf16[2,128,1024]{2,1,0:T(8,128)(2,1)S(1)}, bf16[2,128,1024]{2,1,0:T(8,128)(2,1)S(1)}, u32[]{:S(2)}, u32[]{:S(2)}) %collective-permute-start.5) | collective-permute-done | bytes 524320 | tf_op jit(solution)/shard_map/ppermute | solution.py:24
  25.5 0.8 shard_map.60
  26.4 2.0 %collective-permute-start.9 = (bf16[2,128,1024]{2,1,0:T(8,128)(2,1)S(1)}, bf16[2,128,1024]{2,1,0:T(8,128)(2,1)S(1)}, u32[]{:S(2)}, u32[]{:S(2)}) collective-permute-start(bf16[2,128,1024]{2,1,0:T(8,128)(2,1)S(1)} %get-tuple-element.74.refs_3_), channel_id=1, source_target_pairs={{0,192},{64,0},{128,64},{192,128},{1,193},{65,1},{129,65},{193,129... | collective-permute-start | bytes 1572872 | tf_op jit(solution)/shard_map/ppermute | solution.py:24
  28.4 0.8 shard_map.61
  29.2 4.9 %collective-permute-done.2.refs_1_ = bf16[2,128,1024]{2,1,0:T(8,128)(2,1)S(1)} collective-permute-done((bf16[2,128,1024]{2,1,0:T(8,128)(2,1)S(1)}, bf16[2,128,1024]{2,1,0:T(8,128)(2,1)S(1)}, u32[]{:S(2)}, u32[]{:S(2)}) %collective-permute-start.2) | collective-permute-done | bytes 524320 | tf_op jit(solution)/shard_map/ppermute | solution.py:24
  34.1 2.6 %collective-permute-done.3.refs_2_ = bf16[2,128,1024]{2,1,0:T(8,128)(2,1)S(1)} collective-permute-done((bf16[2,128,1024]{2,1,0:T(8,128)(2,1)S(1)}, bf16[2,128,1024]{2,1,0:T(8,128)(2,1)S(1)}, u32[]{:S(2)}, u32[]{:S(2)}) %collective-permute-start.3) | collective-permute-done | bytes 524320 | tf_op jit(solution)/shard_map/ppermute | solution.py:24
  37.6 1.9 %collective-permute-start.6 = (bf16[2,64,1024]{2,1,0:T(8,128)(2,1)S(1)}, bf16[2,64,1024]{2,1,0:T(8,128)(2,1)S(1)}, u32[]{:S(2)}, u32[]{:S(2)}) collective-permute-start(bf16[2,64,1024]{2,1,0:T(8,128)(2,1)S(1)} %get-tuple-element.77.refs_2_), channel_id=1, source_target_pairs={{0,16},{16,0},{32,48},{48,32},{1,17},{17,1},{33,49},{49,33},{2,18}... | collective-permute-start | bytes 786440 | tf_op jit(solution)/shard_map/ppermute | solution.py:28
  39.5 2.0 %collective-permute-start.14 = (bf16[2,128,1024]{2,1,0:T(8,128)(2,1)S(1)}, bf16[2,128,1024]{2,1,0:T(8,128)(2,1)S(1)}, u32[]{:S(2)}, u32[]{:S(2)}) collective-permute-start(bf16[2,128,1024]{2,1,0:T(8,128)(2,1)S(1)} %get-tuple-element.75.refs_3_), channel_id=1, source_target_pairs={{0,192},{64,0},{128,64},{192,128},{1,193},{65,1},{129,65},{193,129... | collective-permute-start | bytes 1572872 | tf_op jit(solution)/shard_map/ppermute | solution.py:24
  41.5 2.5 %collective-permute-done.6.refs_1_ = bf16[2,64,1024]{2,1,0:T(8,128)(2,1)S(1)} collective-permute-done((bf16[2,64,1024]{2,1,0:T(8,128)(2,1)S(1)}, bf16[2,64,1024]{2,1,0:T(8,128)(2,1)S(1)}, u32[]{:S(2)}, u32[]{:S(2)}) %collective-permute-start.6) | collective-permute-done | bytes 262176 | tf_op jit(solution)/shard_map/ppermute | solution.py:28
  44.6 3.0 %collective-permute-start.7 = (bf16[2,32,1024]{2,1,0:T(8,128)(2,1)S(1)}, bf16[2,32,1024]{2,1,0:T(8,128)(2,1)S(1)}, u32[]{:S(2)}, u32[]{:S(2)}) collective-permute-start(bf16[2,32,1024]{2,1,0:T(8,128)(2,1)S(1)} %get-tuple-element.79.refs_3_), channel_id=1, source_target_pairs={{0,48},{16,32},{32,16},{48,0},{1,49},{17,33},{33,17},{49,1},{2,50}... | collective-permute-start | bytes 393224 | tf_op jit(solution)/shard_map/ppermute | solution.py:28
  48.0 0.8 shard_map.64
  48.8 1.9 %collective-permute-start.15 = (bf16[2,64,1024]{2,1,0:T(8,128)(2,1)S(1)}, bf16[2,64,1024]{2,1,0:T(8,128)(2,1)S(1)}, u32[]{:S(2)}, u32[]{:S(2)}) collective-permute-start(bf16[2,64,1024]{2,1,0:T(8,128)(2,1)S(1)} %get-tuple-element.81.refs_4_), channel_id=1, source_target_pairs={{0,16},{16,0},{32,48},{48,32},{1,17},{17,1},{33,49},{49,33},{2,18}... | collective-permute-start | bytes 786440 | tf_op jit(solution)/shard_map/ppermute | solution.py:28
  52.1 2.0 %collective-permute-start.11 = (bf16[1,128,1024]{2,1,0:T(8,128)(2,1)S(1)}, bf16[1,128,1024]{2,1,0:T(8,128)(2,1)S(1)}, u32[]{:S(2)}, u32[]{:S(2)}) collective-permute-start(bf16[1,128,1024]{2,1,0:T(8,128)(2,1)S(1)} %get-tuple-element.84.refs_2_), channel_id=1, source_target_pairs={{0,192},{64,0},{128,64},{192,128},{1,193},{65,1},{129,65},{193,129... | collective-permute-start | bytes 786440 | tf_op jit(solution)/shard_map/ppermute | solution.py:24
  54.1 1.1 collective-permute-done.15.refs_1_
  55.3 2.2 %collective-permute-start.12 = (bf16[2,32,1024]{2,1,0:T(8,128)(2,1)S(1)}, bf16[2,32,1024]{2,1,0:T(8,128)(2,1)S(1)}, u32[]{:S(2)}, u32[]{:S(2)}) collective-permute-start(bf16[2,32,1024]{2,1,0:T(8,128)(2,1)S(1)} %get-tuple-element.82.refs_1_.refs_0_), channel_id=1, source_target_pairs={{0,48},{16,32},{32,16},{48,0},{1,49},{17,33},{33,17},{49,1},{2,50}... | collective-permute-start | bytes 393224 | tf_op jit(solution)/shard_map/ppermute | solution.py:28
  58.1 1.2 collective-permute-done.14.refs_2_
  61.0 2.0 %collective-permute-done.11.refs_2_ = bf16[1,128,1024]{2,1,0:T(8,128)(2,1)S(1)} collective-permute-done((bf16[1,128,1024]{2,1,0:T(8,128)(2,1)S(1)}, bf16[1,128,1024]{2,1,0:T(8,128)(2,1)S(1)}, u32[]{:S(2)}, u32[]{:S(2)}) %collective-permute-start.11) | collective-permute-done | bytes 262176 | tf_op jit(solution)/shard_map/ppermute | solution.py:24
  63.0 0.8 shard_map.70
  64.1 3.6 %collective-permute-start.18 = (bf16[2,64,1024]{2,1,0:T(8,128)(2,1)S(1)}, bf16[2,64,1024]{2,1,0:T(8,128)(2,1)S(1)}, u32[]{:S(2)}, u32[]{:S(2)}) collective-permute-start(bf16[2,64,1024]{2,1,0:T(8,128)(2,1)S(1)} %get-tuple-element.88.refs_2_), channel_id=1, source_target_pairs={{0,16},{16,0},{32,48},{48,32},{1,17},{17,1},{33,49},{49,33},{2,18}... | collective-permute-start | bytes 786440 | tf_op jit(solution)/shard_map/ppermute | solution.py:28
  68.4 1.3 collective-permute-start.17
  69.7 1.0 collective-permute-start.21
  70.7 2.3 %collective-permute-done.19.refs_1_ = bf16[2,32,1024]{2,1,0:T(8,128)(2,1)S(1)} collective-permute-done((bf16[2,32,1024]{2,1,0:T(8,128)(2,1)S(1)}, bf16[2,32,1024]{2,1,0:T(8,128)(2,1)S(1)}, u32[]{:S(2)}, u32[]{:S(2)}) %collective-permute-start.19) | collective-permute-done | bytes 131104 | tf_op jit(solution)/shard_map/ppermute | solution.py:28
  74.1 1.8 %collective-permute-done.18.refs_1_ = bf16[2,64,1024]{2,1,0:T(8,128)(2,1)S(1)} collective-permute-done((bf16[2,64,1024]{2,1,0:T(8,128)(2,1)S(1)}, bf16[2,64,1024]{2,1,0:T(8,128)(2,1)S(1)}, u32[]{:S(2)}, u32[]{:S(2)}) %collective-permute-start.18) | collective-permute-done | bytes 262176 | tf_op jit(solution)/shard_map/ppermute | solution.py:28
  76.7 4.5 %collective-permute-done.22.refs_1_ = bf16[2,32,1024]{2,1,0:T(8,128)(2,1)S(1)} collective-permute-done((bf16[2,32,1024]{2,1,0:T(8,128)(2,1)S(1)}, bf16[2,32,1024]{2,1,0:T(8,128)(2,1)S(1)}, u32[]{:S(2)}, u32[]{:S(2)}) %collective-permute-start.22) | collective-permute-done | bytes 131104 | tf_op jit(solution)/shard_map/ppermute | solution.py:28
  81.8 7.4 %collective-permute-start.25 = (bf16[2,64,1024]{2,1,0:T(8,128)(2,1)S(1)}, bf16[2,64,1024]{2,1,0:T(8,128)(2,1)S(1)}, u32[]{:S(2)}, u32[]{:S(2)}) collective-permute-start(bf16[2,64,1024]{2,1,0:T(8,128)(2,1)S(1)} %get-tuple-element.103.refs_0_), channel_id=1, source_target_pairs={{0,16},{16,0},{32,48},{48,32},{1,17},{17,1},{33,49},{49,33},{2,18}... | collective-permute-start | bytes 786440 | tf_op jit(solution)/shard_map/ppermute | solution.py:28
  89.8 2.0 %collective-permute-start.28 = (bf16[2,128,1024]{2,1,0:T(8,128)(2,1)S(1)}, bf16[2,128,1024]{2,1,0:T(8,128)(2,1)S(1)}, u32[]{:S(2)}, u32[]{:S(2)}) collective-permute-start(bf16[2,128,1024]{2,1,0:T(8,128)(2,1)S(1)} %get-tuple-element.108.refs_0_), channel_id=1, source_target_pairs={{0,192},{64,0},{128,64},{192,128},{1,193},{65,1},{129,65},{193,129... | collective-permute-start | bytes 1572872 | tf_op jit(solution)/shard_map/ppermute | solution.py:24
  92.5 1.1 collective-permute-start.24
  93.6 0.8 shard_map.76
  94.4 1.7 collective-permute-start.23
  96.7 2.2 %collective-permute-start.31 = (bf16[2,128,1024]{2,1,0:T(8,128)(2,1)S(1)}, bf16[2,128,1024]{2,1,0:T(8,128)(2,1)S(1)}, u32[]{:S(2)}, u32[]{:S(2)}) collective-permute-start(bf16[2,128,1024]{2,1,0:T(8,128)(2,1)S(1)} %get-tuple-element.112.refs_0_), channel_id=1, source_target_pairs={{0,64},{64,128},{128,192},{192,0},{1,65},{65,129},{129,193},{193,1... | collective-permute-start | bytes 1572872 | tf_op jit(solution)/shard_map/ppermute | solution.py:24
  99.0 1.3 collective-permute-start.32
  100.9 2.3 %collective-permute-done.23.refs_1_ = bf16[2,64,1024]{2,1,0:T(8,128)(2,1)S(1)} collective-permute-done((bf16[2,64,1024]{2,1,0:T(8,128)(2,1)S(1)}, bf16[2,64,1024]{2,1,0:T(8,128)(2,1)S(1)}, u32[]{:S(2)}, u32[]{:S(2)}) %collective-permute-start.23) | collective-permute-done | bytes 262176 | tf_op jit(solution)/shard_map/ppermute | solution.py:28
  103.7 1.2 collective-permute-start.26
  104.9 3.4 %collective-permute-start.30 = (bf16[2,64,1024]{2,1,0:T(8,128)(2,1)S(1)}, bf16[2,64,1024]{2,1,0:T(8,128)(2,1)S(1)}, u32[]{:S(2)}, u32[]{:S(2)}) collective-permute-start(bf16[2,64,1024]{2,1,0:T(8,128)(2,1)S(1)} %get-tuple-element.111.refs_0_), channel_id=1, source_target_pairs={{0,16},{16,0},{32,48},{48,32},{1,17},{17,1},{33,49},{49,33},{2,18}... | collective-permute-start | bytes 786440 | tf_op jit(solution)/shard_map/ppermute | solution.py:28
  108.3 1.8 %shard_map.80 = (bf16[8,512,1024]{2,1,0:T(8,128)(2,1)}, bf16[1,128,1024]{2,1,0:T(8,128)(2,1)S(1)}, bf16[1,128,1024]{2,1,0:T(8,128)(2,1)S(1)}) custom-call(s32[2]{0:T(128)S(1)} %pad_add_fusion.where, bf16[2,128,1024]{2,1,0:T(8,128)(2,1)S(1)} %get-tuple-element.108.refs_0_, bf16[2,128,1024]{2,1,0:T(8,128)(2,1)S(1)} %collective-permute-done.27.refs_1_, ...), custom_call_target="tpu_custom_call" | custom-call | flops 1000 | bytes 1000 | tf_op jit(solution)/shard_map/pallas_call | solution.py:72
  110.8 1.4 collective-permute-start.29
  112.2 1.8 %shard_map.82 = (bf16[8,512,1024]{2,1,0:T(8,128)(2,1)}, bf16[1,128,1024]{2,1,0:T(8,128)(2,1)S(1)}, bf16[1,128,1024]{2,1,0:T(8,128)(2,1)S(1)}) custom-call(s32[2]{0:T(128)S(1)} %pad_add_fusion.where, bf16[2,128,1024]{2,1,0:T(8,128)(2,1)S(1)} %get-tuple-element.112.refs_0_, ...), custom_call_target="tpu_custom_call", output_to_operand_aliasing={{0}: (4, {})} | custom-call | flops 1000 | bytes 1000 | tf_op jit(solution)/shard_map/pallas_call | solution.py:72
  114.0 1.4 collective-permute-done.30.refs_1_
  116.7 4.9 %collective-permute-start.33 = (bf16[2,64,1024]{2,1,0:T(8,128)(2,1)S(1)}, bf16[2,64,1024]{2,1,0:T(8,128)(2,1)S(1)}, u32[]{:S(2)}, u32[]{:S(2)}) collective-permute-start(bf16[2,64,1024]{2,1,0:T(8,128)(2,1)S(1)} %get-tuple-element.116.refs_0_), channel_id=1, source_target_pairs={{0,16},{16,0},{32,48},{48,32},{1,17},{17,1},{33,49},{49,33},{2,18}... | collective-permute-start | bytes 786440 | tf_op jit(solution)/shard_map/ppermute | solution.py:28
  121.5 2.3 %collective-permute-start.40 = (bf16[1,128,1024]{2,1,0:T(8,128)(2,1)S(1)}, bf16[1,128,1024]{2,1,0:T(8,128)(2,1)S(1)}, u32[]{:S(2)}, u32[]{:S(2)}) collective-permute-start(bf16[1,128,1024]{2,1,0:T(8,128)(2,1)S(1)} %get-tuple-element.121), channel_id=1, source_target_pairs={{0,64},{64,128},{128,192},{192,0},{1,65},{65,129},{129,193},{193,1... | collective-permute-start | bytes 786440 | tf_op jit(solution)/shard_map/ppermute | solution.py:24
  123.9 3.2 %collective-permute-start.38 = (bf16[1,128,1024]{2,1,0:T(8,128)(2,1)S(1)}, bf16[1,128,1024]{2,1,0:T(8,128)(2,1)S(1)}, u32[]{:S(2)}, u32[]{:S(2)}) collective-permute-start(bf16[1,128,1024]{2,1,0:T(8,128)(2,1)S(1)} %get-tuple-element.120), channel_id=1, source_target_pairs={{0,64},{64,128},{128,192},{192,0},{1,65},{65,129},{129,193},{193,1... | collective-permute-start | bytes 786440 | tf_op jit(solution)/shard_map/ppermute | solution.py:24
  127.1 2.0 %collective-permute-start.37 = (bf16[2,128,1024]{2,1,0:T(8,128)(2,1)S(1)}, bf16[2,128,1024]{2,1,0:T(8,128)(2,1)S(1)}, u32[]{:S(2)}, u32[]{:S(2)}) collective-permute-start(bf16[2,128,1024]{2,1,0:T(8,128)(2,1)S(1)} %get-tuple-element.119.refs_0_), channel_id=1, source_target_pairs={{0,192},{64,0},{128,64},{192,128},{1,193},{65,1},{129,65},{193,129... | collective-permute-start | bytes 1572872 | tf_op jit(solution)/shard_map/ppermute | solution.py:24
  129.7 1.1 collective-permute-done.40.refs_0_
  130.8 3.5 %collective-permute-start.34 = (bf16[2,128,1024]{2,1,0:T(8,128)(2,1)S(1)}, bf16[2,128,1024]{2,1,0:T(8,128)(2,1)S(1)}, u32[]{:S(2)}, u32[]{:S(2)}) collective-permute-start(bf16[2,128,1024]{2,1,0:T(8,128)(2,1)S(1)} %get-tuple-element.118.refs_0_.refs_2_), channel_id=1, source_target_pairs={{0,64},{64,128},{128,192},{192,0},{1,65},{65,129},{129,193},{193,1... | collective-permute-start | bytes 1572872 | tf_op jit(solution)/shard_map/ppermute | solution.py:24
  134.3 2.1 %collective-permute-done.38.refs_0_ = bf16[1,128,1024]{2,1,0:T(8,128)(2,1)S(1)} collective-permute-done((bf16[1,128,1024]{2,1,0:T(8,128)(2,1)S(1)}, bf16[1,128,1024]{2,1,0:T(8,128)(2,1)S(1)}, u32[]{:S(2)}, u32[]{:S(2)}) %collective-permute-start.38) | collective-permute-done | bytes 262176 | tf_op jit(solution)/shard_map/ppermute | solution.py:24
  136.4 1.4 shard_map.86.refs_2_
  137.8 14.0 %collective-permute-done.39.refs_1_ = bf16[1,128,1024]{2,1,0:T(8,128)(2,1)S(1)} collective-permute-done((bf16[1,128,1024]{2,1,0:T(8,128)(2,1)S(1)}, bf16[1,128,1024]{2,1,0:T(8,128)(2,1)S(1)}, u32[]{:S(2)}, u32[]{:S(2)}) %collective-permute-start.39) | collective-permute-done | bytes 262176 | tf_op jit(solution)/shard_map/ppermute | solution.py:24
  151.8 1.4 shard_map.87.refs_3_
  153.2 1.8 %shard_map.88 = (bf16[8,512,1024]{2,1,0:T(8,128)(2,1)}, bf16[1,128,1024]{2,1,0:T(8,128)(2,1)S(1)}, bf16[1,128,1024]{2,1,0:T(8,128)(2,1)S(1)}) custom-call(s32[2]{0:T(128)S(1)} %pad_add_fusion.where, bf16[2,128,1024]{2,1,0:T(8,128)(2,1)S(1)} %get-tuple-element.119.refs_0_, ...), custom_call_target="tpu_custom_call", output_to_operand_aliasing={{0}: (4, {})} | custom-call | flops 1000 | bytes 1000 | tf_op jit(solution)/shard_map/pallas_call | solution.py:72
  155.0 3.1 %collective-permute-start.44 = (bf16[1,128,1024]{2,1,0:T(8,128)(2,1)S(1)}, bf16[1,128,1024]{2,1,0:T(8,128)(2,1)S(1)}, u32[]{:S(2)}, u32[]{:S(2)}) collective-permute-start(bf16[1,128,1024]{2,1,0:T(8,128)(2,1)S(1)} %get-tuple-element.127), channel_id=1, source_target_pairs={{0,64},{64,128},{128,192},{192,0},{1,65},{65,129},{129,193},{193,1... | collective-permute-start | bytes 786440 | tf_op jit(solution)/shard_map/ppermute | solution.py:24
  158.8 3.3 %collective-permute-start.42 = (bf16[1,128,1024]{2,1,0:T(8,128)(2,1)S(1)}, bf16[1,128,1024]{2,1,0:T(8,128)(2,1)S(1)}, u32[]{:S(2)}, u32[]{:S(2)}) collective-permute-start(bf16[1,128,1024]{2,1,0:T(8,128)(2,1)S(1)} %get-tuple-element.125), channel_id=1, source_target_pairs={{0,64},{64,128},{128,192},{192,0},{1,65},{65,129},{129,193},{193,1... | collective-permute-start | bytes 786440 | tf_op jit(solution)/shard_map/ppermute | solution.py:24
  162.1 1.5 pad_maximum_fusion
  163.6 2.1 %collective-permute-done.45.refs_1_ = bf16[1,128,1024]{2,1,0:T(8,128)(2,1)S(1)} collective-permute-done((bf16[1,128,1024]{2,1,0:T(8,128)(2,1)S(1)}, bf16[1,128,1024]{2,1,0:T(8,128)(2,1)S(1)}, u32[]{:S(2)}, u32[]{:S(2)}) %collective-permute-start.45) | collective-permute-done | bytes 262176 | tf_op jit(solution)/shard_map/ppermute | solution.py:24
  165.7 1.9 %shard_map.90.refs_2_ = bf16[8,512,1024]{2,1,0:T(8,128)(2,1)} custom-call(s32[2]{0:T(128)S(1)} %pad_add_fusion.where, bf16[1,128,1024]{2,1,0:T(8,128)(2,1)S(1)} %collective-permute-done.44.refs_0_, bf16[1,128,1024]{2,1,0:T(8,128)(2,1)S(1)} %collective-permute-done.45.refs_1_, ...), custom_call_target="tpu_custom_call", output_to_operand_aliasing={{}: (6, {})} | custom-call | flops 1000 | bytes 1000 | tf_op jit(solution)/shard_map/pallas_call | solution.py:72
  167.6 2.0 %collective-permute-done.43.refs_1_ = bf16[1,128,1024]{2,1,0:T(8,128)(2,1)S(1)} collective-permute-done((bf16[1,128,1024]{2,1,0:T(8,128)(2,1)S(1)}, bf16[1,128,1024]{2,1,0:T(8,128)(2,1)S(1)}, u32[]{:S(2)}, u32[]{:S(2)}) %collective-permute-start.43) | collective-permute-done | bytes 262176 | tf_op jit(solution)/shard_map/ppermute | solution.py:24
  169.7 1.4 shard_map.91
  (76 shorter events, 17.6 us)
Async XLA Ops:
  1.7 8.3 %collective-permute-start = (bf16[1,128,1024]{2,1,0:T(8,128)(2,1)S(1)}, bf16[1,128,1024]{2,1,0:T(8,128)(2,1)S(1)}, u32[]{:S(2)}, u32[]{:S(2)}) collective-permute-start(bf16[1,128,1024]{2,1,0:T(8,128)(2,1)S(1)} %get-tuple-element.138.refs_1_), channel_id=1, source_target_pairs={{0,64},{64,128},{128,192},{192,0},{1,65},{65,129},{129,193},{193,1... | collective-permute-start | bytes 786440 | tf_op jit(solution)/shard_map/ppermute | solution.py:24
  2.0 9.1 %collective-permute-start.1 = (bf16[1,128,1024]{2,1,0:T(8,128)(2,1)S(1)}, bf16[1,128,1024]{2,1,0:T(8,128)(2,1)S(1)}, u32[]{:S(2)}, u32[]{:S(2)}) collective-permute-start(bf16[1,128,1024]{2,1,0:T(8,128)(2,1)S(1)} %get-tuple-element.137), channel_id=1, source_target_pairs={{0,192},{64,0},{128,64},{192,128},{1,193},{65,1},{129,65},{193,129... | collective-permute-start | bytes 786440 | tf_op jit(solution)/shard_map/ppermute | solution.py:24
  3.9 3.4 %copy-start = (bf16[1,8,512,1024]{3,2,1,0:T(8,128)(2,1)S(1)}, bf16[1,8,512,1024]{3,2,1,0:T(8,128)(2,1)}, u32[]{:S(2)}) copy-start(bf16[1,8,512,1024]{3,2,1,0:T(8,128)(2,1)} %refs_0_.19) | copy-start | bytes 25165828
  8.0 14.9 %collective-permute-start.4 = (bf16[2,128,1024]{2,1,0:T(8,128)(2,1)S(1)}, bf16[2,128,1024]{2,1,0:T(8,128)(2,1)S(1)}, u32[]{:S(2)}, u32[]{:S(2)}) collective-permute-start(bf16[2,128,1024]{2,1,0:T(8,128)(2,1)S(1)} %get-tuple-element.73), channel_id=1, source_target_pairs={{0,64},{64,128},{128,192},{192,0},{1,65},{65,129},{129,193},{193,1... | collective-permute-start | bytes 1572872 | tf_op jit(solution)/shard_map/ppermute | solution.py:24
  9.5 16.1 %collective-permute-start.5 = (bf16[2,128,1024]{2,1,0:T(8,128)(2,1)S(1)}, bf16[2,128,1024]{2,1,0:T(8,128)(2,1)S(1)}, u32[]{:S(2)}, u32[]{:S(2)}) collective-permute-start(bf16[2,128,1024]{2,1,0:T(8,128)(2,1)S(1)} %get-tuple-element.70.refs_3_), channel_id=1, source_target_pairs={{0,192},{64,0},{128,64},{192,128},{1,193},{65,1},{129,65},{193,129... | collective-permute-start | bytes 1572872 | tf_op jit(solution)/shard_map/ppermute | solution.py:24
  11.9 22.2 %collective-permute-start.2 = (bf16[2,128,1024]{2,1,0:T(8,128)(2,1)S(1)}, bf16[2,128,1024]{2,1,0:T(8,128)(2,1)S(1)}, u32[]{:S(2)}, u32[]{:S(2)}) collective-permute-start(bf16[2,128,1024]{2,1,0:T(8,128)(2,1)S(1)} %get-tuple-element.71), channel_id=1, source_target_pairs={{0,64},{64,128},{128,192},{192,0},{1,65},{65,129},{129,193},{193,1... | collective-permute-start | bytes 1572872 | tf_op jit(solution)/shard_map/ppermute | solution.py:24
  13.6 23.2 %collective-permute-start.3 = (bf16[2,128,1024]{2,1,0:T(8,128)(2,1)S(1)}, bf16[2,128,1024]{2,1,0:T(8,128)(2,1)S(1)}, u32[]{:S(2)}, u32[]{:S(2)}) collective-permute-start(bf16[2,128,1024]{2,1,0:T(8,128)(2,1)S(1)} %get-tuple-element.72.refs_3_), channel_id=1, source_target_pairs={{0,192},{64,0},{128,64},{192,128},{1,193},{65,1},{129,65},{193,129... | collective-permute-start | bytes 1572872 | tf_op jit(solution)/shard_map/ppermute | solution.py:24
  26.3 21.3 %collective-permute-start.8 = (bf16[2,128,1024]{2,1,0:T(8,128)(2,1)S(1)}, bf16[2,128,1024]{2,1,0:T(8,128)(2,1)S(1)}, u32[]{:S(2)}, u32[]{:S(2)}) collective-permute-start(bf16[2,128,1024]{2,1,0:T(8,128)(2,1)S(1)} %get-tuple-element.80), channel_id=1, source_target_pairs={{0,64},{64,128},{128,192},{192,0},{1,65},{65,129},{129,193},{193,1... | collective-permute-start | bytes 1572872 | tf_op jit(solution)/shard_map/ppermute | solution.py:24
  26.4 21.6 %slice-start = ((s8[8388608]{0:T(1024)(128)(4,1)}), s8[4194304]{0:T(1024)(128)(4,1)S(1)}, s32[]{:S(2)}) async-start(s8[8388608]{0:T(1024)(128)(4,1)} %bitcast.6), calls=%async_computation | async-start | bytes 8388608
  26.4 21.6 %collective-permute-start.9 = (bf16[2,128,1024]{2,1,0:T(8,128)(2,1)S(1)}, bf16[2,128,1024]{2,1,0:T(8,128)(2,1)S(1)}, u32[]{:S(2)}, u32[]{:S(2)}) collective-permute-start(bf16[2,128,1024]{2,1,0:T(8,128)(2,1)S(1)} %get-tuple-element.74.refs_3_), channel_id=1, source_target_pairs={{0,192},{64,0},{128,64},{192,128},{1,193},{65,1},{129,65},{193,129... | collective-permute-start | bytes 1572872 | tf_op jit(solution)/shard_map/ppermute | solution.py:24
  36.8 11.2 %slice-start.1 = ((s8[8388608]{0:T(1024)(128)(4,1)}), s8[4194304]{0:T(1024)(128)(4,1)S(1)}, s32[]{:S(2)}) async-start(s8[8388608]{0:T(1024)(128)(4,1)} %bitcast.6), calls=%async_computation.1 | async-start | bytes 8388608
  36.8 14.0 %copy-start.1 = (f32[8,32,1024]{2,1,0:T(8,128)S(1)}, f32[8,32,1024]{2,1,0:T(8,128)}, u32[]{:S(2)}) copy-start(f32[8,32,1024]{2,1,0:T(8,128)} %refs_2_.7) | copy-start | bytes 3145732
  36.8 14.0 %copy-start.2 = (f32[8,32,1024]{2,1,0:T(8,128)S(1)}, f32[8,32,1024]{2,1,0:T(8,128)}, u32[]{:S(2)}) copy-start(f32[8,32,1024]{2,1,0:T(8,128)} %refs_3_.7) | copy-start | bytes 3145732
  37.6 6.5 %collective-permute-start.6 = (bf16[2,64,1024]{2,1,0:T(8,128)(2,1)S(1)}, bf16[2,64,1024]{2,1,0:T(8,128)(2,1)S(1)}, u32[]{:S(2)}, u32[]{:S(2)}) collective-permute-start(bf16[2,64,1024]{2,1,0:T(8,128)(2,1)S(1)} %get-tuple-element.77.refs_2_), channel_id=1, source_target_pairs={{0,16},{16,0},{32,48},{48,32},{1,17},{17,1},{33,49},{49,33},{2,18}... | collective-permute-start | bytes 786440 | tf_op jit(solution)/shard_map/ppermute | solution.py:28
  39.5 18.6 %collective-permute-start.13 = (bf16[2,128,1024]{2,1,0:T(8,128)(2,1)S(1)}, bf16[2,128,1024]{2,1,0:T(8,128)(2,1)S(1)}, u32[]{:S(2)}, u32[]{:S(2)}) collective-permute-start(bf16[2,128,1024]{2,1,0:T(8,128)(2,1)S(1)} %get-tuple-element.85), channel_id=1, source_target_pairs={{0,64},{64,128},{128,192},{192,0},{1,65},{65,129},{129,193},{193,1... | collective-permute-start | bytes 1572872 | tf_op jit(solution)/shard_map/ppermute | solution.py:24
  39.5 19.7 %collective-permute-start.14 = (bf16[2,128,1024]{2,1,0:T(8,128)(2,1)S(1)}, bf16[2,128,1024]{2,1,0:T(8,128)(2,1)S(1)}, u32[]{:S(2)}, u32[]{:S(2)}) collective-permute-start(bf16[2,128,1024]{2,1,0:T(8,128)(2,1)S(1)} %get-tuple-element.75.refs_3_), channel_id=1, source_target_pairs={{0,192},{64,0},{128,64},{192,128},{1,193},{65,1},{129,65},{193,129... | collective-permute-start | bytes 1572872 | tf_op jit(solution)/shard_map/ppermute | solution.py:24
  44.6 6.1 %collective-permute-start.7 = (bf16[2,32,1024]{2,1,0:T(8,128)(2,1)S(1)}, bf16[2,32,1024]{2,1,0:T(8,128)(2,1)S(1)}, u32[]{:S(2)}, u32[]{:S(2)}) collective-permute-start(bf16[2,32,1024]{2,1,0:T(8,128)(2,1)S(1)} %get-tuple-element.79.refs_3_), channel_id=1, source_target_pairs={{0,48},{16,32},{32,16},{48,0},{1,49},{17,33},{33,17},{49,1},{2,50}... | collective-permute-start | bytes 393224 | tf_op jit(solution)/shard_map/ppermute | solution.py:28
  48.8 6.5 %collective-permute-start.15 = (bf16[2,64,1024]{2,1,0:T(8,128)(2,1)S(1)}, bf16[2,64,1024]{2,1,0:T(8,128)(2,1)S(1)}, u32[]{:S(2)}, u32[]{:S(2)}) collective-permute-start(bf16[2,64,1024]{2,1,0:T(8,128)(2,1)S(1)} %get-tuple-element.81.refs_4_), channel_id=1, source_target_pairs={{0,16},{16,0},{32,48},{48,32},{1,17},{17,1},{33,49},{49,33},{2,18}... | collective-permute-start | bytes 786440 | tf_op jit(solution)/shard_map/ppermute | solution.py:28
  52.0 9.0 %collective-permute-start.10 = (bf16[1,128,1024]{2,1,0:T(8,128)(2,1)S(1)}, bf16[1,128,1024]{2,1,0:T(8,128)(2,1)S(1)}, u32[]{:S(2)}, u32[]{:S(2)}) collective-permute-start(bf16[1,128,1024]{2,1,0:T(8,128)(2,1)S(1)} %get-tuple-element.83), channel_id=1, source_target_pairs={{0,64},{64,128},{128,192},{192,0},{1,65},{65,129},{129,193},{193,1... | collective-permute-start | bytes 786440 | tf_op jit(solution)/shard_map/ppermute | solution.py:24
  52.1 10.9 %collective-permute-start.11 = (bf16[1,128,1024]{2,1,0:T(8,128)(2,1)S(1)}, bf16[1,128,1024]{2,1,0:T(8,128)(2,1)S(1)}, u32[]{:S(2)}, u32[]{:S(2)}) collective-permute-start(bf16[1,128,1024]{2,1,0:T(8,128)(2,1)S(1)} %get-tuple-element.84.refs_2_), channel_id=1, source_target_pairs={{0,192},{64,0},{128,64},{192,128},{1,193},{65,1},{129,65},{193,129... | collective-permute-start | bytes 786440 | tf_op jit(solution)/shard_map/ppermute | solution.py:24
  55.3 5.2 %collective-permute-start.12 = (bf16[2,32,1024]{2,1,0:T(8,128)(2,1)S(1)}, bf16[2,32,1024]{2,1,0:T(8,128)(2,1)S(1)}, u32[]{:S(2)}, u32[]{:S(2)}) collective-permute-start(bf16[2,32,1024]{2,1,0:T(8,128)(2,1)S(1)} %get-tuple-element.82.refs_1_.refs_0_), channel_id=1, source_target_pairs={{0,48},{16,32},{32,16},{48,0},{1,49},{17,33},{33,17},{49,1},{2,50}... | collective-permute-start | bytes 393224 | tf_op jit(solution)/shard_map/ppermute | solution.py:28
  63.8 28.7 %collective-permute-start.16 = (bf16[2,128,1024]{2,1,0:T(8,128)(2,1)S(1)}, bf16[2,128,1024]{2,1,0:T(8,128)(2,1)S(1)}, u32[]{:S(2)}, u32[]{:S(2)}) collective-permute-start(bf16[2,128,1024]{2,1,0:T(8,128)(2,1)S(1)} %get-tuple-element.90), channel_id=1, source_target_pairs={{0,64},{64,128},{128,192},{192,0},{1,65},{65,129},{129,193},{193,1... | collective-permute-start | bytes 1572872 | tf_op jit(solution)/shard_map/ppermute | solution.py:24
  64.1 11.9 %collective-permute-start.18 = (bf16[2,64,1024]{2,1,0:T(8,128)(2,1)S(1)}, bf16[2,64,1024]{2,1,0:T(8,128)(2,1)S(1)}, u32[]{:S(2)}, u32[]{:S(2)}) collective-permute-start(bf16[2,64,1024]{2,1,0:T(8,128)(2,1)S(1)} %get-tuple-element.88.refs_2_), channel_id=1, source_target_pairs={{0,16},{16,0},{32,48},{48,32},{1,17},{17,1},{33,49},{49,33},{2,18}... | collective-permute-start | bytes 786440 | tf_op jit(solution)/shard_map/ppermute | solution.py:28
  67.7 5.2 %collective-permute-start.19 = (bf16[2,32,1024]{2,1,0:T(8,128)(2,1)S(1)}, bf16[2,32,1024]{2,1,0:T(8,128)(2,1)S(1)}, u32[]{:S(2)}, u32[]{:S(2)}) collective-permute-start(bf16[2,32,1024]{2,1,0:T(8,128)(2,1)S(1)} %get-tuple-element.87.refs_3_), channel_id=1, source_target_pairs={{0,48},{16,32},{32,16},{48,0},{1,49},{17,33},{33,17},{49,1},{2,50}... | collective-permute-start | bytes 393224 | tf_op jit(solution)/shard_map/ppermute | solution.py:28
  68.4 25.2 %collective-permute-start.17 = (bf16[2,128,1024]{2,1,0:T(8,128)(2,1)S(1)}, bf16[2,128,1024]{2,1,0:T(8,128)(2,1)S(1)}, u32[]{:S(2)}, u32[]{:S(2)}) collective-permute-start(bf16[2,128,1024]{2,1,0:T(8,128)(2,1)S(1)} %get-tuple-element.91.refs_4_), channel_id=1, source_target_pairs={{0,192},{64,0},{128,64},{192,128},{1,193},{65,1},{129,65},{193,129... | collective-permute-start | bytes 1572872 | tf_op jit(solution)/shard_map/ppermute | solution.py:24
  69.7 19.4 %collective-permute-start.21 = (bf16[2,64,1024]{2,1,0:T(8,128)(2,1)S(1)}, bf16[2,64,1024]{2,1,0:T(8,128)(2,1)S(1)}, u32[]{:S(2)}, u32[]{:S(2)}) collective-permute-start(bf16[2,64,1024]{2,1,0:T(8,128)(2,1)S(1)} %get-tuple-element.97.refs_0_), channel_id=1, source_target_pairs={{0,16},{16,0},{32,48},{48,32},{1,17},{17,1},{33,49},{49,33},{2,18}... | collective-permute-start | bytes 786440 | tf_op jit(solution)/shard_map/ppermute | solution.py:28
  73.6 7.6 %collective-permute-start.22 = (bf16[2,32,1024]{2,1,0:T(8,128)(2,1)S(1)}, bf16[2,32,1024]{2,1,0:T(8,128)(2,1)S(1)}, u32[]{:S(2)}, u32[]{:S(2)}) collective-permute-start(bf16[2,32,1024]{2,1,0:T(8,128)(2,1)S(1)} %get-tuple-element.94.refs_2_.refs_0_), channel_id=1, source_target_pairs={{0,48},{16,32},{32,16},{48,0},{1,49},{17,33},{33,17},{49,1},{2,50}... | collective-permute-start | bytes 393224 | tf_op jit(solution)/shard_map/ppermute | solution.py:28
  76.6 13.2 %collective-permute-start.20 = (bf16[2,32,1024]{2,1,0:T(8,128)(2,1)S(1)}, bf16[2,32,1024]{2,1,0:T(8,128)(2,1)S(1)}, u32[]{:S(2)}, u32[]{:S(2)}) collective-permute-start(bf16[2,32,1024]{2,1,0:T(8,128)(2,1)S(1)} %get-tuple-element.96.refs_2_), channel_id=1, source_target_pairs={{0,48},{16,32},{32,16},{48,0},{1,49},{17,33},{33,17},{49,1},{2,50}... | collective-permute-start | bytes 393224 | tf_op jit(solution)/shard_map/ppermute | solution.py:28
  81.8 14.4 %collective-permute-start.25 = (bf16[2,64,1024]{2,1,0:T(8,128)(2,1)S(1)}, bf16[2,64,1024]{2,1,0:T(8,128)(2,1)S(1)}, u32[]{:S(2)}, u32[]{:S(2)}) collective-permute-start(bf16[2,64,1024]{2,1,0:T(8,128)(2,1)S(1)} %get-tuple-element.103.refs_0_), channel_id=1, source_target_pairs={{0,16},{16,0},{32,48},{48,32},{1,17},{17,1},{33,49},{49,33},{2,18}... | collective-permute-start | bytes 786440 | tf_op jit(solution)/shard_map/ppermute | solution.py:28
  89.7 15.2 %collective-permute-start.27 = (bf16[2,128,1024]{2,1,0:T(8,128)(2,1)S(1)}, bf16[2,128,1024]{2,1,0:T(8,128)(2,1)S(1)}, u32[]{:S(2)}, u32[]{:S(2)}) collective-permute-start(bf16[2,128,1024]{2,1,0:T(8,128)(2,1)S(1)} %get-tuple-element.108.refs_0_), channel_id=1, source_target_pairs={{0,64},{64,128},{128,192},{192,0},{1,65},{65,129},{129,193},{193,1... | collective-permute-start | bytes 1572872 | tf_op jit(solution)/shard_map/ppermute | solution.py:24
  89.8 18.4 %collective-permute-start.28 = (bf16[2,128,1024]{2,1,0:T(8,128)(2,1)S(1)}, bf16[2,128,1024]{2,1,0:T(8,128)(2,1)S(1)}, u32[]{:S(2)}, u32[]{:S(2)}) collective-permute-start(bf16[2,128,1024]{2,1,0:T(8,128)(2,1)S(1)} %get-tuple-element.108.refs_0_), channel_id=1, source_target_pairs={{0,192},{64,0},{128,64},{192,128},{1,193},{65,1},{129,65},{193,129... | collective-permute-start | bytes 1572872 | tf_op jit(solution)/shard_map/ppermute | solution.py:24
  92.5 6.5 %collective-permute-start.24 = (bf16[2,32,1024]{2,1,0:T(8,128)(2,1)S(1)}, bf16[2,32,1024]{2,1,0:T(8,128)(2,1)S(1)}, u32[]{:S(2)}, u32[]{:S(2)}) collective-permute-start(bf16[2,32,1024]{2,1,0:T(8,128)(2,1)S(1)} %get-tuple-element.100.refs_3_.refs_0_), channel_id=1, source_target_pairs={{0,48},{16,32},{32,16},{48,0},{1,49},{17,33},{33,17},{49,1},{2,50}... | collective-permute-start | bytes 393224 | tf_op jit(solution)/shard_map/ppermute | solution.py:28
  94.4 8.7 %collective-permute-start.23 = (bf16[2,64,1024]{2,1,0:T(8,128)(2,1)S(1)}, bf16[2,64,1024]{2,1,0:T(8,128)(2,1)S(1)}, u32[]{:S(2)}, u32[]{:S(2)}) collective-permute-start(bf16[2,64,1024]{2,1,0:T(8,128)(2,1)S(1)} %get-tuple-element.102.refs_2_), channel_id=1, source_target_pairs={{0,16},{16,0},{32,48},{48,32},{1,17},{17,1},{33,49},{49,33},{2,18}... | collective-permute-start | bytes 786440 | tf_op jit(solution)/shard_map/ppermute | solution.py:28
  96.7 15.5 %collective-permute-start.31 = (bf16[2,128,1024]{2,1,0:T(8,128)(2,1)S(1)}, bf16[2,128,1024]{2,1,0:T(8,128)(2,1)S(1)}, u32[]{:S(2)}, u32[]{:S(2)}) collective-permute-start(bf16[2,128,1024]{2,1,0:T(8,128)(2,1)S(1)} %get-tuple-element.112.refs_0_), channel_id=1, source_target_pairs={{0,64},{64,128},{128,192},{192,0},{1,65},{65,129},{129,193},{193,1... | collective-permute-start | bytes 1572872 | tf_op jit(solution)/shard_map/ppermute | solution.py:24
  99.0 13.2 %collective-permute-start.32 = (bf16[2,128,1024]{2,1,0:T(8,128)(2,1)S(1)}, bf16[2,128,1024]{2,1,0:T(8,128)(2,1)S(1)}, u32[]{:S(2)}, u32[]{:S(2)}) collective-permute-start(bf16[2,128,1024]{2,1,0:T(8,128)(2,1)S(1)} %get-tuple-element.112.refs_0_), channel_id=1, source_target_pairs={{0,192},{64,0},{128,64},{192,128},{1,193},{65,1},{129,65},{193,129... | collective-permute-start | bytes 1572872 | tf_op jit(solution)/shard_map/ppermute | solution.py:24
  103.7 6.5 %collective-permute-start.26 = (bf16[2,32,1024]{2,1,0:T(8,128)(2,1)S(1)}, bf16[2,32,1024]{2,1,0:T(8,128)(2,1)S(1)}, u32[]{:S(2)}, u32[]{:S(2)}) collective-permute-start(bf16[2,32,1024]{2,1,0:T(8,128)(2,1)S(1)} %get-tuple-element.107.refs_3_), channel_id=1, source_target_pairs={{0,48},{16,32},{32,16},{48,0},{1,49},{17,33},{33,17},{49,1},{2,50}... | collective-permute-start | bytes 393224 | tf_op jit(solution)/shard_map/ppermute | solution.py:28
  104.9 10.5 %collective-permute-start.30 = (bf16[2,64,1024]{2,1,0:T(8,128)(2,1)S(1)}, bf16[2,64,1024]{2,1,0:T(8,128)(2,1)S(1)}, u32[]{:S(2)}, u32[]{:S(2)}) collective-permute-start(bf16[2,64,1024]{2,1,0:T(8,128)(2,1)S(1)} %get-tuple-element.111.refs_0_), channel_id=1, source_target_pairs={{0,16},{16,0},{32,48},{48,32},{1,17},{17,1},{33,49},{49,33},{2,18}... | collective-permute-start | bytes 786440 | tf_op jit(solution)/shard_map/ppermute | solution.py:28
  110.8 5.3 %collective-permute-start.29 = (bf16[2,32,1024]{2,1,0:T(8,128)(2,1)S(1)}, bf16[2,32,1024]{2,1,0:T(8,128)(2,1)S(1)}, u32[]{:S(2)}, u32[]{:S(2)}) collective-permute-start(bf16[2,32,1024]{2,1,0:T(8,128)(2,1)S(1)} %get-tuple-element.110.refs_4_.refs_0_), channel_id=1, source_target_pairs={{0,48},{16,32},{32,16},{48,0},{1,49},{17,33},{33,17},{49,1},{2,50}... | collective-permute-start | bytes 393224 | tf_op jit(solution)/shard_map/ppermute | solution.py:28
  116.7 10.5 %collective-permute-start.33 = (bf16[2,64,1024]{2,1,0:T(8,128)(2,1)S(1)}, bf16[2,64,1024]{2,1,0:T(8,128)(2,1)S(1)}, u32[]{:S(2)}, u32[]{:S(2)}) collective-permute-start(bf16[2,64,1024]{2,1,0:T(8,128)(2,1)S(1)} %get-tuple-element.116.refs_0_), channel_id=1, source_target_pairs={{0,16},{16,0},{32,48},{48,32},{1,17},{17,1},{33,49},{49,33},{2,18}... | collective-permute-start | bytes 786440 | tf_op jit(solution)/shard_map/ppermute | solution.py:28
  121.5 9.2 %collective-permute-start.40 = (bf16[1,128,1024]{2,1,0:T(8,128)(2,1)S(1)}, bf16[1,128,1024]{2,1,0:T(8,128)(2,1)S(1)}, u32[]{:S(2)}, u32[]{:S(2)}) collective-permute-start(bf16[1,128,1024]{2,1,0:T(8,128)(2,1)S(1)} %get-tuple-element.121), channel_id=1, source_target_pairs={{0,64},{64,128},{128,192},{192,0},{1,65},{65,129},{129,193},{193,1... | collective-permute-start | bytes 786440 | tf_op jit(solution)/shard_map/ppermute | solution.py:24
  123.9 10.5 %collective-permute-start.41 = (bf16[1,128,1024]{2,1,0:T(8,128)(2,1)S(1)}, bf16[1,128,1024]{2,1,0:T(8,128)(2,1)S(1)}, u32[]{:S(2)}, u32[]{:S(2)}) collective-permute-start(bf16[1,128,1024]{2,1,0:T(8,128)(2,1)S(1)} %get-tuple-element.109.refs_4_), channel_id=1, source_target_pairs={{0,192},{64,0},{128,64},{192,128},{1,193},{65,1},{129,65},{193,129... | collective-permute-start | bytes 786440 | tf_op jit(solution)/shard_map/ppermute | solution.py:24
  123.9 12.5 %collective-permute-start.38 = (bf16[1,128,1024]{2,1,0:T(8,128)(2,1)S(1)}, bf16[1,128,1024]{2,1,0:T(8,128)(2,1)S(1)}, u32[]{:S(2)}, u32[]{:S(2)}) collective-permute-start(bf16[1,128,1024]{2,1,0:T(8,128)(2,1)S(1)} %get-tuple-element.120), channel_id=1, source_target_pairs={{0,64},{64,128},{128,192},{192,0},{1,65},{65,129},{129,193},{193,1... | collective-permute-start | bytes 786440 | tf_op jit(solution)/shard_map/ppermute | solution.py:24
  127.1 26.1 %collective-permute-start.36 = (bf16[2,128,1024]{2,1,0:T(8,128)(2,1)S(1)}, bf16[2,128,1024]{2,1,0:T(8,128)(2,1)S(1)}, u32[]{:S(2)}, u32[]{:S(2)}) collective-permute-start(bf16[2,128,1024]{2,1,0:T(8,128)(2,1)S(1)} %get-tuple-element.119.refs_0_), channel_id=1, source_target_pairs={{0,64},{64,128},{128,192},{192,0},{1,65},{65,129},{129,193},{193,1... | collective-permute-start | bytes 1572872 | tf_op jit(solution)/shard_map/ppermute | solution.py:24
  127.1 26.1 %collective-permute-start.37 = (bf16[2,128,1024]{2,1,0:T(8,128)(2,1)S(1)}, bf16[2,128,1024]{2,1,0:T(8,128)(2,1)S(1)}, u32[]{:S(2)}, u32[]{:S(2)}) collective-permute-start(bf16[2,128,1024]{2,1,0:T(8,128)(2,1)S(1)} %get-tuple-element.119.refs_0_), channel_id=1, source_target_pairs={{0,192},{64,0},{128,64},{192,128},{1,193},{65,1},{129,65},{193,129... | collective-permute-start | bytes 1572872 | tf_op jit(solution)/shard_map/ppermute | solution.py:24
  130.8 27.4 %collective-permute-start.34 = (bf16[2,128,1024]{2,1,0:T(8,128)(2,1)S(1)}, bf16[2,128,1024]{2,1,0:T(8,128)(2,1)S(1)}, u32[]{:S(2)}, u32[]{:S(2)}) collective-permute-start(bf16[2,128,1024]{2,1,0:T(8,128)(2,1)S(1)} %get-tuple-element.118.refs_0_.refs_2_), channel_id=1, source_target_pairs={{0,64},{64,128},{128,192},{192,0},{1,65},{65,129},{129,193},{193,1... | collective-permute-start | bytes 1572872 | tf_op jit(solution)/shard_map/ppermute | solution.py:24
  134.3 23.8 %collective-permute-start.35 = (bf16[2,128,1024]{2,1,0:T(8,128)(2,1)S(1)}, bf16[2,128,1024]{2,1,0:T(8,128)(2,1)S(1)}, u32[]{:S(2)}, u32[]{:S(2)}) collective-permute-start(bf16[2,128,1024]{2,1,0:T(8,128)(2,1)S(1)} %get-tuple-element.118.refs_0_.refs_2_), channel_id=1, source_target_pairs={{0,192},{64,0},{128,64},{192,128},{1,193},{65,1},{129,65},{193,129... | collective-permute-start | bytes 1572872 | tf_op jit(solution)/shard_map/ppermute | solution.py:24
  136.4 15.4 %collective-permute-start.39 = (bf16[1,128,1024]{2,1,0:T(8,128)(2,1)S(1)}, bf16[1,128,1024]{2,1,0:T(8,128)(2,1)S(1)}, u32[]{:S(2)}, u32[]{:S(2)}) collective-permute-start(bf16[1,128,1024]{2,1,0:T(8,128)(2,1)S(1)} %get-tuple-element.114.refs_2_.refs_3_), channel_id=1, source_target_pairs={{0,192},{64,0},{128,64},{192,128},{1,193},{65,1},{129,65},{193,129... | collective-permute-start | bytes 786440 | tf_op jit(solution)/shard_map/ppermute | solution.py:24
  155.0 8.6 %collective-permute-start.44 = (bf16[1,128,1024]{2,1,0:T(8,128)(2,1)S(1)}, bf16[1,128,1024]{2,1,0:T(8,128)(2,1)S(1)}, u32[]{:S(2)}, u32[]{:S(2)}) collective-permute-start(bf16[1,128,1024]{2,1,0:T(8,128)(2,1)S(1)} %get-tuple-element.127), channel_id=1, source_target_pairs={{0,64},{64,128},{128,192},{192,0},{1,65},{65,129},{129,193},{193,1... | collective-permute-start | bytes 786440 | tf_op jit(solution)/shard_map/ppermute | solution.py:24
  158.1 7.6 %collective-permute-start.45 = (bf16[1,128,1024]{2,1,0:T(8,128)(2,1)S(1)}, bf16[1,128,1024]{2,1,0:T(8,128)(2,1)S(1)}, u32[]{:S(2)}, u32[]{:S(2)}) collective-permute-start(bf16[1,128,1024]{2,1,0:T(8,128)(2,1)S(1)} %get-tuple-element.124.refs_3_), channel_id=1, source_target_pairs={{0,192},{64,0},{128,64},{192,128},{1,193},{65,1},{129,65},{193,129... | collective-permute-start | bytes 786440 | tf_op jit(solution)/shard_map/ppermute | solution.py:24
  158.8 8.8 %collective-permute-start.42 = (bf16[1,128,1024]{2,1,0:T(8,128)(2,1)S(1)}, bf16[1,128,1024]{2,1,0:T(8,128)(2,1)S(1)}, u32[]{:S(2)}, u32[]{:S(2)}) collective-permute-start(bf16[1,128,1024]{2,1,0:T(8,128)(2,1)S(1)} %get-tuple-element.125), channel_id=1, source_target_pairs={{0,64},{64,128},{128,192},{192,0},{1,65},{65,129},{129,193},{193,1... | collective-permute-start | bytes 786440 | tf_op jit(solution)/shard_map/ppermute | solution.py:24
  162.1 7.6 %collective-permute-start.43 = (bf16[1,128,1024]{2,1,0:T(8,128)(2,1)S(1)}, bf16[1,128,1024]{2,1,0:T(8,128)(2,1)S(1)}, u32[]{:S(2)}, u32[]{:S(2)}) collective-permute-start(bf16[1,128,1024]{2,1,0:T(8,128)(2,1)S(1)} %get-tuple-element.126.refs_6_.refs_3_), channel_id=1, source_target_pairs={{0,192},{64,0},{128,64},{192,128},{1,193},{65,1},{129,65},{193,129... | collective-permute-start | bytes 786440 | tf_op jit(solution)/shard_map/ppermute | solution.py:24
